TPU v7x, 256 devices: a whole 4x4x8 slice. The times are simulated.
256 devices in a mesh: row: 16 (over x, z_lo, core), col: 16 (over y, z_hi).
Axes of the slice: x: 4, y: 4, z: 8 (z_hi: 4, z_lo: 2; z = z_hi * 2 + z_lo), core: 2. Of those that a mesh axis runs over, the one named last changes fastest.
Arguments:
- amplitudes: bfloat16 [9984, 4096], P('row', 'col'), may hold values from -6 to 6
- tiles: bfloat16 [16, 128, 128, 128], P('col', 'row'), may hold values from -0.09375 to 0.09375
- tile_ids: int32 [16, 128], P('col', 'row'), may hold values from -1 to 511, as said below
Outputs:
- ladder: bfloat16 [9984, 32768], P('row', 'col')
Inputs may be any that keep to these rules, and one draw needn't show every extreme that they name: `tile_ids`: within one grid column the non-negative ids are distinct; in every column one device's block of 8 slots is all live, and within each device's block live slots come first.
All inputs are finite; a program needn't handle non-finite values.
Results may differ from a plain program's by a relative error of at most 0.001.
Values may be sent and summed in bfloat16 or wider, within the bound.
No kernel may reach another device: no remote copies, remote signals or barrier semaphores. Data moves between devices by JAX's collectives and lax.ppermute only.
A program may use at most 128 MiB of HBM per device.

v0:
```python
import jax
import jax.numpy as jnp
from jax import lax
from jax.sharding import PartitionSpec as P

TILE = 128
KT = 32
NQ = 16


def shards(amplitudes, tiles, tile_ids):
    all_tiles, all_ids = (
        lax.all_gather(tiles, "row", axis=1, tiled=True),
        lax.all_gather(tile_ids, "row", axis=1, tiled=True),
    )
    index = jnp.where(all_ids[0] >= 0, all_ids[0], KT * NQ).astype(jnp.int32)
    dense = jnp.zeros((KT * NQ + 1, TILE, TILE), all_tiles.dtype).at[index].set(all_tiles[0])
    dense = (
        dense[: KT * NQ]
        .reshape(KT, NQ, TILE, TILE)
        .transpose(0, 2, 1, 3)
        .reshape(KT * TILE, NQ * TILE)
    )
    panel = lax.all_gather(amplitudes, "col", axis=1, tiled=True)
    result = jnp.dot(panel, dense, preferred_element_type=jnp.float32)
    return result.astype(jnp.bfloat16)


def solution(mesh):
    in_specs = (P("row", "col"), P("col", "row", None, None), P("col", "row"))
    out_specs = P("row", "col")
    return jax.shard_map(shards, mesh=mesh, in_specs=in_specs, out_specs=out_specs, check_vma=False)
```

profile of v0, /device:TPU:1, one launch (start us, length us, event | category | flops | bytes accessed | tf_op | source)
XLA Modules:
  0.0 171.5 jit_solution(10060578647502765072)
XLA Ops:
  6.5 0.0 all-gather.3.cloned.1.call-start
  6.5 0.7 all-gather.3.cloned.1.call-update
  7.3 0.0 all-gather.5.cloned.1.call-start
  7.3 0.7 all-gather.5.cloned.1.call-update
  8.0 1.3 dynamic-slice
  9.9 0.8 bitcast_dynamic-update-slice_fusion
  10.7 11.2 %all-reduce = s32[128]{0:T(128)S(1)} all-reduce(s32[128]{0:T(128)S(1)} %bitcast_dynamic-update-slice_fusion), channel_id=1, replica_groups=mesh['row'=16,'col'=16] {'row'}, use_global_device_ids=true, to_apply=%add | all-reduce | flops 128 | bytes 1024
  21.9 31.6 %all-gather.3.cloned.1.call-done = bf16[1,128,128,128]{3,2,0,1:T(8,128)(2,1)} async-done(((bf16[1,8,128,128]{3,2,0,1:T(8,128)(2,1)}), bf16[1,128,128,128]{3,2,0,1:T(8,128)(2,1)}) %all-gather.3.cloned.1.call-update) | async-done | bytes 4194320 | tf_op jit(solution)/shard_map/all_gather | solution.py:13
  53.5 6.1 %broadcast_in_dim.8 = bf16[513,128,128]{2,1,0:T(8,128)(2,1)} broadcast(bf16[]{:T(256)} %constant.0.clone.1), dimensions={} | broadcast | bytes 16809986 | tf_op jit(solution)/shard_map/broadcast_in_dim | solution.py:17
  59.6 19.4 %scatter_fusion = bf16[513,128,128]{2,1,0:T(8,128)(2,1)} fusion(bf16[513,128,128]{2,1,0:T(8,128)(2,1)} %broadcast_in_dim.8, s32[128]{0:T(128)S(1)} %fusion.9, bf16[128,128,128]{2,1,0:T(8,128)(2,1)} %bitcast.26), kind=kCustom, calls=%fused_computation | custom fusion | bytes 12583424 | tf_op jit(solution)/shard_map/scatter | solution.py:17
  78.9 8.0 %slice.4 = bf16[512,128,128]{2,1,0:T(8,128)(2,1)S(1)} slice(bf16[513,128,128]{2,1,0:T(8,128)(2,1)} %scatter_fusion), slice={[0:512], [0:128], [0:128]} | slice | bytes 33554432 | tf_op jit(solution)/shard_map/slice | solution.py:19
  87.0 12.1 %copy.6 = bf16[32,128,16,128]{3,2,1,0:T(8,128)(2,1)} copy(bf16[32,128,16,128]{3,1,2,0:T(8,128)(2,1)S(1)} %bitcast.24) | data formatting | bytes 33554432 | tf_op jit(solution)/shard_map/transpose | solution.py:21
  99.1 48.6 %all-gather.5.cloned.1.call-done = bf16[624,4096]{1,0:T(8,128)(2,1)} async-done(((bf16[624,256]{1,0:T(8,128)(2,1)}), bf16[624,4096]{1,0:T(8,128)(2,1)}) %all-gather.5.cloned.1.call-update) | async-done | bytes 5111824 | tf_op jit(solution)/shard_map/all_gather | solution.py:24
  147.8 16.9 %fusion.6 = bf16[624,2048]{1,0:T(8,128)(2,1)} fusion(bf16[624,4096]{1,0:T(8,128)(2,1)} %all-gather.5.cloned.1.call-done, bf16[512,8,16,128]{3,2,1,0:T(8,128)(2,1)} %bitcast.25), kind=kOutput, calls=%fused_computation.5 | convolution fusion | flops 10470260736 | bytes 24444928 | tf_op jit(solution)/shard_map/dot_general | solution.py:25
  (2 shorter events, 0.0 us)
Async XLA Ops:
  6.5 47.0 %all-gather.3.cloned.1.call-start = ((), (), s32[]{:S(2)}) async-start(), calls=%async_computation | async-start | bytes 4456448 | tf_op jit(solution)/shard_map/all_gather | solution.py:13
  7.3 140.5 %all-gather.5.cloned.1.call-start = ((), (), s32[]{:S(2)}) async-start(), calls=%async_computation.1 | async-start | bytes 5431296 | tf_op jit(solution)/shard_map/all_gather | solution.py:24
Sparse Core Ops, SparseCore 0:
  9.2 44.2 all-gather.2
  55.9 91.8 all-gather.4
where the time goes:
time: 172 us; the launch traced here: 171 us
  waiting for transfers between devices  81.7 us (48%)
  local copies, waits for them, and re-layouts  47.6 us (28%)
  matrix products  16.9 us (10%)
  between operations  14.1 us (8%)
  blocking collectives  11.2 us (7%)
    all_gather x1, waiting for transfers between devices, shards(): panel = lax.all_gather(amplitudes, 'col', axis=1, tiled=True)  48.6 us
    all_gather x1, waiting for transfers between devices, shards(): lax.all_gather(tiles, 'row', axis=1, tiled=True)  31.6 us
    scatter x1, local copies, waits for them, and re-layouts, shards(): jnp.zeros((KT * NQ + 1, TILE, TILE), all_tiles.dtype).at[index]  19.4 us
    dot_general x1, matrix products, shards(): result = jnp.dot(panel, dense, preferred_element_type=jnp.float32)  16.9 us
    transpose x1, local copies, waits for them, and re-layouts, shards(): dense = dense[:KT * NQ].reshape(KT, NQ, TILE, TILE).transpose(0, 2, 1, 3)...  12.1 us
    unnamed x1, blocking collectives  11.2 us
    slice x1, local copies, waits for them, and re-layouts, shards(): dense[:KT * NQ].reshape(KT, NQ, TILE, TILE).transpose(0, 2, 1, 3)  8.03 us
    broadcast_in_dim x1, local copies, waits for them, and re-layouts, shards(): jnp.zeros((KT * NQ + 1, TILE, TILE), all_tiles.dtype).at[index]  6.09 us
  transfers between devices with their start and end apart: 2, of which 2 were waited for; matrix products, arithmetic and copies ran while one was open for 28% of the time, Pallas kernels for 0%

commit v1 on v0

v1 whole, which is shorter than its diff:
```python
import functools
import itertools

import jax
import jax.numpy as jnp
from jax import lax
from jax.experimental import pallas as pl
from jax.experimental.pallas import tpu as pltpu
from jax.sharding import PartitionSpec as P

TILE = 128
NQ = 16
ROWS = 624
ROWS_A = 480
ROWS_B = ROWS - ROWS_A
HALF = 320
HALF_A = ROWS_A // 2
SLOTS = 8
HELD = 64
EARLY_SLOTS = 48
EARLY = (0, 1, 2, 3, 4, 5, 6, 8, 9, 10)
GROUP = 4
PAIR = 2
STEPS = NQ // PAIR
WIDTH = TILE * PAIR


def rank_of(d):
    return d ^ (d >> 1)


def fence(*values):
    return lax.optimization_barrier(values)


def from_col(value, dy=0, dz=0):
    perm = [
        ((y + dy) % 4 * 4 + (z + dz) % 4, y * 4 + z) for y in range(4) for z in range(4)
    ]
    return lax.ppermute(value, "col", perm)


def from_row(value, dx=0, dz=0, dcore=0):
    perm = []
    for x, z, core in itertools.product(range(4), range(2), range(2)):
        at_x = (x + dx * (1 - 2 * core)) % 4
        perm.append(((at_x * 2 + (z ^ dz)) * 2 + (core ^ dcore), (x * 2 + z) * 2 + core))
    return lax.ppermute(value, "row", perm)


def sort_tiles(position, tiles, wanted, codes, codes_smem, lists, counts, sem):
    n = tiles.shape[0]
    y, z = position[0], position[1]
    lane = lax.broadcasted_iota(jnp.int32, (1, TILE), 1)
    for i in range(n):
        rows = tiles[i, SLOTS * TILE : SLOTS * TILE + 16, :].astype(jnp.float32)
        kt, qt = rows[0:1].astype(jnp.int32), rows[1:2].astype(jnp.int32)
        owner = kt >> 1
        place = rank_of(((owner & 3) - z) & 3) * 4 + rank_of(((owner >> 2) - y) & 3)
        block = (place * 2 + (kt & 1)) & 31
        live = (kt >= 0) & wanted(i * SLOTS + lane, block)
        codes[i : i + 1, :] = jnp.where(live, (qt & 15) * 32 + block, NQ * 32)
    copy = pltpu.make_async_copy(codes, codes_smem, sem)
    copy.start()
    for q in range(NQ + 1):
        counts[q] = 0
    copy.wait()

    def put(i, carry):
        for j in range(SLOTS):
            code = codes_smem[i, j]
            q = code >> 5
            at = counts[q]
            lists[q * 32 + at] = (i * SLOTS + j) * 32 + (code & 31)
            counts[q] = at + 1
        return carry

    lax.fori_loop(0, n, put, 0)


def products(lists, counts, tiles, amps, step):
    groups, functions = [], []
    for i in range(PAIR):
        q = step * PAIR + i
        count = counts[q]

        def product(group, q=q, count=count):
            left, right = [], []
            for j in range(GROUP):
                at = group * GROUP + j
                live = at < count
                item = jnp.where(live, lists[q * 32 + jnp.minimum(at, 31)], 0)
                slot = item >> 5
                row = pl.ds(pl.multiple_of((slot & 7) * TILE, TILE), TILE)
                tile = tiles[slot >> 3, row, :]
                right.append(jnp.where(live, tile, jnp.zeros_like(tile)))
                left.append(amps[item & 31])
            return jnp.dot(
                jnp.concatenate(left, axis=1),
                jnp.concatenate(right, axis=0),
                preferred_element_type=jnp.float32,
            )

        groups.append((count + GROUP - 1) // GROUP)
        functions.append(product)
    return functools.reduce(jnp.maximum, groups), functions


def accumulate(lists, counts, tiles, amps, step, before, total):
    groups, functions = products(lists, counts, tiles, amps, step)
    for i, value in enumerate([function(0) for function in functions]):
        part = slice(i * TILE, (i + 1) * TILE)
        total[:, part] = value if before is None else before[:, part] + value

    def more(group, carry):
        for i, value in enumerate([function(group) for function in functions]):
            total[:, i * TILE : (i + 1) * TILE] += value
        return carry

    lax.fori_loop(1, groups, more, 0)


def moves(plan, pieces, amps, sem):
    return [
        pltpu.make_async_copy(
            pieces[ref].at[pl.ds(src, rows), pl.ds(sub * TILE, TILE)],
            amps.at[place * 2 + sub, pl.ds(dst, rows)],
            sem,
        )
        for ref, src, rows, place, dst in plan
        for sub in range(2)
    ]


def early_pair(slot, block):
    early = functools.reduce(jnp.logical_or, [(block >> 1) == place for place in EARLY])
    return (slot < EARLY_SLOTS) & early


def first_part(plan, n_pieces, position, tiles, *refs):
    amps, partial, codes, codes_smem, lists, counts, sem, code_sem = refs[n_pieces:]
    copies = moves(plan, refs[:n_pieces], amps, sem)
    for copy in copies:
        copy.start()
    sort_tiles(position, tiles, early_pair, codes, codes_smem, lists, counts, code_sem)
    for copy in copies:
        copy.wait()

    @pl.loop(0, STEPS)
    def _(step):
        accumulate(lists, counts, tiles, amps, step, None, partial.at[step])


def second_part(plan, n_pieces, position, tiles, before_amps, before, *refs):
    amps, partial, codes, codes_smem, lists, counts, sem, code_sem = refs[n_pieces:]
    copies = moves(plan, refs[:n_pieces], amps, sem)
    for copy in copies:
        copy.start()
    sort_tiles(
        position, tiles, lambda slot, block: jnp.logical_not(early_pair(slot, block)),
        codes, codes_smem, lists, counts, code_sem,
    )
    for copy in copies:
        copy.wait()

    @pl.loop(0, STEPS)
    def _(step):
        accumulate(lists, counts, tiles, amps, step, before.at[step], partial.at[step])


def last_part(position, tiles, amps, before, out, codes, codes_smem, lists, counts, total, stage, code_sem, out_sem):
    sort_tiles(
        position, tiles, lambda slot, block: slot >= 0, codes, codes_smem, lists, counts, code_sem
    )

    def write(step, slot):
        columns = pl.ds(pl.multiple_of(step * WIDTH, WIDTH), WIDTH)
        return pltpu.make_async_copy(stage.at[slot], out.at[:, columns], out_sem.at[slot])

    @pl.loop(0, STEPS)
    def _(step):
        slot = lax.rem(step, 2)

        @pl.when(step >= 2)
        def _():
            write(step - 2, slot).wait()

        accumulate(lists, counts, tiles, amps, step, before.at[step], total)
        stage[slot] = total[...].astype(jnp.bfloat16)
        write(step, slot).start()

    for step in range(STEPS - 2, STEPS):
        write(step, step % 2).wait()


def call(body, out_shape, out_specs, arguments, scratch, name, aliases={}):
    sorting = [
        pltpu.VMEM((8, TILE), jnp.int32),
        pltpu.SMEM((8, TILE), jnp.int32),
        pltpu.SMEM((NQ * 32 + HELD,), jnp.int32),
        pltpu.SMEM((NQ + 1,), jnp.int32),
    ]
    return pl.pallas_call(
        body,
        out_shape=out_shape,
        in_specs=[pl.BlockSpec(memory_space=space) for _, space in arguments],
        out_specs=out_specs,
        scratch_shapes=sorting + scratch,
        input_output_aliases=aliases,
        compiler_params=pltpu.CompilerParams(vmem_limit_bytes=24 * 2**20),
        cost_estimate=pl.CostEstimate(
            flops=5_000_000_000, bytes_accessed=16_000_000, transcendentals=0
        ),
        name=name,
    )(*(array for array, _ in arguments))


def chosen_part(plan, arrays, chosen, space):
    steps = [step for step in plan if step[0] in chosen]
    return [(step[0] - chosen[0],) + step[1:] for step in steps], [(arrays[i], space) for i in chosen]


IN_VMEM = pl.BlockSpec(memory_space=pltpu.VMEM)
SUMS = [
    jax.ShapeDtypeStruct((32, ROWS, TILE), jnp.bfloat16),
    jax.ShapeDtypeStruct((STEPS, ROWS, WIDTH), jnp.float32),
]


def contract_early(position, tiles, steps, pieces):
    return call(
        functools.partial(first_part, steps, len(pieces)),
        SUMS, [IN_VMEM, IN_VMEM],
        [(position, pltpu.SMEM), (tiles, pltpu.VMEM)] + pieces,
        [pltpu.SemaphoreType.DMA] * 2, "first_part",
    )


def contract_late(position, own, other, amps, partial, steps, pieces):
    smem, vmem, dma = pltpu.SMEM, pltpu.VMEM, pltpu.SemaphoreType.DMA
    amps, partial = call(
        functools.partial(second_part, steps, len(pieces)),
        SUMS, [IN_VMEM, IN_VMEM],
        [(position, smem), (own, vmem), (amps, vmem), (partial, vmem)] + pieces,
        [dma, dma], "second_part", {2: 0, 3: 1},
    )
    return call(
        last_part,
        jax.ShapeDtypeStruct((ROWS, NQ * TILE), jnp.bfloat16),
        pl.BlockSpec(memory_space=pl.ANY),
        [(position, smem), (other, vmem), (amps, vmem), (partial, vmem)],
        [pltpu.VMEM((ROWS, WIDTH), jnp.float32), pltpu.VMEM((2, ROWS, WIDTH), jnp.bfloat16), dma, dma((2,))],
        "last_part",
    )


def touch(*arrays):
    anywhere = pl.BlockSpec(memory_space=pl.ANY)
    return pl.pallas_call(
        lambda *refs: None,
        out_shape=[jax.ShapeDtypeStruct(array.shape, array.dtype) for array in arrays],
        in_specs=[anywhere] * len(arrays),
        out_specs=[anywhere] * len(arrays),
        input_output_aliases={i: i for i in range(len(arrays))},
        cost_estimate=pl.CostEstimate(
            flops=10_000_000_000, bytes_accessed=1_000_000, transcendentals=0
        ),
        name="touch",
    )(*arrays)


def shards(amplitudes, tiles, tile_ids):
    kt = jnp.where(tile_ids >= 0, tile_ids >> 4, -1)
    qt = tile_ids & 15
    ids = jnp.concatenate([kt, qt], axis=0).astype(jnp.bfloat16)
    ids = jnp.pad(ids, ((0, 14), (0, TILE - SLOTS)))
    block = jnp.concatenate([tiles.reshape(SLOTS * TILE, TILE), ids], axis=0)

    block_z = from_row(block, dz=1)
    y_up, y_down = (from_col(amplitudes, dy=dy) for dy in (1, 3))
    first = amplitudes[:ROWS_A]
    z_up, z_down = (from_col(first, dz=dz) for dz in (1, 3))
    z_up, z_down = touch(z_up, z_down)
    block_z, y_up, y_down, z_up, z_down = fence(block_z, y_up, y_down, z_up, z_down)

    x_blocks = [jnp.stack([block, block_z])]
    x_blocks.append(from_row(x_blocks[-1], dx=1))
    y_top, y_low = from_col(y_down[:HALF], dy=3), from_col(y_up[HALF:], dy=1)
    z_top, z_low = from_col(z_down[:HALF_A], dz=3), from_col(z_up[HALF_A:], dz=1)
    x_blocks[-1], y_top, y_low, z_top, z_low = fence(x_blocks[-1], y_top, y_low, z_top, z_low)

    firsts = [jnp.concatenate([z_up, z_down, z_top, z_low], axis=0)]
    lasts = [jnp.concatenate([rows[ROWS_A:] for rows in (amplitudes, y_up, y_down)] + [y_low[ROWS_A - HALF :]], axis=0)]
    x_blocks.append(from_row(x_blocks[-1], dx=1))
    firsts += [from_col(firsts[0], dy=dy) for dy in (1, 3)]
    lasts += [from_col(lasts[0], dz=dz) for dz in (1, 3)]
    x_blocks[-1], firsts[1], firsts[2], lasts[1], lasts[2] = fence(
        x_blocks[-1], firsts[1], firsts[2], lasts[1], lasts[2]
    )

    plan = [(0, 0, ROWS, 0, 0), (1, 0, ROWS, 1, 0), (2, 0, ROWS, 2, 0), (3, 0, HALF, 3, 0)]
    plan.append((4, 0, ROWS - HALF, 3, HALF))
    for i in range(3):
        for j in range(3):
            plan.append((5 + i, j * ROWS_A, ROWS_A, 4 * (j + 1) + i, 0))
    plan += [(10, 0, ROWS_A, 7, 0), (10, ROWS_A, HALF_A, 11, 0)]
    plan += [(11, 0, HALF_A, 11, HALF_A), (11, HALF_A, ROWS_A, 15, 0)]
    for j in range(4):
        plan.append((8, j * ROWS_B, ROWS_B, 4 + j, ROWS_A))
        plan.append((9, j * ROWS_B, ROWS_B, 8 + j, ROWS_A))
        plan.append((12 + j // 2, j % 2 * ROWS_B, ROWS_B, 12 + j, ROWS_A))
    cut, cut_b = 3 * ROWS_A // 2, 2 * ROWS_B
    early_tiles = jnp.concatenate(x_blocks, axis=0)
    x_blocks.append(from_row(x_blocks[-1], dx=1))
    firsts += [from_col(firsts[2][:cut], dy=3), from_col(firsts[1][cut:], dy=1)]
    lasts += [from_col(lasts[2][:cut_b], dz=3), from_col(lasts[1][cut_b:], dz=1)]
    position = jnp.stack([lax.axis_index("col") // 4, lax.axis_index("col") % 4]).astype(jnp.int32)
    arrays = [amplitudes, y_up, y_down, y_top, y_low] + firsts[:3] + lasts[1:3] + firsts[3:] + lasts[3:]
    amps, partial = contract_early(
        position, early_tiles, *chosen_part(plan, arrays, range(10), pl.ANY)
    )
    x_blocks[-1], amps, partial, *arrays[10:] = fence(x_blocks[-1], amps, partial, *arrays[10:])

    own = jnp.concatenate(x_blocks, axis=0)
    other = from_row(own, dcore=1)
    late = chosen_part(plan, arrays, range(10, 14), pltpu.HBM)
    return contract_late(position, own, other, amps, partial, *late)


def solution(mesh):
    in_specs = (P("row", "col"), P("col", "row", None, None), P("col", "row"))
    out_specs = P("row", "col")
    return jax.shard_map(shards, mesh=mesh, in_specs=in_specs, out_specs=out_specs, check_vma=False)
```

time: 172 us -> 93 us (0.54)
  waiting for transfers between devices: 81.7 us -> 24.6 us
  local copies, waits for them, and re-layouts: 47.6 us -> 4.8 us
  starting transfers between devices: 0.04 us -> 39.4 us
  Pallas kernels: 0 us -> 21.7 us
  matrix products: 16.9 us -> 0 us
  between operations: 14.1 us -> 0.42 us
  blocking collectives: 11.2 us -> 0 us
  other arithmetic: 0.01 us -> 2.03 us
    all_gather x2 -> x0, waiting for transfers between devices: 80.3 us -> none  [the longest x1 48.6 us: shards(): panel = lax.all_gather(amplitudes, 'col', axis=1, tiled=True)]
    ppermute x0 -> x21, starting transfers between devices: none -> 39.4 us  [the longest x16 27.8 us: from_col(): return lax.ppermute(value, 'col', perm)]
    ppermute x0 -> x21, waiting for transfers between devices: none -> 24.6 us  [the longest x16 18.3 us: from_col(): return lax.ppermute(value, 'col', perm)]
    pallas_call x0 -> x4, Pallas kernels: none -> 21.7 us  [the longest x3 21.7 us: call(): pl.pallas_call(body, out_shape=out_shape, in_specs=[pl.BlockSpec(memory_s...]
    scatter x1 -> x0, local copies, waits for them, and re-layouts: 19.4 us -> none  [shards(): jnp.zeros((KT * NQ + 1, TILE, TILE), all_tiles.dtype).at[index]]
    dot_general x1 -> x0, matrix products: 16.9 us -> none  [shards(): result = jnp.dot(panel, dense, preferred_element_type=jnp.float32)]
    transpose x1 -> x0, local copies, waits for them, and re-layouts: 12.1 us -> none  [shards(): dense = dense[:KT * NQ].reshape(KT, NQ, TILE, TILE).transpose(0, 2, 1, 3)...]
    unnamed x1 -> x0, blocking collectives: 11.2 us -> none
  transfers between devices with their start and end apart: 2 -> 21, of which waited for: 2 -> 8; matrix products, arithmetic and copies ran while one was open for 28% -> 5% of each run, Pallas kernels for 0% -> 14%
where the time goes in v1:
time: 93 us
  starting transfers between devices  39.4 us (42%)
  waiting for transfers between devices  24.6 us (26%)
  Pallas kernels  21.7 us (23%)
  local copies, waits for them, and re-layouts  4.8 us (5%)
  other arithmetic  2.03 us (2%)
    ppermute x16, starting transfers between devices, from_col(): return lax.ppermute(value, 'col', perm)  27.8 us
    pallas_call x3, Pallas kernels, call(): pl.pallas_call(body, out_shape=out_shape, in_specs=[pl.BlockSpec(memory_s...  21.7 us
    ppermute x16, waiting for transfers between devices, from_col(): return lax.ppermute(value, 'col', perm)  18.3 us
    ppermute x5, starting transfers between devices, from_row(): return lax.ppermute(value, 'row', perm)  11.6 us
    ppermute x5, waiting for transfers between devices, from_row(): return lax.ppermute(value, 'row', perm)  6.3 us
  transfers between devices with their start and end apart: 21, of which 8 were waited for; matrix products, arithmetic and copies ran while one was open for 5% of the time, Pallas kernels for 14%

profile of v1, /device:TPU:1, one launch (start us, length us, event | category | flops | bytes accessed | tf_op | source)
XLA Modules:
  0.0 93.0 jit_solution(14541928699875201846)
XLA Ops:
  0.0 1.0 %slice.39 = bf16[480,256]{1,0:T(8,128)(2,1)S(1)} slice(bf16[624,256]{1,0:T(8,128)(2,1)} %refs_0_.1), slice={[0:480], [0:256]} | slice | bytes 491520 | tf_op jit(solution)/shard_map/slice | solution.py:281
  1.0 3.9 %collective-permute-start.4 = (bf16[480,256]{1,0:T(8,128)(2,1)S(1)}, bf16[480,256]{1,0:T(8,128)(2,1)S(1)}, u32[]{:S(2)}, u32[]{:S(2)}) collective-permute-start(bf16[480,256]{1,0:T(8,128)(2,1)S(1)} %slice.39), channel_id=1, source_target_pairs={{3,0},{0,1},{1,2},{2,3},{7,4},{4,5},{5,6},{6,7},{11,8},{8,9},{9,10... | collective-permute-start | bytes 737288 | tf_op jit(solution)/shard_map/ppermute | solution.py:40
  4.9 3.1 %collective-permute-start.3 = (bf16[480,256]{1,0:T(8,128)(2,1)S(1)}, bf16[480,256]{1,0:T(8,128)(2,1)S(1)}, u32[]{:S(2)}, u32[]{:S(2)}) collective-permute-start(bf16[480,256]{1,0:T(8,128)(2,1)S(1)} %slice.39), channel_id=1, source_target_pairs={{1,0},{2,1},{3,2},{0,3},{5,4},{6,5},{7,6},{4,7},{9,8},{10,9},{11,1... | collective-permute-start | bytes 737288 | tf_op jit(solution)/shard_map/ppermute | solution.py:40
  8.0 1.3 %collective-permute-start.2 = (bf16[624,256]{1,0:T(8,128)(2,1)}, bf16[624,256]{1,0:T(8,128)(2,1)S(1)}, u32[]{:S(2)}, u32[]{:S(2)}) collective-permute-start(bf16[624,256]{1,0:T(8,128)(2,1)} %refs_0_.1), channel_id=1, source_target_pairs={{12,0},{13,1},{14,2},{15,3},{0,4},{1,5},{2,6},{3,7},{4,8},{5,9},{6... | collective-permute-start | bytes 958472 | tf_op jit(solution)/shard_map/ppermute | solution.py:40
  9.3 1.4 %collective-permute-start.1 = (bf16[624,256]{1,0:T(8,128)(2,1)}, bf16[624,256]{1,0:T(8,128)(2,1)S(1)}, u32[]{:S(2)}, u32[]{:S(2)}) collective-permute-start(bf16[624,256]{1,0:T(8,128)(2,1)} %refs_0_.1), channel_id=1, source_target_pairs={{4,0},{5,1},{6,2},{7,3},{8,4},{9,5},{10,6},{11,7},{12,8},{13,9},{1... | collective-permute-start | bytes 958472 | tf_op jit(solution)/shard_map/ppermute | solution.py:40
  10.7 0.7 fusion.6
  11.4 1.0 %fusion.7 = (bf16[1,1040,128]{2,1,0:T(8,128)(2,1)S(1)}, bf16[1040,128]{1,0:T(8,128)(2,1)S(1)}) fusion(bf16[16,128]{1,0:T(8,128)(2,1)S(1)} %fusion.5, bf16[1024,128]{1,0:T(8,128)(2,1)} %bitcast.10), kind=kLoop, calls=%fused_computation.25 | loop fusion | flops 532480 | bytes 798720 | tf_op jit(solution)/shard_map/stack | solution.py:286
  12.4 0.8 collective-permute-start
  13.2 0.9 slice.44
  14.1 1.0 %collective-permute-done.4.refs_1_ = bf16[480,256]{1,0:T(8,128)(2,1)S(1)} collective-permute-done((bf16[480,256]{1,0:T(8,128)(2,1)S(1)}, bf16[480,256]{1,0:T(8,128)(2,1)S(1)}, u32[]{:S(2)}, u32[]{:S(2)}) %collective-permute-start.4) | collective-permute-done | bytes 245792 | tf_op jit(solution)/shard_map/ppermute | solution.py:40
  15.1 5.2 %collective-permute-done.3.refs_0_ = bf16[480,256]{1,0:T(8,128)(2,1)S(1)} collective-permute-done((bf16[480,256]{1,0:T(8,128)(2,1)S(1)}, bf16[480,256]{1,0:T(8,128)(2,1)S(1)}, u32[]{:S(2)}, u32[]{:S(2)}) %collective-permute-start.3) | collective-permute-done | bytes 245792 | tf_op jit(solution)/shard_map/ppermute | solution.py:40
  20.3 0.0 copy-done.2
  20.3 0.7 copy-done.4
  21.0 4.6 %collective-permute-done = bf16[1040,128]{1,0:T(8,128)(2,1)S(1)} collective-permute-done((bf16[1040,128]{1,0:T(8,128)(2,1)S(1)}, bf16[1040,128]{1,0:T(8,128)(2,1)S(1)}, u32[]{:S(2)}, u32[]{:S(2)}) %collective-permute-start) | collective-permute-done | bytes 266272 | tf_op jit(solution)/shard_map/ppermute | solution.py:48
  25.6 0.0 collective-permute-done.2.refs_2_
  25.6 0.0 collective-permute-done.1.refs_1_
  25.6 0.1 pad_maximum_fusion.1
  25.7 1.3 %collective-permute-start.5 = (bf16[2,1040,128]{2,1,0:T(8,128)(2,1)S(1)}, bf16[2,1040,128]{2,1,0:T(8,128)(2,1)S(1)}, u32[]{:S(2)}, u32[]{:S(2)}) collective-permute-start(bf16[2,1040,128]{2,1,0:T(8,128)(2,1)S(1)} %pad_maximum_fusion.1), channel_id=1, source_target_pairs={{64,0},{208,16},{96,32},{240,48},{128,64},{16,80},{160,96},{48,112... | collective-permute-start | bytes 1597448 | tf_op jit(solution)/shard_map/ppermute | solution.py:48
  27.0 0.1 pad_add_fusion.position
  27.0 0.0 copy-done.1
  27.1 0.9 slice.42
  28.0 0.9 slice.43
  28.9 2.0 %collective-permute-start.9 = (bf16[240,256]{1,0:T(8,128)(2,1)S(1)}, bf16[240,256]{1,0:T(8,128)(2,1)S(1)}, u32[]{:S(2)}, u32[]{:S(2)}) collective-permute-start(bf16[240,256]{1,0:T(8,128)(2,1)S(1)} %slice.43), channel_id=1, source_target_pairs={{1,0},{2,1},{3,2},{0,3},{5,4},{6,5},{7,6},{4,7},{9,8},{10,9},{11,1... | collective-permute-start | bytes 368648 | tf_op jit(solution)/shard_map/ppermute | solution.py:40
  30.9 0.4 collective-permute-start.8
  31.4 2.8 %collective-permute-start.7 = (bf16[304,256]{1,0:T(8,128)(2,1)S(1)}, bf16[304,256]{1,0:T(8,128)(2,1)S(1)}, u32[]{:S(2)}, u32[]{:S(2)}) collective-permute-start(bf16[304,256]{1,0:T(8,128)(2,1)S(1)} %slice.41), channel_id=1, source_target_pairs={{4,0},{5,1},{6,2},{7,3},{8,4},{9,5},{10,6},{11,7},{12,8},{13,9},{1... | collective-permute-start | bytes 466952 | tf_op jit(solution)/shard_map/ppermute | solution.py:40
  34.2 0.0 collective-permute-start.6
  34.2 0.0 copy-done.5
  34.2 0.0 copy-done.3
  34.3 0.0 collective-permute-done.9
  34.3 2.6 %collective-permute-done.8 = bf16[240,256]{1,0:T(8,128)(2,1)S(1)} collective-permute-done((bf16[240,256]{1,0:T(8,128)(2,1)S(1)}, bf16[240,256]{1,0:T(8,128)(2,1)S(1)}, u32[]{:S(2)}, u32[]{:S(2)}) %collective-permute-start.8) | collective-permute-done | bytes 122912 | tf_op jit(solution)/shard_map/ppermute | solution.py:40
  36.8 0.0 collective-permute-done.7.refs_4_
  36.8 3.0 %collective-permute-done.6.refs_3_ = bf16[320,256]{1,0:T(8,128)(2,1)S(1)} collective-permute-done((bf16[320,256]{1,0:T(8,128)(2,1)S(1)}, bf16[320,256]{1,0:T(8,128)(2,1)S(1)}, u32[]{:S(2)}, u32[]{:S(2)}) %collective-permute-start.6) | collective-permute-done | bytes 163872 | tf_op jit(solution)/shard_map/ppermute | solution.py:40
  39.8 0.0 collective-permute-done.5
  39.9 0.1 collective-permute-start.12
  40.0 2.7 %collective-permute-start.11 = (bf16[1440,256]{1,0:T(8,128)(2,1)S(1)}, bf16[1440,256]{1,0:T(8,128)(2,1)S(1)}, u32[]{:S(2)}, u32[]{:S(2)}) collective-permute-start(bf16[1440,256]{1,0:T(8,128)(2,1)S(1)} %constant_dynamic-update-slice_fusion.refs_5_), channel_id=1, source_target_pairs={{4,0},{5,1},{6,2},{7,3},{8,4},{9,5},{10,6},{11,7},{12,8},{13,9},{1... | collective-permute-start | bytes 2211848 | tf_op jit(solution)/shard_map/ppermute | solution.py:40
  42.7 1.6 %collective-permute-start.14 = (bf16[576,256]{1,0:T(8,128)(2,1)S(1)}, bf16[576,256]{1,0:T(8,128)(2,1)S(1)}, u32[]{:S(2)}, u32[]{:S(2)}) collective-permute-start(bf16[576,256]{1,0:T(8,128)(2,1)S(1)} %pad_maximum_fusion.2), channel_id=1, source_target_pairs={{3,0},{0,1},{1,2},{2,3},{7,4},{4,5},{5,6},{6,7},{11,8},{8,9},{9,10... | collective-permute-start | bytes 884744 | tf_op jit(solution)/shard_map/ppermute | solution.py:40
  44.3 2.0 %collective-permute-start.13 = (bf16[576,256]{1,0:T(8,128)(2,1)S(1)}, bf16[576,256]{1,0:T(8,128)(2,1)S(1)}, u32[]{:S(2)}, u32[]{:S(2)}) collective-permute-start(bf16[576,256]{1,0:T(8,128)(2,1)S(1)} %pad_maximum_fusion.2), channel_id=1, source_target_pairs={{1,0},{2,1},{3,2},{0,3},{5,4},{6,5},{7,6},{4,7},{9,8},{10,9},{11,1... | collective-permute-start | bytes 884744 | tf_op jit(solution)/shard_map/ppermute | solution.py:40
  46.3 1.3 %collective-permute-start.10 = (bf16[2,1040,128]{2,1,0:T(8,128)(2,1)S(1)}, bf16[2,1040,128]{2,1,0:T(8,128)(2,1)S(1)}, u32[]{:S(2)}, u32[]{:S(2)}) collective-permute-start(bf16[2,1040,128]{2,1,0:T(8,128)(2,1)S(1)} %collective-permute-done.5), channel_id=1, source_target_pairs={{64,0},{208,16},{96,32},{240,48},{128,64},{16,80},{160,96},{48,112... | collective-permute-start | bytes 1597448 | tf_op jit(solution)/shard_map/ppermute | solution.py:48
  47.6 0.1 constant_dynamic-update-slice_fusion.6
  47.7 0.0 copy-start
  47.7 6.2 %collective-permute-done.14.refs_9_ = bf16[576,256]{1,0:T(8,128)(2,1)S(1)} collective-permute-done((bf16[576,256]{1,0:T(8,128)(2,1)S(1)}, bf16[576,256]{1,0:T(8,128)(2,1)S(1)}, u32[]{:S(2)}, u32[]{:S(2)}) %collective-permute-start.14) | collective-permute-done | bytes 294944 | tf_op jit(solution)/shard_map/ppermute | solution.py:40
  53.9 0.3 collective-permute-done.13.refs_8_
  54.2 1.7 %collective-permute-done.10 = bf16[2,1040,128]{2,1,0:T(8,128)(2,1)S(1)} collective-permute-done((bf16[2,1040,128]{2,1,0:T(8,128)(2,1)S(1)}, bf16[2,1040,128]{2,1,0:T(8,128)(2,1)S(1)}, u32[]{:S(2)}, u32[]{:S(2)}) %collective-permute-start.10) | collective-permute-done | bytes 532512 | tf_op jit(solution)/shard_map/ppermute | solution.py:48
  55.9 0.0 collective-permute-done.12.refs_7_
  55.9 0.0 collective-permute-done.11.refs_6_
  55.9 4.3 %collective-permute-start.15 = (bf16[2,1040,128]{2,1,0:T(8,128)(2,1)S(1)}, bf16[2,1040,128]{2,1,0:T(8,128)(2,1)S(1)}, u32[]{:S(2)}, u32[]{:S(2)}) collective-permute-start(bf16[2,1040,128]{2,1,0:T(8,128)(2,1)S(1)} %collective-permute-done.10), channel_id=1, source_target_pairs={{64,0},{208,16},{96,32},{240,48},{128,64},{16,80},{160,96},{48,112... | collective-permute-start | bytes 1597448 | tf_op jit(solution)/shard_map/ppermute | solution.py:48
  60.3 0.2 pad_maximum_fusion.tiles
  60.5 1.9 %collective-permute-start.18 = (bf16[288,256]{1,0:T(8,128)(2,1)S(1)}, bf16[288,256]{1,0:T(8,128)(2,1)S(1)}, u32[]{:S(2)}, u32[]{:S(2)}) collective-permute-start(bf16[288,256]{1,0:T(8,128)(2,1)S(1)} %slice.50), channel_id=1, source_target_pairs={{3,0},{0,1},{1,2},{2,3},{7,4},{4,5},{5,6},{6,7},{11,8},{8,9},{9,10... | collective-permute-start | bytes 442376 | tf_op jit(solution)/shard_map/ppermute | solution.py:40
  62.4 1.8 %collective-permute-start.19 = (bf16[288,256]{1,0:T(8,128)(2,1)S(1)}, bf16[288,256]{1,0:T(8,128)(2,1)S(1)}, u32[]{:S(2)}, u32[]{:S(2)}) collective-permute-start(bf16[288,256]{1,0:T(8,128)(2,1)S(1)} %slice.51), channel_id=1, source_target_pairs={{1,0},{2,1},{3,2},{0,3},{5,4},{6,5},{7,6},{4,7},{9,8},{10,9},{11,1... | collective-permute-start | bytes 442376 | tf_op jit(solution)/shard_map/ppermute | solution.py:40
  64.2 0.1 collective-permute-start.16
  64.3 2.7 %collective-permute-start.17 = (bf16[720,256]{1,0:T(8,128)(2,1)S(1)}, bf16[720,256]{1,0:T(8,128)(2,1)S(1)}, u32[]{:S(2)}, u32[]{:S(2)}) collective-permute-start(bf16[720,256]{1,0:T(8,128)(2,1)S(1)} %slice.49), channel_id=1, source_target_pairs={{4,0},{5,1},{6,2},{7,3},{8,4},{9,5},{10,6},{11,7},{12,8},{13,9},{1... | collective-permute-start | bytes 1105928 | tf_op jit(solution)/shard_map/ppermute | solution.py:40
  67.0 0.0 copy-done
  67.0 6.4 %first_part.1 = (bf16[32,624,128]{2,1,0:T(8,128)(2,1)S(1)}, f32[8,624,256]{2,1,0:T(8,128)S(1)}) custom-call(s32[2]{0:T(128)S(1)} %pad_add_fusion.position, bf16[6,1040,128]{2,1,0:T(8,128)(2,1)S(1)} %pad_maximum_fusion.tiles, bf16[624,256]{1,0:T(8,128)(2,1)S(1)} %copy-done, bf16[624,256]{1,0:T(8,128)(2,1)S(1)} %collective-permute-done.1.refs_1_, ...), custom_call_target="tpu_custom_call" | custom-call | flops 5000000000 | bytes 16000000 | tf_op jit(solution)/shard_map/first_part/pallas_call | solution.py:203
  73.3 0.1 constant_dynamic-update-slice_fusion.5
  73.4 0.0 collective-permute-done.18.refs_2_
  73.4 0.0 collective-permute-done.19.refs_3_
  73.4 0.0 collective-permute-done.16.refs_0_
  73.5 0.0 collective-permute-done.17.refs_1_
  73.5 0.0 collective-permute-done.15
  73.5 0.1 constant_dynamic-update-slice_fusion.4.tiles
  73.6 3.9 %collective-permute-start.20 = (bf16[8,1040,128]{2,1,0:T(8,128)(2,1)S(1)}, bf16[8,1040,128]{2,1,0:T(8,128)(2,1)S(1)}, u32[]{:S(2)}, u32[]{:S(2)}) collective-permute-start(bf16[8,1040,128]{2,1,0:T(8,128)(2,1)S(1)} %constant_dynamic-update-slice_fusion.4.tiles), channel_id=1, source_target_pairs={{16,0},{0,16},{48,32},{32,48},{80,64},{64,80},{112,96},{96,112},{1... | collective-permute-start | bytes 6389768 | tf_op jit(solution)/shard_map/ppermute | solution.py:48
  77.5 6.6 %second_part.1 = (bf16[32,624,128]{2,1,0:T(8,128)(2,1)S(1)}, f32[8,624,256]{2,1,0:T(8,128)S(1)}) custom-call(s32[2]{0:T(128)S(1)} %pad_add_fusion.position, bf16[8,1040,128]{2,1,0:T(8,128)(2,1)S(1)} %constant_dynamic-update-slice_fusion.4.tiles, ...), custom_call_target="tpu_custom_call", output_to_operand_aliasing={{0}: (2, {}), {1}: (3, {})} | custom-call | flops 5000000000 | bytes 16000000 | tf_op jit(solution)/shard_map/second_part/pallas_call | solution.py:203
  84.0 0.0 collective-permute-done.20.tiles
  84.0 8.8 %last_part.1 = bf16[624,2048]{1,0:T(8,128)(2,1)} custom-call(s32[2]{0:T(128)S(1)} %pad_add_fusion.position, bf16[8,1040,128]{2,1,0:T(8,128)(2,1)S(1)} %collective-permute-done.20.tiles, bf16[32,624,128]{2,1,0:T(8,128)(2,1)S(1)} %get-tuple-element.59.amps, f32[8,624,256]{2,1,0:T(8,128)S(1)} %get-tuple-element.60.before), custom_call_target="tpu_custom_call" | custom-call | flops 5000000000 | bytes 16000000 | tf_op jit(solution)/shard_map/last_part/pallas_call | solution.py:203
  (23 shorter events, 0.3 us)
Async XLA Ops:
  1.0 14.2 %collective-permute-start.4 = (bf16[480,256]{1,0:T(8,128)(2,1)S(1)}, bf16[480,256]{1,0:T(8,128)(2,1)S(1)}, u32[]{:S(2)}, u32[]{:S(2)}) collective-permute-start(bf16[480,256]{1,0:T(8,128)(2,1)S(1)} %slice.39), channel_id=1, source_target_pairs={{3,0},{0,1},{1,2},{2,3},{7,4},{4,5},{5,6},{6,7},{11,8},{8,9},{9,10... | collective-permute-start | bytes 737288 | tf_op jit(solution)/shard_map/ppermute | solution.py:40
  4.9 15.5 %collective-permute-start.3 = (bf16[480,256]{1,0:T(8,128)(2,1)S(1)}, bf16[480,256]{1,0:T(8,128)(2,1)S(1)}, u32[]{:S(2)}, u32[]{:S(2)}) collective-permute-start(bf16[480,256]{1,0:T(8,128)(2,1)S(1)} %slice.39), channel_id=1, source_target_pairs={{1,0},{2,1},{3,2},{0,3},{5,4},{6,5},{7,6},{4,7},{9,8},{10,9},{11,1... | collective-permute-start | bytes 737288 | tf_op jit(solution)/shard_map/ppermute | solution.py:40
  8.0 17.6 %collective-permute-start.2 = (bf16[624,256]{1,0:T(8,128)(2,1)}, bf16[624,256]{1,0:T(8,128)(2,1)S(1)}, u32[]{:S(2)}, u32[]{:S(2)}) collective-permute-start(bf16[624,256]{1,0:T(8,128)(2,1)} %refs_0_.1), channel_id=1, source_target_pairs={{12,0},{13,1},{14,2},{15,3},{0,4},{1,5},{2,6},{3,7},{4,8},{5,9},{6... | collective-permute-start | bytes 958472 | tf_op jit(solution)/shard_map/ppermute | solution.py:40
  9.3 16.3 %collective-permute-start.1 = (bf16[624,256]{1,0:T(8,128)(2,1)}, bf16[624,256]{1,0:T(8,128)(2,1)S(1)}, u32[]{:S(2)}, u32[]{:S(2)}) collective-permute-start(bf16[624,256]{1,0:T(8,128)(2,1)} %refs_0_.1), channel_id=1, source_target_pairs={{4,0},{5,1},{6,2},{7,3},{8,4},{9,5},{10,6},{11,7},{12,8},{13,9},{1... | collective-permute-start | bytes 958472 | tf_op jit(solution)/shard_map/ppermute | solution.py:40
  12.4 13.2 %collective-permute-start = (bf16[1040,128]{1,0:T(8,128)(2,1)S(1)}, bf16[1040,128]{1,0:T(8,128)(2,1)S(1)}, u32[]{:S(2)}, u32[]{:S(2)}) collective-permute-start(bf16[1040,128]{1,0:T(8,128)(2,1)S(1)} %get-tuple-element.62), channel_id=1, source_target_pairs={{32,0},{48,16},{0,32},{16,48},{96,64},{112,80},{64,96},{80,112},{1... | collective-permute-start | bytes 798728 | tf_op jit(solution)/shard_map/ppermute | solution.py:48
  14.1 12.9 %copy-start.1 = (bf16[1,8,128,128]{3,2,1,0:T(8,128)(2,1)S(1)}, bf16[1,8,128,128]{3,2,1,0:T(8,128)(2,1)}, u32[]{:S(2)}) copy-start(bf16[1,8,128,128]{3,2,1,0:T(8,128)(2,1)} %param.4) | copy-start | bytes 786436
  15.1 5.2 %copy-start.2 = (bf16[480,256]{1,0:T(8,128)(2,1)}, bf16[480,256]{1,0:T(8,128)(2,1)S(1)}, u32[]{:S(2)}) copy-start(bf16[480,256]{1,0:T(8,128)(2,1)S(1)} %collective-permute-done.4.refs_1_) | copy-start | bytes 737284
  20.3 0.7 copy-start.4
  21.0 13.1 %copy-start.5 = (bf16[480,256]{1,0:T(8,128)(2,1)S(1)}, bf16[480,256]{1,0:T(8,128)(2,1)}, u32[]{:S(2)}) copy-start(bf16[480,256]{1,0:T(8,128)(2,1)} %get-tuple-element.39) | copy-start | bytes 737284
  21.0 13.2 %copy-start.3 = (bf16[480,256]{1,0:T(8,128)(2,1)S(1)}, bf16[480,256]{1,0:T(8,128)(2,1)}, u32[]{:S(2)}) copy-start(bf16[480,256]{1,0:T(8,128)(2,1)} %get-tuple-element.38) | copy-start | bytes 737284
  25.7 14.2 %collective-permute-start.5 = (bf16[2,1040,128]{2,1,0:T(8,128)(2,1)S(1)}, bf16[2,1040,128]{2,1,0:T(8,128)(2,1)S(1)}, u32[]{:S(2)}, u32[]{:S(2)}) collective-permute-start(bf16[2,1040,128]{2,1,0:T(8,128)(2,1)S(1)} %pad_maximum_fusion.1), channel_id=1, source_target_pairs={{64,0},{208,16},{96,32},{240,48},{128,64},{16,80},{160,96},{48,112... | collective-permute-start | bytes 1597448 | tf_op jit(solution)/shard_map/ppermute | solution.py:48
  28.9 5.4 %collective-permute-start.9 = (bf16[240,256]{1,0:T(8,128)(2,1)S(1)}, bf16[240,256]{1,0:T(8,128)(2,1)S(1)}, u32[]{:S(2)}, u32[]{:S(2)}) collective-permute-start(bf16[240,256]{1,0:T(8,128)(2,1)S(1)} %slice.43), channel_id=1, source_target_pairs={{1,0},{2,1},{3,2},{0,3},{5,4},{6,5},{7,6},{4,7},{9,8},{10,9},{11,1... | collective-permute-start | bytes 368648 | tf_op jit(solution)/shard_map/ppermute | solution.py:40
  30.9 5.9 %collective-permute-start.8 = (bf16[240,256]{1,0:T(8,128)(2,1)S(1)}, bf16[240,256]{1,0:T(8,128)(2,1)S(1)}, u32[]{:S(2)}, u32[]{:S(2)}) collective-permute-start(bf16[240,256]{1,0:T(8,128)(2,1)S(1)} %slice.42), channel_id=1, source_target_pairs={{3,0},{0,1},{1,2},{2,3},{7,4},{4,5},{5,6},{6,7},{11,8},{8,9},{9,10... | collective-permute-start | bytes 368648 | tf_op jit(solution)/shard_map/ppermute | solution.py:40
  31.4 5.5 %collective-permute-start.7 = (bf16[304,256]{1,0:T(8,128)(2,1)S(1)}, bf16[304,256]{1,0:T(8,128)(2,1)S(1)}, u32[]{:S(2)}, u32[]{:S(2)}) collective-permute-start(bf16[304,256]{1,0:T(8,128)(2,1)S(1)} %slice.41), channel_id=1, source_target_pairs={{4,0},{5,1},{6,2},{7,3},{8,4},{9,5},{10,6},{11,7},{12,8},{13,9},{1... | collective-permute-start | bytes 466952 | tf_op jit(solution)/shard_map/ppermute | solution.py:40
  34.2 5.7 %collective-permute-start.6 = (bf16[320,256]{1,0:T(8,128)(2,1)S(1)}, bf16[320,256]{1,0:T(8,128)(2,1)S(1)}, u32[]{:S(2)}, u32[]{:S(2)}) collective-permute-start(bf16[320,256]{1,0:T(8,128)(2,1)S(1)} %slice.40), channel_id=1, source_target_pairs={{12,0},{13,1},{14,2},{15,3},{0,4},{1,5},{2,6},{3,7},{4,8},{5,9},{6... | collective-permute-start | bytes 491528 | tf_op jit(solution)/shard_map/ppermute | solution.py:40
  39.9 16.1 %collective-permute-start.12 = (bf16[1440,256]{1,0:T(8,128)(2,1)S(1)}, bf16[1440,256]{1,0:T(8,128)(2,1)S(1)}, u32[]{:S(2)}, u32[]{:S(2)}) collective-permute-start(bf16[1440,256]{1,0:T(8,128)(2,1)S(1)} %constant_dynamic-update-slice_fusion.refs_5_), channel_id=1, source_target_pairs={{12,0},{13,1},{14,2},{15,3},{0,4},{1,5},{2,6},{3,7},{4,8},{5,9},{6... | collective-permute-start | bytes 2211848 | tf_op jit(solution)/shard_map/ppermute | solution.py:40
  40.0 16.0 %collective-permute-start.11 = (bf16[1440,256]{1,0:T(8,128)(2,1)S(1)}, bf16[1440,256]{1,0:T(8,128)(2,1)S(1)}, u32[]{:S(2)}, u32[]{:S(2)}) collective-permute-start(bf16[1440,256]{1,0:T(8,128)(2,1)S(1)} %constant_dynamic-update-slice_fusion.refs_5_), channel_id=1, source_target_pairs={{4,0},{5,1},{6,2},{7,3},{8,4},{9,5},{10,6},{11,7},{12,8},{13,9},{1... | collective-permute-start | bytes 2211848 | tf_op jit(solution)/shard_map/ppermute | solution.py:40
  42.7 11.3 %collective-permute-start.14 = (bf16[576,256]{1,0:T(8,128)(2,1)S(1)}, bf16[576,256]{1,0:T(8,128)(2,1)S(1)}, u32[]{:S(2)}, u32[]{:S(2)}) collective-permute-start(bf16[576,256]{1,0:T(8,128)(2,1)S(1)} %pad_maximum_fusion.2), channel_id=1, source_target_pairs={{3,0},{0,1},{1,2},{2,3},{7,4},{4,5},{5,6},{6,7},{11,8},{8,9},{9,10... | collective-permute-start | bytes 884744 | tf_op jit(solution)/shard_map/ppermute | solution.py:40
  44.3 10.0 %collective-permute-start.13 = (bf16[576,256]{1,0:T(8,128)(2,1)S(1)}, bf16[576,256]{1,0:T(8,128)(2,1)S(1)}, u32[]{:S(2)}, u32[]{:S(2)}) collective-permute-start(bf16[576,256]{1,0:T(8,128)(2,1)S(1)} %pad_maximum_fusion.2), channel_id=1, source_target_pairs={{1,0},{2,1},{3,2},{0,3},{5,4},{6,5},{7,6},{4,7},{9,8},{10,9},{11,1... | collective-permute-start | bytes 884744 | tf_op jit(solution)/shard_map/ppermute | solution.py:40
  46.3 9.6 %collective-permute-start.10 = (bf16[2,1040,128]{2,1,0:T(8,128)(2,1)S(1)}, bf16[2,1040,128]{2,1,0:T(8,128)(2,1)S(1)}, u32[]{:S(2)}, u32[]{:S(2)}) collective-permute-start(bf16[2,1040,128]{2,1,0:T(8,128)(2,1)S(1)} %collective-permute-done.5), channel_id=1, source_target_pairs={{64,0},{208,16},{96,32},{240,48},{128,64},{16,80},{160,96},{48,112... | collective-permute-start | bytes 1597448 | tf_op jit(solution)/shard_map/ppermute | solution.py:48
  47.7 19.3 %copy-start = (bf16[624,256]{1,0:T(8,128)(2,1)S(1)}, bf16[624,256]{1,0:T(8,128)(2,1)}, u32[]{:S(2)}) copy-start(bf16[624,256]{1,0:T(8,128)(2,1)} %refs_0_.1) | copy-start | bytes 958468
  55.9 17.5 %collective-permute-start.15 = (bf16[2,1040,128]{2,1,0:T(8,128)(2,1)S(1)}, bf16[2,1040,128]{2,1,0:T(8,128)(2,1)S(1)}, u32[]{:S(2)}, u32[]{:S(2)}) collective-permute-start(bf16[2,1040,128]{2,1,0:T(8,128)(2,1)S(1)} %collective-permute-done.10), channel_id=1, source_target_pairs={{64,0},{208,16},{96,32},{240,48},{128,64},{16,80},{160,96},{48,112... | collective-permute-start | bytes 1597448 | tf_op jit(solution)/shard_map/ppermute | solution.py:48
  60.5 12.9 %collective-permute-start.18 = (bf16[288,256]{1,0:T(8,128)(2,1)S(1)}, bf16[288,256]{1,0:T(8,128)(2,1)S(1)}, u32[]{:S(2)}, u32[]{:S(2)}) collective-permute-start(bf16[288,256]{1,0:T(8,128)(2,1)S(1)} %slice.50), channel_id=1, source_target_pairs={{3,0},{0,1},{1,2},{2,3},{7,4},{4,5},{5,6},{6,7},{11,8},{8,9},{9,10... | collective-permute-start | bytes 442376 | tf_op jit(solution)/shard_map/ppermute | solution.py:40
  62.4 11.0 %collective-permute-start.19 = (bf16[288,256]{1,0:T(8,128)(2,1)S(1)}, bf16[288,256]{1,0:T(8,128)(2,1)S(1)}, u32[]{:S(2)}, u32[]{:S(2)}) collective-permute-start(bf16[288,256]{1,0:T(8,128)(2,1)S(1)} %slice.51), channel_id=1, source_target_pairs={{1,0},{2,1},{3,2},{0,3},{5,4},{6,5},{7,6},{4,7},{9,8},{10,9},{11,1... | collective-permute-start | bytes 442376 | tf_op jit(solution)/shard_map/ppermute | solution.py:40
  64.2 9.2 %collective-permute-start.16 = (bf16[720,256]{1,0:T(8,128)(2,1)S(1)}, bf16[720,256]{1,0:T(8,128)(2,1)S(1)}, u32[]{:S(2)}, u32[]{:S(2)}) collective-permute-start(bf16[720,256]{1,0:T(8,128)(2,1)S(1)} %slice.48), channel_id=1, source_target_pairs={{12,0},{13,1},{14,2},{15,3},{0,4},{1,5},{2,6},{3,7},{4,8},{5,9},{6... | collective-permute-start | bytes 1105928 | tf_op jit(solution)/shard_map/ppermute | solution.py:40
  64.3 9.1 %collective-permute-start.17 = (bf16[720,256]{1,0:T(8,128)(2,1)S(1)}, bf16[720,256]{1,0:T(8,128)(2,1)S(1)}, u32[]{:S(2)}, u32[]{:S(2)}) collective-permute-start(bf16[720,256]{1,0:T(8,128)(2,1)S(1)} %slice.49), channel_id=1, source_target_pairs={{4,0},{5,1},{6,2},{7,3},{8,4},{9,5},{10,6},{11,7},{12,8},{13,9},{1... | collective-permute-start | bytes 1105928 | tf_op jit(solution)/shard_map/ppermute | solution.py:40
  73.6 10.5 %collective-permute-start.20 = (bf16[8,1040,128]{2,1,0:T(8,128)(2,1)S(1)}, bf16[8,1040,128]{2,1,0:T(8,128)(2,1)S(1)}, u32[]{:S(2)}, u32[]{:S(2)}) collective-permute-start(bf16[8,1040,128]{2,1,0:T(8,128)(2,1)S(1)} %constant_dynamic-update-slice_fusion.4.tiles), channel_id=1, source_target_pairs={{16,0},{0,16},{48,32},{32,48},{80,64},{64,80},{112,96},{96,112},{1... | collective-permute-start | bytes 6389768 | tf_op jit(solution)/shard_map/ppermute | solution.py:48

commit v2 on v1

v2 whole, which is shorter than its diff:
```python
import functools
import itertools

import jax
import jax.numpy as jnp
from jax import lax
from jax.experimental import pallas as pl
from jax.experimental.pallas import tpu as pltpu
from jax.sharding import PartitionSpec as P

TILE = 128
NQ = 16
ROWS = 624
ROWS_A = 480
ROWS_B = ROWS - ROWS_A
HALF = 320
HALF_A = ROWS_A // 2
SLOTS = 8
HELD = 64
EARLY_SLOTS = 48
EARLY = (0, 1, 2, 3, 4, 5, 6, 8, 9, 10)
BATCH = 6
SPAN = 4
EMPTY = -1


def rank_of(d):
    return d ^ (d >> 1)


def fence(*values):
    return lax.optimization_barrier(values)


def from_col(value, dy=0, dz=0):
    perm = [
        ((y + dy) % 4 * 4 + (z + dz) % 4, y * 4 + z) for y in range(4) for z in range(4)
    ]
    return lax.ppermute(value, "col", perm)


def from_row(value, dx=0, dz=0, dcore=0):
    perm = []
    for x, z, core in itertools.product(range(4), range(2), range(2)):
        at_x = (x + dx * (1 - 2 * core)) % 4
        perm.append(((at_x * 2 + (z ^ dz)) * 2 + (core ^ dcore), (x * 2 + z) * 2 + core))
    return lax.ppermute(value, "row", perm)


def pair_tiles(position, tiles, wanted, codes, codes_smem, pairs, last, counts, sem):
    n = tiles.shape[0]
    y, z = position[0], position[1]
    lane = lax.broadcasted_iota(jnp.int32, (1, TILE), 1)
    for i in range(n):
        rows = tiles[i, SLOTS * TILE : SLOTS * TILE + 16, :].astype(jnp.float32)
        kt, qt = rows[0:1].astype(jnp.int32), rows[1:2].astype(jnp.int32)
        owner = kt >> 1
        place = rank_of(((owner & 3) - z) & 3) * 4 + rank_of(((owner >> 2) - y) & 3)
        block = (place * 2 + (kt & 1)) & 31
        slot = i * SLOTS + lane
        live = (kt >= 0) & wanted(slot, block)
        codes[i : i + 1, :] = jnp.where(live, ((qt & 15) * HELD + slot) * 32 + block, EMPTY)
    copy = pltpu.make_async_copy(codes, codes_smem, sem)
    copy.start()
    for q in range(NQ + 1):
        counts[q] = 0
    copy.wait()

    def put(i, n_pairs):
        for j in range(SLOTS):
            code = codes_smem[i, j]
            live = code >= 0
            q = jnp.where(live, code >> 11, NQ)
            count = counts[q]
            opens = (count & 1) == 0
            at = jnp.where(live, jnp.where(opens, n_pairs, last[q]), HELD + BATCH)
            counts[q] = count + 1
            last[q] = at
            pairs[at * 2] = jnp.where(opens, code, pairs[at * 2])
            pairs[at * 2 + 1] = jnp.where(opens, EMPTY, code)
            n_pairs = n_pairs + (live & opens).astype(jnp.int32)
        return n_pairs

    for q in range(NQ + 1):
        last[q] = 0
    n_pairs = lax.fori_loop(0, n, put, jnp.int32(0))
    for i in range(2 * BATCH):
        pairs[n_pairs * 2 + i] = EMPTY
    return n_pairs


def accumulate(n_pairs, pairs, tiles, amps, sums):
    def load(code):
        item = jnp.maximum(code, 0)
        slot = (item >> 5) & (HELD - 1)
        row = pl.ds(pl.multiple_of((slot & 7) * TILE, TILE), TILE)
        tile = tiles[slot >> 3, row, :]
        return amps[item & 31], jnp.where(code >= 0, tile, jnp.zeros_like(tile))

    def step(batch, carry):
        values = []
        for i in range(BATCH):
            at = (batch * BATCH + i) * 2
            (left, upper), (right, lower) = load(pairs[at]), load(pairs[at + 1])
            value = jnp.dot(
                jnp.concatenate([left, right], axis=1),
                jnp.concatenate([upper, lower], axis=0),
                preferred_element_type=jnp.float32,
            )
            values.append((jnp.maximum(pairs[at], 0) >> 11, value))
        for q, value in values:
            sums[q] += value
        return carry

    lax.fori_loop(0, (n_pairs + BATCH - 1) // BATCH, step, 0)


def moves(plan, pieces, amps, sem):
    return [
        pltpu.make_async_copy(
            pieces[ref].at[pl.ds(src, rows), pl.ds(sub * TILE, TILE)],
            amps.at[place * 2 + sub, pl.ds(dst, rows)],
            sem,
        )
        for ref, src, rows, place, dst in plan
        for sub in range(2)
    ]


def early_pair(slot, block):
    early = functools.reduce(jnp.logical_or, [(block >> 1) == place for place in EARLY])
    return (slot < EARLY_SLOTS) & early


def first_part(plan, n_pieces, position, tiles, *refs):
    sums, *pairing, code_sem, sem, amps = refs[n_pieces:]
    copies = moves(plan, refs[:n_pieces], amps, sem)
    for copy in copies:
        copy.start()
    sums[...] = jnp.zeros_like(sums)
    n_pairs = pair_tiles(position, tiles, early_pair, *pairing, code_sem)
    for copy in copies:
        copy.wait()
    accumulate(n_pairs, pairing[2], tiles, amps, sums)


def second_part(plan, n_pieces, position, tiles, *refs):
    amps, sums, *pairing, code_sem, sem = refs[n_pieces:]
    copies = moves(plan, refs[:n_pieces], amps, sem)
    for copy in copies:
        copy.start()
    sums[...] = jnp.zeros_like(sums)

    def wanted(slot, block):
        return jnp.logical_not(early_pair(slot, block))

    n_pairs = pair_tiles(position, tiles, wanted, *pairing, code_sem)
    for copy in copies:
        copy.wait()
    accumulate(n_pairs, pairing[2], tiles, amps, sums)


def last_part(position, tiles, amps, first_sums, second_sums, out, *refs):
    *pairing, code_sem, sums, stage, out_sem = refs
    sums[...] = first_sums[...] + second_sums[...]
    n_pairs = pair_tiles(position, tiles, lambda slot, block: slot >= 0, *pairing, code_sem)
    accumulate(n_pairs, pairing[2], tiles, amps, sums)
    writes = []
    for i in range(NQ // SPAN):
        for j in range(SPAN):
            stage[i, :, j * TILE : (j + 1) * TILE] = sums[i * SPAN + j].astype(jnp.bfloat16)
        columns = pl.ds(i * SPAN * TILE, SPAN * TILE)
        writes.append(pltpu.make_async_copy(stage.at[i], out.at[:, columns], out_sem.at[i]))
        writes[i].start()
    for write in writes:
        write.wait()


def call(body, out_shape, out_specs, arguments, scratch, name, aliases={}):
    pairing = [
        pltpu.VMEM((8, TILE), jnp.int32),
        pltpu.SMEM((8, TILE), jnp.int32),
        pltpu.SMEM((2 * (HELD + BATCH + 1),), jnp.int32),
        pltpu.SMEM((NQ + 1,), jnp.int32),
        pltpu.SMEM((NQ + 1,), jnp.int32),
        pltpu.SemaphoreType.DMA,
    ]
    return pl.pallas_call(
        body,
        out_shape=out_shape,
        in_specs=[pl.BlockSpec(memory_space=space) for _, space in arguments],
        out_specs=out_specs,
        scratch_shapes=pairing + scratch,
        input_output_aliases=aliases,
        compiler_params=pltpu.CompilerParams(vmem_limit_bytes=24 * 2**20),
        cost_estimate=pl.CostEstimate(
            flops=5_000_000_000, bytes_accessed=16_000_000, transcendentals=0
        ),
        name=name,
    )(*(array for array, _ in arguments))


def chosen_part(plan, arrays, chosen, space):
    steps = [step for step in plan if step[0] in chosen]
    return [(step[0] - chosen[0],) + step[1:] for step in steps], [(arrays[i], space) for i in chosen]


IN_VMEM = pl.BlockSpec(memory_space=pltpu.VMEM)
SUMS = [
    jax.ShapeDtypeStruct((32, ROWS, TILE), jnp.bfloat16),
    jax.ShapeDtypeStruct((NQ, ROWS, TILE), jnp.float32),
]


def contract_early(position, tiles, steps, pieces):
    return call(
        functools.partial(first_part, steps, len(pieces)),
        SUMS[1], IN_VMEM,
        [(position, pltpu.SMEM), (tiles, pltpu.VMEM)] + pieces,
        [pltpu.SemaphoreType.DMA, pltpu.VMEM((32, ROWS, TILE), jnp.bfloat16)], "first_part",
    )


def contract_late(position, own, other, first_sums, steps, pieces):
    smem, vmem, dma = pltpu.SMEM, pltpu.VMEM, pltpu.SemaphoreType.DMA
    amps, second_sums = call(
        functools.partial(second_part, steps, len(pieces)),
        SUMS, [IN_VMEM, IN_VMEM],
        [(position, smem), (own, vmem)] + pieces,
        [dma], "second_part",
    )
    return call(
        last_part,
        jax.ShapeDtypeStruct((ROWS, NQ * TILE), jnp.bfloat16),
        pl.BlockSpec(memory_space=pl.ANY),
        [(position, smem), (other, vmem), (amps, vmem), (first_sums, vmem), (second_sums, vmem)],
        [pltpu.VMEM((NQ, ROWS, TILE), jnp.float32), pltpu.VMEM((NQ // SPAN, ROWS, SPAN * TILE), jnp.bfloat16), dma((NQ // SPAN,))],
        "last_part",
    )


def shards(amplitudes, tiles, tile_ids):
    kt = jnp.where(tile_ids >= 0, tile_ids >> 4, -1)
    qt = tile_ids & 15
    ids = jnp.concatenate([kt, qt], axis=0).astype(jnp.bfloat16)
    ids = jnp.pad(ids, ((0, 14), (0, TILE - SLOTS)))
    block = jnp.concatenate([tiles.reshape(SLOTS * TILE, TILE), ids], axis=0)

    block_z = from_row(block, dz=1)
    y_up, y_down = (from_col(amplitudes, dy=dy) for dy in (1, 3))
    first = amplitudes[:ROWS_A]
    z_up, z_down = (from_col(first, dz=dz) for dz in (1, 3))
    block_z, y_up, y_down, z_up, z_down = fence(block_z, y_up, y_down, z_up, z_down)

    x_blocks = [jnp.stack([block, block_z])]
    x_blocks.append(from_row(x_blocks[-1], dx=1))
    y_top, y_low = from_col(y_down[:HALF], dy=3), from_col(y_up[HALF:], dy=1)
    z_top, z_low = from_col(z_down[:HALF_A], dz=3), from_col(z_up[HALF_A:], dz=1)
    x_blocks[-1], y_top, y_low, z_top, z_low = fence(x_blocks[-1], y_top, y_low, z_top, z_low)

    firsts = [jnp.concatenate([z_up, z_down, z_top, z_low], axis=0)]
    lasts = [jnp.concatenate([rows[ROWS_A:] for rows in (amplitudes, y_up, y_down)] + [y_low[ROWS_A - HALF :]], axis=0)]
    x_blocks.append(from_row(x_blocks[-1], dx=1))
    firsts += [from_col(firsts[0], dy=dy) for dy in (1, 3)]
    lasts += [from_col(lasts[0], dz=dz) for dz in (1, 3)]
    x_blocks[-1], firsts[1], firsts[2], lasts[1], lasts[2] = fence(
        x_blocks[-1], firsts[1], firsts[2], lasts[1], lasts[2]
    )

    plan = [(0, 0, ROWS, 0, 0), (1, 0, ROWS, 1, 0), (2, 0, ROWS, 2, 0), (3, 0, HALF, 3, 0)]
    plan.append((4, 0, ROWS - HALF, 3, HALF))
    for i in range(3):
        for j in range(3):
            plan.append((5 + i, j * ROWS_A, ROWS_A, 4 * (j + 1) + i, 0))
    plan += [(10, 0, ROWS_A, 7, 0), (10, ROWS_A, HALF_A, 11, 0)]
    plan += [(11, 0, HALF_A, 11, HALF_A), (11, HALF_A, ROWS_A, 15, 0)]
    for j in range(4):
        plan.append((8, j * ROWS_B, ROWS_B, 4 + j, ROWS_A))
        plan.append((9, j * ROWS_B, ROWS_B, 8 + j, ROWS_A))
        plan.append((12 + j // 2, j % 2 * ROWS_B, ROWS_B, 12 + j, ROWS_A))
    cut, cut_b = 3 * ROWS_A // 2, 2 * ROWS_B
    early_tiles = jnp.concatenate(x_blocks, axis=0)
    x_blocks.append(from_row(x_blocks[-1], dx=1))
    firsts += [from_col(firsts[2][:cut], dy=3), from_col(firsts[1][cut:], dy=1)]
    lasts += [from_col(lasts[2][:cut_b], dz=3), from_col(lasts[1][cut_b:], dz=1)]
    position = jnp.stack([lax.axis_index("col") // 4, lax.axis_index("col") % 4]).astype(jnp.int32)
    arrays = [amplitudes, y_up, y_down, y_top, y_low] + firsts[:3] + lasts[1:3] + firsts[3:] + lasts[3:]
    sums = contract_early(
        position, early_tiles, *chosen_part(plan, arrays, range(10), pl.ANY)
    )
    x_blocks[-1], sums, *arrays[10:] = fence(x_blocks[-1], sums, *arrays[10:])

    own = jnp.concatenate(x_blocks, axis=0)
    other = from_row(own, dcore=1)
    steps, pieces = chosen_part(plan, arrays, range(14), pl.ANY)
    return contract_late(position, own, other, sums, steps, pieces)


def solution(mesh):
    in_specs = (P("row", "col"), P("col", "row", None, None), P("col", "row"))
    out_specs = P("row", "col")
    return jax.shard_map(shards, mesh=mesh, in_specs=in_specs, out_specs=out_specs, check_vma=False)
```

time: 93 us -> 90.3 us (0.971)
  Pallas kernels: 21.7 us -> 17.4 us
  starting transfers between devices: 39.4 us -> 43.1 us
  local copies, waits for them, and re-layouts: 4.8 us -> 2.3 us
    ppermute x16, waiting for transfers between devices: 18.3 us -> 24.8 us  [from_col(): return lax.ppermute(value, 'col', perm)]
    ppermute x5, waiting for transfers between devices: 6.3 us -> 0.01 us  [from_row(): return lax.ppermute(value, 'row', perm)]
    pallas_call x3, Pallas kernels: 21.7 us -> 17.4 us  [call(): pl.pallas_call(body, out_shape=out_shape, in_specs=[pl.BlockSpec(memory_s...]
    ppermute x5, starting transfers between devices: 11.6 us -> 15.5 us  [from_row(): return lax.ppermute(value, 'row', perm)]
  transfers between devices with their start and end apart: 21 -> 21, of which waited for: 8 -> 6; matrix products, arithmetic and copies ran while one was open for 5% -> 4% of each run, Pallas kernels for 14% -> 11%
where the time goes in v2:
time: 90.3 us; the launch traced here: 90 us
  starting transfers between devices  43.1 us (48%)
  waiting for transfers between devices  24.8 us (27%)
  Pallas kernels  17.4 us (19%)
  local copies, waits for them, and re-layouts  2.3 us (3%)
  other arithmetic  2.03 us (2%)
    ppermute x16, starting transfers between devices, from_col(): return lax.ppermute(value, 'col', perm)  27.6 us
    ppermute x16, waiting for transfers between devices, from_col(): return lax.ppermute(value, 'col', perm)  24.8 us
    pallas_call x3, Pallas kernels, call(): pl.pallas_call(body, out_shape=out_shape, in_specs=[pl.BlockSpec(memory_s...  17.4 us
    ppermute x5, starting transfers between devices, from_row(): return lax.ppermute(value, 'row', perm)  15.5 us
  transfers between devices with their start and end apart: 21, of which 6 were waited for; matrix products, arithmetic and copies ran while one was open for 4% of the time, Pallas kernels for 11%

profile of v2, /device:TPU:1, one launch (start us, length us, event | category | flops | bytes accessed | tf_op | source)
XLA Modules:
  0.0 90.0 jit_solution(13434563538402111404)
XLA Ops:
  0.0 0.0 copy-start.1
  0.0 3.6 %collective-permute-start.1 = (bf16[624,256]{1,0:T(8,128)(2,1)}, bf16[624,256]{1,0:T(8,128)(2,1)S(1)}, u32[]{:S(2)}, u32[]{:S(2)}) collective-permute-start(bf16[624,256]{1,0:T(8,128)(2,1)} %refs_0_.3), channel_id=1, source_target_pairs={{4,0},{5,1},{6,2},{7,3},{8,4},{9,5},{10,6},{11,7},{12,8},{13,9},{1... | collective-permute-start | bytes 958472 | tf_op jit(solution)/shard_map/ppermute | solution.py:39
  3.6 0.0 collective-permute-start.2
  3.6 0.7 fusion.6
  4.2 1.0 %fusion.7 = (bf16[1,1040,128]{2,1,0:T(8,128)(2,1)S(1)}, bf16[1040,128]{1,0:T(8,128)(2,1)S(1)}) fusion(bf16[16,128]{1,0:T(8,128)(2,1)S(1)} %fusion.5, bf16[1024,128]{1,0:T(8,128)(2,1)} %bitcast.10), kind=kLoop, calls=%fused_computation.25 | loop fusion | flops 532480 | bytes 798720 | tf_op jit(solution)/shard_map/stack | solution.py:255
  5.3 1.7 %collective-permute-start = (bf16[1040,128]{1,0:T(8,128)(2,1)S(1)}, bf16[1040,128]{1,0:T(8,128)(2,1)S(1)}, u32[]{:S(2)}, u32[]{:S(2)}) collective-permute-start(bf16[1040,128]{1,0:T(8,128)(2,1)S(1)} %get-tuple-element.52), channel_id=1, source_target_pairs={{32,0},{48,16},{0,32},{16,48},{96,64},{112,80},{64,96},{80,112},{1... | collective-permute-start | bytes 798728 | tf_op jit(solution)/shard_map/ppermute | solution.py:47
  7.0 1.0 %slice.39 = bf16[480,256]{1,0:T(8,128)(2,1)S(1)} slice(bf16[624,256]{1,0:T(8,128)(2,1)} %refs_0_.3), slice={[0:480], [0:256]} | slice | bytes 491520 | tf_op jit(solution)/shard_map/slice | solution.py:251
  8.0 5.2 %collective-permute-start.3 = (bf16[480,256]{1,0:T(8,128)(2,1)S(1)}, bf16[480,256]{1,0:T(8,128)(2,1)S(1)}, u32[]{:S(2)}, u32[]{:S(2)}) collective-permute-start(bf16[480,256]{1,0:T(8,128)(2,1)S(1)} %slice.39), channel_id=1, source_target_pairs={{1,0},{2,1},{3,2},{0,3},{5,4},{6,5},{7,6},{4,7},{9,8},{10,9},{11,1... | collective-permute-start | bytes 737288 | tf_op jit(solution)/shard_map/ppermute | solution.py:39
  13.2 0.0 collective-permute-start.4
  13.2 0.9 slice.44
  14.0 3.2 %collective-permute-done.3 = bf16[480,256]{1,0:T(8,128)(2,1)S(1)} collective-permute-done((bf16[480,256]{1,0:T(8,128)(2,1)S(1)}, bf16[480,256]{1,0:T(8,128)(2,1)S(1)}, u32[]{:S(2)}, u32[]{:S(2)}) %collective-permute-start.3) | collective-permute-done | bytes 245792 | tf_op jit(solution)/shard_map/ppermute | solution.py:39
  17.2 10.9 %collective-permute-done.4 = bf16[480,256]{1,0:T(8,128)(2,1)S(1)} collective-permute-done((bf16[480,256]{1,0:T(8,128)(2,1)S(1)}, bf16[480,256]{1,0:T(8,128)(2,1)S(1)}, u32[]{:S(2)}, u32[]{:S(2)}) %collective-permute-start.4) | collective-permute-done | bytes 245792 | tf_op jit(solution)/shard_map/ppermute | solution.py:39
  28.1 0.0 collective-permute-done
  28.1 0.0 collective-permute-done.1.refs_1_
  28.1 0.0 collective-permute-done.2.refs_2_
  28.1 0.1 pad_maximum_fusion.1
  28.2 1.3 %collective-permute-start.5 = (bf16[2,1040,128]{2,1,0:T(8,128)(2,1)S(1)}, bf16[2,1040,128]{2,1,0:T(8,128)(2,1)S(1)}, u32[]{:S(2)}, u32[]{:S(2)}) collective-permute-start(bf16[2,1040,128]{2,1,0:T(8,128)(2,1)S(1)} %pad_maximum_fusion.1), channel_id=1, source_target_pairs={{64,0},{208,16},{96,32},{240,48},{128,64},{16,80},{160,96},{48,112... | collective-permute-start | bytes 1597448 | tf_op jit(solution)/shard_map/ppermute | solution.py:47
  29.5 0.1 pad_add_fusion.position
  29.6 0.0 copy-done.1
  29.6 0.1 collective-permute-start.6
  29.7 2.7 %collective-permute-start.7 = (bf16[304,256]{1,0:T(8,128)(2,1)S(1)}, bf16[304,256]{1,0:T(8,128)(2,1)S(1)}, u32[]{:S(2)}, u32[]{:S(2)}) collective-permute-start(bf16[304,256]{1,0:T(8,128)(2,1)S(1)} %slice.41), channel_id=1, source_target_pairs={{4,0},{5,1},{6,2},{7,3},{8,4},{9,5},{10,6},{11,7},{12,8},{13,9},{1... | collective-permute-start | bytes 466952 | tf_op jit(solution)/shard_map/ppermute | solution.py:39
  32.5 0.1 collective-permute-start.8
  32.6 3.6 %collective-permute-start.9 = (bf16[240,256]{1,0:T(8,128)(2,1)S(1)}, bf16[240,256]{1,0:T(8,128)(2,1)S(1)}, u32[]{:S(2)}, u32[]{:S(2)}) collective-permute-start(bf16[240,256]{1,0:T(8,128)(2,1)S(1)} %slice.43), channel_id=1, source_target_pairs={{1,0},{2,1},{3,2},{0,3},{5,4},{6,5},{7,6},{4,7},{9,8},{10,9},{11,1... | collective-permute-start | bytes 368648 | tf_op jit(solution)/shard_map/ppermute | solution.py:39
  36.3 2.1 %collective-permute-done.8 = bf16[240,256]{1,0:T(8,128)(2,1)S(1)} collective-permute-done((bf16[240,256]{1,0:T(8,128)(2,1)S(1)}, bf16[240,256]{1,0:T(8,128)(2,1)S(1)}, u32[]{:S(2)}, u32[]{:S(2)}) %collective-permute-start.8) | collective-permute-done | bytes 122912 | tf_op jit(solution)/shard_map/ppermute | solution.py:39
  38.4 0.3 collective-permute-done.9
  38.7 0.0 collective-permute-done.7.refs_4_
  38.7 0.0 collective-permute-done.6.refs_3_
  38.7 0.0 collective-permute-done.5
  38.8 1.4 %collective-permute-start.11 = (bf16[1440,256]{1,0:T(8,128)(2,1)S(1)}, bf16[1440,256]{1,0:T(8,128)(2,1)S(1)}, u32[]{:S(2)}, u32[]{:S(2)}) collective-permute-start(bf16[1440,256]{1,0:T(8,128)(2,1)S(1)} %constant_dynamic-update-slice_fusion.refs_5_), channel_id=1, source_target_pairs={{4,0},{5,1},{6,2},{7,3},{8,4},{9,5},{10,6},{11,7},{12,8},{13,9},{1... | collective-permute-start | bytes 2211848 | tf_op jit(solution)/shard_map/ppermute | solution.py:39
  40.2 0.2 collective-permute-start.12
  40.3 4.2 %collective-permute-start.13 = (bf16[576,256]{1,0:T(8,128)(2,1)S(1)}, bf16[576,256]{1,0:T(8,128)(2,1)S(1)}, u32[]{:S(2)}, u32[]{:S(2)}) collective-permute-start(bf16[576,256]{1,0:T(8,128)(2,1)S(1)} %pad_maximum_fusion.2), channel_id=1, source_target_pairs={{1,0},{2,1},{3,2},{0,3},{5,4},{6,5},{7,6},{4,7},{9,8},{10,9},{11,1... | collective-permute-start | bytes 884744 | tf_op jit(solution)/shard_map/ppermute | solution.py:39
  44.5 0.0 collective-permute-start.14
  44.5 3.0 %collective-permute-start.10 = (bf16[2,1040,128]{2,1,0:T(8,128)(2,1)S(1)}, bf16[2,1040,128]{2,1,0:T(8,128)(2,1)S(1)}, u32[]{:S(2)}, u32[]{:S(2)}) collective-permute-start(bf16[2,1040,128]{2,1,0:T(8,128)(2,1)S(1)} %collective-permute-done.5), channel_id=1, source_target_pairs={{64,0},{208,16},{96,32},{240,48},{128,64},{16,80},{160,96},{48,112... | collective-permute-start | bytes 1597448 | tf_op jit(solution)/shard_map/ppermute | solution.py:47
  47.6 0.1 constant_dynamic-update-slice_fusion.6
  47.7 0.0 copy-start
  47.7 3.9 %collective-permute-done.13.refs_8_ = bf16[576,256]{1,0:T(8,128)(2,1)S(1)} collective-permute-done((bf16[576,256]{1,0:T(8,128)(2,1)S(1)}, bf16[576,256]{1,0:T(8,128)(2,1)S(1)}, u32[]{:S(2)}, u32[]{:S(2)}) %collective-permute-start.13) | collective-permute-done | bytes 294944 | tf_op jit(solution)/shard_map/ppermute | solution.py:39
  51.6 4.3 %collective-permute-done.14.refs_9_ = bf16[576,256]{1,0:T(8,128)(2,1)S(1)} collective-permute-done((bf16[576,256]{1,0:T(8,128)(2,1)S(1)}, bf16[576,256]{1,0:T(8,128)(2,1)S(1)}, u32[]{:S(2)}, u32[]{:S(2)}) %collective-permute-start.14) | collective-permute-done | bytes 294944 | tf_op jit(solution)/shard_map/ppermute | solution.py:39
  55.9 0.0 collective-permute-done.10
  55.9 0.0 collective-permute-done.11.refs_6_
  56.0 0.0 collective-permute-done.12.refs_7_
  56.0 0.2 pad_maximum_fusion.tiles
  56.1 6.1 %collective-permute-start.15 = (bf16[2,1040,128]{2,1,0:T(8,128)(2,1)S(1)}, bf16[2,1040,128]{2,1,0:T(8,128)(2,1)S(1)}, u32[]{:S(2)}, u32[]{:S(2)}) collective-permute-start(bf16[2,1040,128]{2,1,0:T(8,128)(2,1)S(1)} %collective-permute-done.10), channel_id=1, source_target_pairs={{64,0},{208,16},{96,32},{240,48},{128,64},{16,80},{160,96},{48,112... | collective-permute-start | bytes 1597448 | tf_op jit(solution)/shard_map/ppermute | solution.py:47
  62.3 0.5 collective-permute-start.16
  62.8 2.4 %collective-permute-start.17 = (bf16[720,256]{1,0:T(8,128)(2,1)S(1)}, bf16[720,256]{1,0:T(8,128)(2,1)S(1)}, u32[]{:S(2)}, u32[]{:S(2)}) collective-permute-start(bf16[720,256]{1,0:T(8,128)(2,1)S(1)} %slice.49), channel_id=1, source_target_pairs={{4,0},{5,1},{6,2},{7,3},{8,4},{9,5},{10,6},{11,7},{12,8},{13,9},{1... | collective-permute-start | bytes 1105928 | tf_op jit(solution)/shard_map/ppermute | solution.py:39
  65.2 1.8 %collective-permute-start.18 = (bf16[288,256]{1,0:T(8,128)(2,1)S(1)}, bf16[288,256]{1,0:T(8,128)(2,1)S(1)}, u32[]{:S(2)}, u32[]{:S(2)}) collective-permute-start(bf16[288,256]{1,0:T(8,128)(2,1)S(1)} %slice.50), channel_id=1, source_target_pairs={{3,0},{0,1},{1,2},{2,3},{7,4},{4,5},{5,6},{6,7},{11,8},{8,9},{9,10... | collective-permute-start | bytes 442376 | tf_op jit(solution)/shard_map/ppermute | solution.py:39
  67.0 1.9 %collective-permute-start.19 = (bf16[288,256]{1,0:T(8,128)(2,1)S(1)}, bf16[288,256]{1,0:T(8,128)(2,1)S(1)}, u32[]{:S(2)}, u32[]{:S(2)}) collective-permute-start(bf16[288,256]{1,0:T(8,128)(2,1)S(1)} %slice.51), channel_id=1, source_target_pairs={{1,0},{2,1},{3,2},{0,3},{5,4},{6,5},{7,6},{4,7},{9,8},{10,9},{11,1... | collective-permute-start | bytes 442376 | tf_op jit(solution)/shard_map/ppermute | solution.py:39
  68.9 0.0 copy-done
  68.9 5.0 %first_part.1.first_sums = f32[16,624,128]{2,1,0:T(8,128)S(1)} custom-call(s32[2]{0:T(128)S(1)} %pad_add_fusion.position, bf16[6,1040,128]{2,1,0:T(8,128)(2,1)S(1)} %pad_maximum_fusion.tiles, bf16[624,256]{1,0:T(8,128)(2,1)S(1)} %copy-done, bf16[624,256]{1,0:T(8,128)(2,1)S(1)} %collective-permute-done.1.refs_1_, ...), custom_call_target="tpu_custom_call" | custom-call | flops 5000000000 | bytes 16000000 | tf_op jit(solution)/shard_map/first_part/pallas_call | solution.py:188
  73.9 0.1 constant_dynamic-update-slice_fusion.5
  74.0 0.0 collective-permute-done.18.refs_12_
  74.0 0.0 collective-permute-done.19.refs_13_
  74.0 0.0 collective-permute-done.16.refs_10_
  74.0 0.0 collective-permute-done.17.refs_11_
  74.0 0.0 collective-permute-done.15
  74.0 0.1 constant_dynamic-update-slice_fusion.4.tiles
  74.1 3.3 %collective-permute-start.20 = (bf16[8,1040,128]{2,1,0:T(8,128)(2,1)S(1)}, bf16[8,1040,128]{2,1,0:T(8,128)(2,1)S(1)}, u32[]{:S(2)}, u32[]{:S(2)}) collective-permute-start(bf16[8,1040,128]{2,1,0:T(8,128)(2,1)S(1)} %constant_dynamic-update-slice_fusion.4.tiles), channel_id=1, source_target_pairs={{16,0},{0,16},{48,32},{32,48},{80,64},{64,80},{112,96},{96,112},{1... | collective-permute-start | bytes 6389768 | tf_op jit(solution)/shard_map/ppermute | solution.py:47
  77.4 5.3 %second_part.1 = (bf16[32,624,128]{2,1,0:T(8,128)(2,1)S(1)}, f32[16,624,128]{2,1,0:T(8,128)S(1)}) custom-call(s32[2]{0:T(128)S(1)} %pad_add_fusion.position, bf16[8,1040,128]{2,1,0:T(8,128)(2,1)S(1)} %constant_dynamic-update-slice_fusion.4.tiles, bf16[624,256]{1,0:T(8,128)(2,1)S(1)} %copy-done, bf16[624,256]{1,0:T(8,128)(2,1)S(1)} %collective-permute-done.1.refs_1_, ...), custom_call_target="tpu_custom_call" | custom-call | flops 5000000000 | bytes 16000000 | tf_op jit(solution)/shard_map/second_part/pallas_call | solution.py:188
  82.7 0.0 collective-permute-done.20.tiles
  82.7 7.2 %last_part.1 = bf16[624,2048]{1,0:T(8,128)(2,1)} custom-call(s32[2]{0:T(128)S(1)} %pad_add_fusion.position, bf16[8,1040,128]{2,1,0:T(8,128)(2,1)S(1)} %collective-permute-done.20.tiles, bf16[32,624,128]{2,1,0:T(8,128)(2,1)S(1)} %get-tuple-element.48.amps, f32[16,624,128]{2,1,0:T(8,128)S(1)} %first_part.1.first_sums, ...), custom_call_target="tpu_custom_call" | custom-call | flops 5000000000 | bytes 16000000 | tf_op jit(solution)/shard_map/last_part/pallas_call | solution.py:188
  (19 shorter events, 0.3 us)
Async XLA Ops:
  0.0 29.6 %copy-start.1 = (bf16[1,8,128,128]{3,2,1,0:T(8,128)(2,1)S(1)}, bf16[1,8,128,128]{3,2,1,0:T(8,128)(2,1)}, u32[]{:S(2)}) copy-start(bf16[1,8,128,128]{3,2,1,0:T(8,128)(2,1)} %param.4) | copy-start | bytes 786436
  0.0 28.1 %collective-permute-start.1 = (bf16[624,256]{1,0:T(8,128)(2,1)}, bf16[624,256]{1,0:T(8,128)(2,1)S(1)}, u32[]{:S(2)}, u32[]{:S(2)}) collective-permute-start(bf16[624,256]{1,0:T(8,128)(2,1)} %refs_0_.3), channel_id=1, source_target_pairs={{4,0},{5,1},{6,2},{7,3},{8,4},{9,5},{10,6},{11,7},{12,8},{13,9},{1... | collective-permute-start | bytes 958472 | tf_op jit(solution)/shard_map/ppermute | solution.py:39
  3.6 24.6 %collective-permute-start.2 = (bf16[624,256]{1,0:T(8,128)(2,1)}, bf16[624,256]{1,0:T(8,128)(2,1)S(1)}, u32[]{:S(2)}, u32[]{:S(2)}) collective-permute-start(bf16[624,256]{1,0:T(8,128)(2,1)} %refs_0_.3), channel_id=1, source_target_pairs={{12,0},{13,1},{14,2},{15,3},{0,4},{1,5},{2,6},{3,7},{4,8},{5,9},{6... | collective-permute-start | bytes 958472 | tf_op jit(solution)/shard_map/ppermute | solution.py:39
  5.3 22.9 %collective-permute-start = (bf16[1040,128]{1,0:T(8,128)(2,1)S(1)}, bf16[1040,128]{1,0:T(8,128)(2,1)S(1)}, u32[]{:S(2)}, u32[]{:S(2)}) collective-permute-start(bf16[1040,128]{1,0:T(8,128)(2,1)S(1)} %get-tuple-element.52), channel_id=1, source_target_pairs={{32,0},{48,16},{0,32},{16,48},{96,64},{112,80},{64,96},{80,112},{1... | collective-permute-start | bytes 798728 | tf_op jit(solution)/shard_map/ppermute | solution.py:47
  8.0 9.3 %collective-permute-start.3 = (bf16[480,256]{1,0:T(8,128)(2,1)S(1)}, bf16[480,256]{1,0:T(8,128)(2,1)S(1)}, u32[]{:S(2)}, u32[]{:S(2)}) collective-permute-start(bf16[480,256]{1,0:T(8,128)(2,1)S(1)} %slice.39), channel_id=1, source_target_pairs={{1,0},{2,1},{3,2},{0,3},{5,4},{6,5},{7,6},{4,7},{9,8},{10,9},{11,1... | collective-permute-start | bytes 737288 | tf_op jit(solution)/shard_map/ppermute | solution.py:39
  13.2 15.0 %collective-permute-start.4 = (bf16[480,256]{1,0:T(8,128)(2,1)S(1)}, bf16[480,256]{1,0:T(8,128)(2,1)S(1)}, u32[]{:S(2)}, u32[]{:S(2)}) collective-permute-start(bf16[480,256]{1,0:T(8,128)(2,1)S(1)} %slice.39), channel_id=1, source_target_pairs={{3,0},{0,1},{1,2},{2,3},{7,4},{4,5},{5,6},{6,7},{11,8},{8,9},{9,10... | collective-permute-start | bytes 737288 | tf_op jit(solution)/shard_map/ppermute | solution.py:39
  28.2 10.5 %collective-permute-start.5 = (bf16[2,1040,128]{2,1,0:T(8,128)(2,1)S(1)}, bf16[2,1040,128]{2,1,0:T(8,128)(2,1)S(1)}, u32[]{:S(2)}, u32[]{:S(2)}) collective-permute-start(bf16[2,1040,128]{2,1,0:T(8,128)(2,1)S(1)} %pad_maximum_fusion.1), channel_id=1, source_target_pairs={{64,0},{208,16},{96,32},{240,48},{128,64},{16,80},{160,96},{48,112... | collective-permute-start | bytes 1597448 | tf_op jit(solution)/shard_map/ppermute | solution.py:47
  29.6 9.1 %collective-permute-start.6 = (bf16[320,256]{1,0:T(8,128)(2,1)S(1)}, bf16[320,256]{1,0:T(8,128)(2,1)S(1)}, u32[]{:S(2)}, u32[]{:S(2)}) collective-permute-start(bf16[320,256]{1,0:T(8,128)(2,1)S(1)} %slice.40), channel_id=1, source_target_pairs={{12,0},{13,1},{14,2},{15,3},{0,4},{1,5},{2,6},{3,7},{4,8},{5,9},{6... | collective-permute-start | bytes 491528 | tf_op jit(solution)/shard_map/ppermute | solution.py:39
  29.7 9.0 %collective-permute-start.7 = (bf16[304,256]{1,0:T(8,128)(2,1)S(1)}, bf16[304,256]{1,0:T(8,128)(2,1)S(1)}, u32[]{:S(2)}, u32[]{:S(2)}) collective-permute-start(bf16[304,256]{1,0:T(8,128)(2,1)S(1)} %slice.41), channel_id=1, source_target_pairs={{4,0},{5,1},{6,2},{7,3},{8,4},{9,5},{10,6},{11,7},{12,8},{13,9},{1... | collective-permute-start | bytes 466952 | tf_op jit(solution)/shard_map/ppermute | solution.py:39
  32.5 5.9 %collective-permute-start.8 = (bf16[240,256]{1,0:T(8,128)(2,1)S(1)}, bf16[240,256]{1,0:T(8,128)(2,1)S(1)}, u32[]{:S(2)}, u32[]{:S(2)}) collective-permute-start(bf16[240,256]{1,0:T(8,128)(2,1)S(1)} %slice.42), channel_id=1, source_target_pairs={{3,0},{0,1},{1,2},{2,3},{7,4},{4,5},{5,6},{6,7},{11,8},{8,9},{9,10... | collective-permute-start | bytes 368648 | tf_op jit(solution)/shard_map/ppermute | solution.py:39
  32.6 6.1 %collective-permute-start.9 = (bf16[240,256]{1,0:T(8,128)(2,1)S(1)}, bf16[240,256]{1,0:T(8,128)(2,1)S(1)}, u32[]{:S(2)}, u32[]{:S(2)}) collective-permute-start(bf16[240,256]{1,0:T(8,128)(2,1)S(1)} %slice.43), channel_id=1, source_target_pairs={{1,0},{2,1},{3,2},{0,3},{5,4},{6,5},{7,6},{4,7},{9,8},{10,9},{11,1... | collective-permute-start | bytes 368648 | tf_op jit(solution)/shard_map/ppermute | solution.py:39
  38.8 17.2 %collective-permute-start.11 = (bf16[1440,256]{1,0:T(8,128)(2,1)S(1)}, bf16[1440,256]{1,0:T(8,128)(2,1)S(1)}, u32[]{:S(2)}, u32[]{:S(2)}) collective-permute-start(bf16[1440,256]{1,0:T(8,128)(2,1)S(1)} %constant_dynamic-update-slice_fusion.refs_5_), channel_id=1, source_target_pairs={{4,0},{5,1},{6,2},{7,3},{8,4},{9,5},{10,6},{11,7},{12,8},{13,9},{1... | collective-permute-start | bytes 2211848 | tf_op jit(solution)/shard_map/ppermute | solution.py:39
  40.2 15.8 %collective-permute-start.12 = (bf16[1440,256]{1,0:T(8,128)(2,1)S(1)}, bf16[1440,256]{1,0:T(8,128)(2,1)S(1)}, u32[]{:S(2)}, u32[]{:S(2)}) collective-permute-start(bf16[1440,256]{1,0:T(8,128)(2,1)S(1)} %constant_dynamic-update-slice_fusion.refs_5_), channel_id=1, source_target_pairs={{12,0},{13,1},{14,2},{15,3},{0,4},{1,5},{2,6},{3,7},{4,8},{5,9},{6... | collective-permute-start | bytes 2211848 | tf_op jit(solution)/shard_map/ppermute | solution.py:39
  40.3 11.3 %collective-permute-start.13 = (bf16[576,256]{1,0:T(8,128)(2,1)S(1)}, bf16[576,256]{1,0:T(8,128)(2,1)S(1)}, u32[]{:S(2)}, u32[]{:S(2)}) collective-permute-start(bf16[576,256]{1,0:T(8,128)(2,1)S(1)} %pad_maximum_fusion.2), channel_id=1, source_target_pairs={{1,0},{2,1},{3,2},{0,3},{5,4},{6,5},{7,6},{4,7},{9,8},{10,9},{11,1... | collective-permute-start | bytes 884744 | tf_op jit(solution)/shard_map/ppermute | solution.py:39
  44.5 11.4 %collective-permute-start.14 = (bf16[576,256]{1,0:T(8,128)(2,1)S(1)}, bf16[576,256]{1,0:T(8,128)(2,1)S(1)}, u32[]{:S(2)}, u32[]{:S(2)}) collective-permute-start(bf16[576,256]{1,0:T(8,128)(2,1)S(1)} %pad_maximum_fusion.2), channel_id=1, source_target_pairs={{3,0},{0,1},{1,2},{2,3},{7,4},{4,5},{5,6},{6,7},{11,8},{8,9},{9,10... | collective-permute-start | bytes 884744 | tf_op jit(solution)/shard_map/ppermute | solution.py:39
  44.5 11.4 %collective-permute-start.10 = (bf16[2,1040,128]{2,1,0:T(8,128)(2,1)S(1)}, bf16[2,1040,128]{2,1,0:T(8,128)(2,1)S(1)}, u32[]{:S(2)}, u32[]{:S(2)}) collective-permute-start(bf16[2,1040,128]{2,1,0:T(8,128)(2,1)S(1)} %collective-permute-done.5), channel_id=1, source_target_pairs={{64,0},{208,16},{96,32},{240,48},{128,64},{16,80},{160,96},{48,112... | collective-permute-start | bytes 1597448 | tf_op jit(solution)/shard_map/ppermute | solution.py:47
  47.7 21.2 %copy-start = (bf16[624,256]{1,0:T(8,128)(2,1)S(1)}, bf16[624,256]{1,0:T(8,128)(2,1)}, u32[]{:S(2)}) copy-start(bf16[624,256]{1,0:T(8,128)(2,1)} %refs_0_.3) | copy-start | bytes 958468
  56.1 17.9 %collective-permute-start.15 = (bf16[2,1040,128]{2,1,0:T(8,128)(2,1)S(1)}, bf16[2,1040,128]{2,1,0:T(8,128)(2,1)S(1)}, u32[]{:S(2)}, u32[]{:S(2)}) collective-permute-start(bf16[2,1040,128]{2,1,0:T(8,128)(2,1)S(1)} %collective-permute-done.10), channel_id=1, source_target_pairs={{64,0},{208,16},{96,32},{240,48},{128,64},{16,80},{160,96},{48,112... | collective-permute-start | bytes 1597448 | tf_op jit(solution)/shard_map/ppermute | solution.py:47
  62.3 11.7 %collective-permute-start.16 = (bf16[720,256]{1,0:T(8,128)(2,1)S(1)}, bf16[720,256]{1,0:T(8,128)(2,1)S(1)}, u32[]{:S(2)}, u32[]{:S(2)}) collective-permute-start(bf16[720,256]{1,0:T(8,128)(2,1)S(1)} %slice.48), channel_id=1, source_target_pairs={{12,0},{13,1},{14,2},{15,3},{0,4},{1,5},{2,6},{3,7},{4,8},{5,9},{6... | collective-permute-start | bytes 1105928 | tf_op jit(solution)/shard_map/ppermute | solution.py:39
  62.8 11.2 %collective-permute-start.17 = (bf16[720,256]{1,0:T(8,128)(2,1)S(1)}, bf16[720,256]{1,0:T(8,128)(2,1)S(1)}, u32[]{:S(2)}, u32[]{:S(2)}) collective-permute-start(bf16[720,256]{1,0:T(8,128)(2,1)S(1)} %slice.49), channel_id=1, source_target_pairs={{4,0},{5,1},{6,2},{7,3},{8,4},{9,5},{10,6},{11,7},{12,8},{13,9},{1... | collective-permute-start | bytes 1105928 | tf_op jit(solution)/shard_map/ppermute | solution.py:39
  65.2 8.8 %collective-permute-start.18 = (bf16[288,256]{1,0:T(8,128)(2,1)S(1)}, bf16[288,256]{1,0:T(8,128)(2,1)S(1)}, u32[]{:S(2)}, u32[]{:S(2)}) collective-permute-start(bf16[288,256]{1,0:T(8,128)(2,1)S(1)} %slice.50), channel_id=1, source_target_pairs={{3,0},{0,1},{1,2},{2,3},{7,4},{4,5},{5,6},{6,7},{11,8},{8,9},{9,10... | collective-permute-start | bytes 442376 | tf_op jit(solution)/shard_map/ppermute | solution.py:39
  67.0 7.0 %collective-permute-start.19 = (bf16[288,256]{1,0:T(8,128)(2,1)S(1)}, bf16[288,256]{1,0:T(8,128)(2,1)S(1)}, u32[]{:S(2)}, u32[]{:S(2)}) collective-permute-start(bf16[288,256]{1,0:T(8,128)(2,1)S(1)} %slice.51), channel_id=1, source_target_pairs={{1,0},{2,1},{3,2},{0,3},{5,4},{6,5},{7,6},{4,7},{9,8},{10,9},{11,1... | collective-permute-start | bytes 442376 | tf_op jit(solution)/shard_map/ppermute | solution.py:39
  74.1 8.6 %collective-permute-start.20 = (bf16[8,1040,128]{2,1,0:T(8,128)(2,1)S(1)}, bf16[8,1040,128]{2,1,0:T(8,128)(2,1)S(1)}, u32[]{:S(2)}, u32[]{:S(2)}) collective-permute-start(bf16[8,1040,128]{2,1,0:T(8,128)(2,1)S(1)} %constant_dynamic-update-slice_fusion.4.tiles), channel_id=1, source_target_pairs={{16,0},{0,16},{48,32},{32,48},{80,64},{64,80},{112,96},{96,112},{1... | collective-permute-start | bytes 6389768 | tf_op jit(solution)/shard_map/ppermute | solution.py:47

commit v3 on v2

--- a/solution.py
+++ b/solution.py
@@ -250,22 +250,21 @@
     y_up, y_down = (from_col(amplitudes, dy=dy) for dy in (1, 3))
     first = amplitudes[:ROWS_A]
     z_up, z_down = (from_col(first, dz=dz) for dz in (1, 3))
-    block_z, y_up, y_down, z_up, z_down = fence(block_z, y_up, y_down, z_up, z_down)
-
-    x_blocks = [jnp.stack([block, block_z])]
+    both = jnp.stack([block, block_z])
+    near = jnp.concatenate([z_up, z_down], axis=0)
+    both, y_up, y_down, near = fence(both, y_up, y_down, near)
+
+    x_blocks = [both]
     x_blocks.append(from_row(x_blocks[-1], dx=1))
     y_top, y_low = from_col(y_down[:HALF], dy=3), from_col(y_up[HALF:], dy=1)
-    z_top, z_low = from_col(z_down[:HALF_A], dz=3), from_col(z_up[HALF_A:], dz=1)
-    x_blocks[-1], y_top, y_low, z_top, z_low = fence(x_blocks[-1], y_top, y_low, z_top, z_low)
-
-    firsts = [jnp.concatenate([z_up, z_down, z_top, z_low], axis=0)]
+    z_top, z_low = from_col(near[ROWS_A : ROWS_A + HALF_A], dz=3), from_col(near[HALF_A:ROWS_A], dz=1)
+    firsts = [jnp.concatenate([near, z_top, z_low], axis=0)]
+    x_blocks[-1], y_top, y_low, firsts[0] = fence(x_blocks[-1], y_top, y_low, firsts[0])
+
     lasts = [jnp.concatenate([rows[ROWS_A:] for rows in (amplitudes, y_up, y_down)] + [y_low[ROWS_A - HALF :]], axis=0)]
     x_blocks.append(from_row(x_blocks[-1], dx=1))
     firsts += [from_col(firsts[0], dy=dy) for dy in (1, 3)]
     lasts += [from_col(lasts[0], dz=dz) for dz in (1, 3)]
-    x_blocks[-1], firsts[1], firsts[2], lasts[1], lasts[2] = fence(
-        x_blocks[-1], firsts[1], firsts[2], lasts[1], lasts[2]
-    )
 
     plan = [(0, 0, ROWS, 0, 0), (1, 0, ROWS, 1, 0), (2, 0, ROWS, 2, 0), (3, 0, HALF, 3, 0)]
     plan.append((4, 0, ROWS - HALF, 3, HALF))

time: 90.3 us -> 85.6 us (0.948)
  starting transfers between devices: 43.1 us -> 38.5 us
    ppermute x5, waiting for transfers between devices: 0.01 us -> 5.76 us  [from_row(): return lax.ppermute(value, 'row', perm)]
    ppermute x16, waiting for transfers between devices: 24.8 us -> 19.4 us  [from_col(): return lax.ppermute(value, 'col', perm)]
    ppermute x5, starting transfers between devices: 15.5 us -> 10.7 us  [from_row(): return lax.ppermute(value, 'row', perm)]
  transfers between devices with their start and end apart: 21 -> 21, of which waited for: 6 -> 8; matrix products, arithmetic and copies ran while one was open for 4% -> 3% of each run, Pallas kernels for 11% -> 12%
where the time goes in v3:
time: 85.6 us; the launch traced here: 85.7 us
  starting transfers between devices  38.5 us (45%)
  waiting for transfers between devices  25.1 us (29%)
  Pallas kernels  18.2 us (21%)
  other arithmetic  2.09 us (2%)
  local copies, waits for them, and re-layouts  1.42 us (2%)
    ppermute x16, starting transfers between devices, from_col(): return lax.ppermute(value, 'col', perm)  27.8 us
    ppermute x16, waiting for transfers between devices, from_col(): return lax.ppermute(value, 'col', perm)  19.4 us
    pallas_call x3, Pallas kernels, call(): pl.pallas_call(body, out_shape=out_shape, in_specs=[pl.BlockSpec(memory_s...  18.2 us
    ppermute x5, starting transfers between devices, from_row(): return lax.ppermute(value, 'row', perm)  10.7 us
    ppermute x5, waiting for transfers between devices, from_row(): return lax.ppermute(value, 'row', perm)  5.76 us
  transfers between devices with their start and end apart: 21, of which 8 were waited for; matrix products, arithmetic and copies ran while one was open for 3% of the time, Pallas kernels for 12%

profile of v3, /device:TPU:1, one launch (start us, length us, event | category | flops | bytes accessed | tf_op | source)
XLA Modules:
  0.0 85.7 jit_solution(14613243437830974076)
XLA Ops:
  0.0 0.0 copy-start
  0.0 1.0 %slice.39 = bf16[480,256]{1,0:T(8,128)(2,1)S(1)} slice(bf16[624,256]{1,0:T(8,128)(2,1)} %refs_0_.3), slice={[0:480], [0:256]} | slice | bytes 491520 | tf_op jit(solution)/shard_map/slice | solution.py:251
  1.0 6.9 %collective-permute-start.3 = (bf16[480,256]{1,0:T(8,128)(2,1)S(1)}, bf16[480,256]{1,0:T(8,128)(2,1)S(1)}, u32[]{:S(2)}, u32[]{:S(2)}) collective-permute-start(bf16[480,256]{1,0:T(8,128)(2,1)S(1)} %slice.39), channel_id=1, source_target_pairs={{1,0},{2,1},{3,2},{0,3},{5,4},{6,5},{7,6},{4,7},{9,8},{10,9},{11,1... | collective-permute-start | bytes 737288 | tf_op jit(solution)/shard_map/ppermute | solution.py:39
  8.0 0.0 collective-permute-start.4
  8.0 0.7 fusion.6
  8.6 1.0 %fusion.7 = (bf16[1,1040,128]{2,1,0:T(8,128)(2,1)S(1)}, bf16[1040,128]{1,0:T(8,128)(2,1)S(1)}) fusion(bf16[16,128]{1,0:T(8,128)(2,1)S(1)} %fusion.5, bf16[1024,128]{1,0:T(8,128)(2,1)} %bitcast.7), kind=kLoop, calls=%fused_computation.22 | loop fusion | flops 532480 | bytes 798720 | tf_op jit(solution)/shard_map/stack | solution.py:253
  9.7 0.8 collective-permute-start
  10.5 2.7 %collective-permute-start.1 = (bf16[624,256]{1,0:T(8,128)(2,1)}, bf16[624,256]{1,0:T(8,128)(2,1)S(1)}, u32[]{:S(2)}, u32[]{:S(2)}) collective-permute-start(bf16[624,256]{1,0:T(8,128)(2,1)} %refs_0_.3), channel_id=1, source_target_pairs={{4,0},{5,1},{6,2},{7,3},{8,4},{9,5},{10,6},{11,7},{12,8},{13,9},{1... | collective-permute-start | bytes 958472 | tf_op jit(solution)/shard_map/ppermute | solution.py:39
  13.2 0.0 collective-permute-start.2
  13.2 2.6 %collective-permute-done.3 = bf16[480,256]{1,0:T(8,128)(2,1)S(1)} collective-permute-done((bf16[480,256]{1,0:T(8,128)(2,1)S(1)}, bf16[480,256]{1,0:T(8,128)(2,1)S(1)}, u32[]{:S(2)}, u32[]{:S(2)}) %collective-permute-start.3) | collective-permute-done | bytes 245792 | tf_op jit(solution)/shard_map/ppermute | solution.py:39
  15.8 2.7 %collective-permute-done.4 = bf16[480,256]{1,0:T(8,128)(2,1)S(1)} collective-permute-done((bf16[480,256]{1,0:T(8,128)(2,1)S(1)}, bf16[480,256]{1,0:T(8,128)(2,1)S(1)}, u32[]{:S(2)}, u32[]{:S(2)}) %collective-permute-start.4) | collective-permute-done | bytes 245792 | tf_op jit(solution)/shard_map/ppermute | solution.py:39
  18.5 5.7 %collective-permute-done = bf16[1040,128]{1,0:T(8,128)(2,1)S(1)} collective-permute-done((bf16[1040,128]{1,0:T(8,128)(2,1)S(1)}, bf16[1040,128]{1,0:T(8,128)(2,1)S(1)}, u32[]{:S(2)}, u32[]{:S(2)}) %collective-permute-start) | collective-permute-done | bytes 266272 | tf_op jit(solution)/shard_map/ppermute | solution.py:47
  24.3 0.1 pad_maximum_fusion.2
  24.4 0.0 collective-permute-done.1.refs_1_
  24.4 0.0 collective-permute-done.2.refs_2_
  24.4 1.3 %collective-permute-start.5 = (bf16[2,1040,128]{2,1,0:T(8,128)(2,1)S(1)}, bf16[2,1040,128]{2,1,0:T(8,128)(2,1)S(1)}, u32[]{:S(2)}, u32[]{:S(2)}) collective-permute-start(bf16[2,1040,128]{2,1,0:T(8,128)(2,1)S(1)} %pad_maximum_fusion.2), channel_id=1, source_target_pairs={{64,0},{208,16},{96,32},{240,48},{128,64},{16,80},{160,96},{48,112... | collective-permute-start | bytes 1597448 | tf_op jit(solution)/shard_map/ppermute | solution.py:47
  25.7 1.1 %collective-permute-start.8 = (bf16[240,256]{1,0:T(8,128)(2,1)S(1)}, bf16[240,256]{1,0:T(8,128)(2,1)S(1)}, u32[]{:S(2)}, u32[]{:S(2)}) collective-permute-start(bf16[240,256]{1,0:T(8,128)(2,1)S(1)} %get-tuple-element.37), channel_id=1, source_target_pairs={{3,0},{0,1},{1,2},{2,3},{7,4},{4,5},{5,6},{6,7},{11,8},{8,9},{9,10... | collective-permute-start | bytes 368648 | tf_op jit(solution)/shard_map/ppermute | solution.py:39
  26.8 2.5 %collective-permute-start.9 = (bf16[240,256]{1,0:T(8,128)(2,1)S(1)}, bf16[240,256]{1,0:T(8,128)(2,1)S(1)}, u32[]{:S(2)}, u32[]{:S(2)}) collective-permute-start(bf16[240,256]{1,0:T(8,128)(2,1)S(1)} %get-tuple-element.38), channel_id=1, source_target_pairs={{1,0},{2,1},{3,2},{0,3},{5,4},{6,5},{7,6},{4,7},{9,8},{10,9},{11,1... | collective-permute-start | bytes 368648 | tf_op jit(solution)/shard_map/ppermute | solution.py:39
  29.3 0.0 copy-done
  29.4 0.1 pad_add_fusion.position
  29.5 1.4 %collective-permute-start.6 = (bf16[320,256]{1,0:T(8,128)(2,1)S(1)}, bf16[320,256]{1,0:T(8,128)(2,1)S(1)}, u32[]{:S(2)}, u32[]{:S(2)}) collective-permute-start(bf16[320,256]{1,0:T(8,128)(2,1)S(1)} %slice.40), channel_id=1, source_target_pairs={{12,0},{13,1},{14,2},{15,3},{0,4},{1,5},{2,6},{3,7},{4,8},{5,9},{6... | collective-permute-start | bytes 491528 | tf_op jit(solution)/shard_map/ppermute | solution.py:39
  30.9 1.5 %collective-permute-start.7 = (bf16[304,256]{1,0:T(8,128)(2,1)S(1)}, bf16[304,256]{1,0:T(8,128)(2,1)S(1)}, u32[]{:S(2)}, u32[]{:S(2)}) collective-permute-start(bf16[304,256]{1,0:T(8,128)(2,1)S(1)} %slice.41), channel_id=1, source_target_pairs={{4,0},{5,1},{6,2},{7,3},{8,4},{9,5},{10,6},{11,7},{12,8},{13,9},{1... | collective-permute-start | bytes 466952 | tf_op jit(solution)/shard_map/ppermute | solution.py:39
  32.4 0.0 collective-permute-done.8
  32.4 0.0 collective-permute-done.9
  32.5 2.8 %collective-permute-done.7.refs_4_ = bf16[304,256]{1,0:T(8,128)(2,1)S(1)} collective-permute-done((bf16[304,256]{1,0:T(8,128)(2,1)S(1)}, bf16[304,256]{1,0:T(8,128)(2,1)S(1)}, u32[]{:S(2)}, u32[]{:S(2)}) %collective-permute-start.7) | collective-permute-done | bytes 155680 | tf_op jit(solution)/shard_map/ppermute | solution.py:39
  35.3 0.1 collective-permute-done.6.refs_3_
  35.3 0.0 collective-permute-done.5
  35.3 1.8 %collective-permute-start.10 = (bf16[2,1040,128]{2,1,0:T(8,128)(2,1)S(1)}, bf16[2,1040,128]{2,1,0:T(8,128)(2,1)S(1)}, u32[]{:S(2)}, u32[]{:S(2)}) collective-permute-start(bf16[2,1040,128]{2,1,0:T(8,128)(2,1)S(1)} %collective-permute-done.5), channel_id=1, source_target_pairs={{64,0},{208,16},{96,32},{240,48},{128,64},{16,80},{160,96},{48,112... | collective-permute-start | bytes 1597448 | tf_op jit(solution)/shard_map/ppermute | solution.py:47
  37.2 1.2 %collective-permute-start.14 = (bf16[576,256]{1,0:T(8,128)(2,1)S(1)}, bf16[576,256]{1,0:T(8,128)(2,1)S(1)}, u32[]{:S(2)}, u32[]{:S(2)}) collective-permute-start(bf16[576,256]{1,0:T(8,128)(2,1)S(1)} %pad_maximum_fusion.4), channel_id=1, source_target_pairs={{1,0},{2,1},{3,2},{0,3},{5,4},{6,5},{7,6},{4,7},{9,8},{10,9},{11,1... | collective-permute-start | bytes 884744 | tf_op jit(solution)/shard_map/ppermute | solution.py:39
  38.4 1.3 %collective-permute-start.15 = (bf16[576,256]{1,0:T(8,128)(2,1)S(1)}, bf16[576,256]{1,0:T(8,128)(2,1)S(1)}, u32[]{:S(2)}, u32[]{:S(2)}) collective-permute-start(bf16[576,256]{1,0:T(8,128)(2,1)S(1)} %pad_maximum_fusion.4), channel_id=1, source_target_pairs={{3,0},{0,1},{1,2},{2,3},{7,4},{4,5},{5,6},{6,7},{11,8},{8,9},{9,10... | collective-permute-start | bytes 884744 | tf_op jit(solution)/shard_map/ppermute | solution.py:39
  39.7 2.4 %collective-permute-start.12 = (bf16[1440,256]{1,0:T(8,128)(2,1)S(1)}, bf16[1440,256]{1,0:T(8,128)(2,1)S(1)}, u32[]{:S(2)}, u32[]{:S(2)}) collective-permute-start(bf16[1440,256]{1,0:T(8,128)(2,1)S(1)} %pad_maximum_fusion.1.refs_5_), channel_id=1, source_target_pairs={{4,0},{5,1},{6,2},{7,3},{8,4},{9,5},{10,6},{11,7},{12,8},{13,9},{1... | collective-permute-start | bytes 2211848 | tf_op jit(solution)/shard_map/ppermute | solution.py:39
  42.1 0.0 collective-permute-start.13
  42.1 0.1 constant_dynamic-update-slice_fusion.2
  42.2 8.3 %collective-permute-done.15.refs_9_ = bf16[576,256]{1,0:T(8,128)(2,1)S(1)} collective-permute-done((bf16[576,256]{1,0:T(8,128)(2,1)S(1)}, bf16[576,256]{1,0:T(8,128)(2,1)S(1)}, u32[]{:S(2)}, u32[]{:S(2)}) %collective-permute-start.15) | collective-permute-done | bytes 294944 | tf_op jit(solution)/shard_map/ppermute | solution.py:39
  50.5 0.3 collective-permute-start.18
  50.8 0.0 collective-permute-done.14.refs_8_
  50.8 3.6 %collective-permute-start.19 = (bf16[288,256]{1,0:T(8,128)(2,1)S(1)}, bf16[288,256]{1,0:T(8,128)(2,1)S(1)}, u32[]{:S(2)}, u32[]{:S(2)}) collective-permute-start(bf16[288,256]{1,0:T(8,128)(2,1)S(1)} %slice.55), channel_id=1, source_target_pairs={{1,0},{2,1},{3,2},{0,3},{5,4},{6,5},{7,6},{4,7},{9,8},{10,9},{11,1... | collective-permute-start | bytes 442376 | tf_op jit(solution)/shard_map/ppermute | solution.py:39
  54.4 0.0 collective-permute-done.10
  54.4 0.0 collective-permute-start.11
  54.4 0.2 pad_maximum_fusion.tiles
  54.6 0.1 constant_dynamic-update-slice_fusion.1
  54.7 2.5 %collective-permute-done.13.refs_7_ = bf16[1440,256]{1,0:T(8,128)(2,1)S(1)} collective-permute-done((bf16[1440,256]{1,0:T(8,128)(2,1)S(1)}, bf16[1440,256]{1,0:T(8,128)(2,1)S(1)}, u32[]{:S(2)}, u32[]{:S(2)}) %collective-permute-start.13) | collective-permute-done | bytes 737312 | tf_op jit(solution)/shard_map/ppermute | solution.py:39
  57.2 0.1 collective-permute-start.16
  57.3 0.0 collective-permute-done.12.refs_6_
  57.3 2.7 %collective-permute-start.17 = (bf16[720,256]{1,0:T(8,128)(2,1)S(1)}, bf16[720,256]{1,0:T(8,128)(2,1)S(1)}, u32[]{:S(2)}, u32[]{:S(2)}) collective-permute-start(bf16[720,256]{1,0:T(8,128)(2,1)S(1)} %slice.53), channel_id=1, source_target_pairs={{4,0},{5,1},{6,2},{7,3},{8,4},{9,5},{10,6},{11,7},{12,8},{13,9},{1... | collective-permute-start | bytes 1105928 | tf_op jit(solution)/shard_map/ppermute | solution.py:39
  60.1 5.0 %first_part.1.first_sums = f32[16,624,128]{2,1,0:T(8,128)S(1)} custom-call(s32[2]{0:T(128)S(1)} %pad_add_fusion.position, bf16[6,1040,128]{2,1,0:T(8,128)(2,1)S(1)} %pad_maximum_fusion.tiles, bf16[624,256]{1,0:T(8,128)(2,1)S(1)} %copy-done, bf16[624,256]{1,0:T(8,128)(2,1)S(1)} %collective-permute-done.1.refs_1_, ...), custom_call_target="tpu_custom_call" | custom-call | flops 5000000000 | bytes 16000000 | tf_op jit(solution)/shard_map/first_part/pallas_call | solution.py:188
  65.0 0.0 collective-permute-done.18.refs_12_
  65.0 0.0 collective-permute-done.19.refs_13_
  65.1 0.0 collective-permute-done.11
  65.1 0.4 collective-permute-done.16.refs_10_
  65.5 0.0 collective-permute-done.17.refs_11_
  65.5 0.1 constant_dynamic-update-slice_fusion.tiles
  65.6 6.7 %collective-permute-start.20 = (bf16[8,1040,128]{2,1,0:T(8,128)(2,1)S(1)}, bf16[8,1040,128]{2,1,0:T(8,128)(2,1)S(1)}, u32[]{:S(2)}, u32[]{:S(2)}) collective-permute-start(bf16[8,1040,128]{2,1,0:T(8,128)(2,1)S(1)} %constant_dynamic-update-slice_fusion.tiles), channel_id=1, source_target_pairs={{16,0},{0,16},{48,32},{32,48},{80,64},{64,80},{112,96},{96,112},{1... | collective-permute-start | bytes 6389768 | tf_op jit(solution)/shard_map/ppermute | solution.py:47
  72.3 5.3 %second_part.1 = (bf16[32,624,128]{2,1,0:T(8,128)(2,1)S(1)}, f32[16,624,128]{2,1,0:T(8,128)S(1)}) custom-call(s32[2]{0:T(128)S(1)} %pad_add_fusion.position, bf16[8,1040,128]{2,1,0:T(8,128)(2,1)S(1)} %constant_dynamic-update-slice_fusion.tiles, bf16[624,256]{1,0:T(8,128)(2,1)S(1)} %copy-done, bf16[624,256]{1,0:T(8,128)(2,1)S(1)} %collective-permute-done.1.refs_1_, ...), custom_call_target="tpu_custom_call" | custom-call | flops 5000000000 | bytes 16000000 | tf_op jit(solution)/shard_map/second_part/pallas_call | solution.py:188
  77.6 0.0 collective-permute-done.20.tiles
  77.6 7.9 %last_part.1 = bf16[624,2048]{1,0:T(8,128)(2,1)} custom-call(s32[2]{0:T(128)S(1)} %pad_add_fusion.position, bf16[8,1040,128]{2,1,0:T(8,128)(2,1)S(1)} %collective-permute-done.20.tiles, bf16[32,624,128]{2,1,0:T(8,128)(2,1)S(1)} %get-tuple-element.34.amps, f32[16,624,128]{2,1,0:T(8,128)S(1)} %first_part.1.first_sums, ...), custom_call_target="tpu_custom_call" | custom-call | flops 5000000000 | bytes 16000000 | tf_op jit(solution)/shard_map/last_part/pallas_call | solution.py:188
  (16 shorter events, 0.3 us)
Async XLA Ops:
  0.0 29.3 %copy-start = (bf16[624,256]{1,0:T(8,128)(2,1)S(1)}, bf16[624,256]{1,0:T(8,128)(2,1)}, u32[]{:S(2)}) copy-start(bf16[624,256]{1,0:T(8,128)(2,1)} %refs_0_.3) | copy-start | bytes 958468
  1.0 14.8 %collective-permute-start.3 = (bf16[480,256]{1,0:T(8,128)(2,1)S(1)}, bf16[480,256]{1,0:T(8,128)(2,1)S(1)}, u32[]{:S(2)}, u32[]{:S(2)}) collective-permute-start(bf16[480,256]{1,0:T(8,128)(2,1)S(1)} %slice.39), channel_id=1, source_target_pairs={{1,0},{2,1},{3,2},{0,3},{5,4},{6,5},{7,6},{4,7},{9,8},{10,9},{11,1... | collective-permute-start | bytes 737288 | tf_op jit(solution)/shard_map/ppermute | solution.py:39
  8.0 10.5 %collective-permute-start.4 = (bf16[480,256]{1,0:T(8,128)(2,1)S(1)}, bf16[480,256]{1,0:T(8,128)(2,1)S(1)}, u32[]{:S(2)}, u32[]{:S(2)}) collective-permute-start(bf16[480,256]{1,0:T(8,128)(2,1)S(1)} %slice.39), channel_id=1, source_target_pairs={{3,0},{0,1},{1,2},{2,3},{7,4},{4,5},{5,6},{6,7},{11,8},{8,9},{9,10... | collective-permute-start | bytes 737288 | tf_op jit(solution)/shard_map/ppermute | solution.py:39
  9.7 14.6 %collective-permute-start = (bf16[1040,128]{1,0:T(8,128)(2,1)S(1)}, bf16[1040,128]{1,0:T(8,128)(2,1)S(1)}, u32[]{:S(2)}, u32[]{:S(2)}) collective-permute-start(bf16[1040,128]{1,0:T(8,128)(2,1)S(1)} %get-tuple-element.40), channel_id=1, source_target_pairs={{32,0},{48,16},{0,32},{16,48},{96,64},{112,80},{64,96},{80,112},{1... | collective-permute-start | bytes 798728 | tf_op jit(solution)/shard_map/ppermute | solution.py:47
  10.5 13.9 %collective-permute-start.1 = (bf16[624,256]{1,0:T(8,128)(2,1)}, bf16[624,256]{1,0:T(8,128)(2,1)S(1)}, u32[]{:S(2)}, u32[]{:S(2)}) collective-permute-start(bf16[624,256]{1,0:T(8,128)(2,1)} %refs_0_.3), channel_id=1, source_target_pairs={{4,0},{5,1},{6,2},{7,3},{8,4},{9,5},{10,6},{11,7},{12,8},{13,9},{1... | collective-permute-start | bytes 958472 | tf_op jit(solution)/shard_map/ppermute | solution.py:39
  13.2 11.1 %collective-permute-start.2 = (bf16[624,256]{1,0:T(8,128)(2,1)}, bf16[624,256]{1,0:T(8,128)(2,1)S(1)}, u32[]{:S(2)}, u32[]{:S(2)}) collective-permute-start(bf16[624,256]{1,0:T(8,128)(2,1)} %refs_0_.3), channel_id=1, source_target_pairs={{12,0},{13,1},{14,2},{15,3},{0,4},{1,5},{2,6},{3,7},{4,8},{5,9},{6... | collective-permute-start | bytes 958472 | tf_op jit(solution)/shard_map/ppermute | solution.py:39
  24.4 11.0 %collective-permute-start.5 = (bf16[2,1040,128]{2,1,0:T(8,128)(2,1)S(1)}, bf16[2,1040,128]{2,1,0:T(8,128)(2,1)S(1)}, u32[]{:S(2)}, u32[]{:S(2)}) collective-permute-start(bf16[2,1040,128]{2,1,0:T(8,128)(2,1)S(1)} %pad_maximum_fusion.2), channel_id=1, source_target_pairs={{64,0},{208,16},{96,32},{240,48},{128,64},{16,80},{160,96},{48,112... | collective-permute-start | bytes 1597448 | tf_op jit(solution)/shard_map/ppermute | solution.py:47
  25.7 6.7 %collective-permute-start.8 = (bf16[240,256]{1,0:T(8,128)(2,1)S(1)}, bf16[240,256]{1,0:T(8,128)(2,1)S(1)}, u32[]{:S(2)}, u32[]{:S(2)}) collective-permute-start(bf16[240,256]{1,0:T(8,128)(2,1)S(1)} %get-tuple-element.37), channel_id=1, source_target_pairs={{3,0},{0,1},{1,2},{2,3},{7,4},{4,5},{5,6},{6,7},{11,8},{8,9},{9,10... | collective-permute-start | bytes 368648 | tf_op jit(solution)/shard_map/ppermute | solution.py:39
  26.8 5.6 %collective-permute-start.9 = (bf16[240,256]{1,0:T(8,128)(2,1)S(1)}, bf16[240,256]{1,0:T(8,128)(2,1)S(1)}, u32[]{:S(2)}, u32[]{:S(2)}) collective-permute-start(bf16[240,256]{1,0:T(8,128)(2,1)S(1)} %get-tuple-element.38), channel_id=1, source_target_pairs={{1,0},{2,1},{3,2},{0,3},{5,4},{6,5},{7,6},{4,7},{9,8},{10,9},{11,1... | collective-permute-start | bytes 368648 | tf_op jit(solution)/shard_map/ppermute | solution.py:39
  29.5 5.8 %collective-permute-start.6 = (bf16[320,256]{1,0:T(8,128)(2,1)S(1)}, bf16[320,256]{1,0:T(8,128)(2,1)S(1)}, u32[]{:S(2)}, u32[]{:S(2)}) collective-permute-start(bf16[320,256]{1,0:T(8,128)(2,1)S(1)} %slice.40), channel_id=1, source_target_pairs={{12,0},{13,1},{14,2},{15,3},{0,4},{1,5},{2,6},{3,7},{4,8},{5,9},{6... | collective-permute-start | bytes 491528 | tf_op jit(solution)/shard_map/ppermute | solution.py:39
  30.9 4.4 %collective-permute-start.7 = (bf16[304,256]{1,0:T(8,128)(2,1)S(1)}, bf16[304,256]{1,0:T(8,128)(2,1)S(1)}, u32[]{:S(2)}, u32[]{:S(2)}) collective-permute-start(bf16[304,256]{1,0:T(8,128)(2,1)S(1)} %slice.41), channel_id=1, source_target_pairs={{4,0},{5,1},{6,2},{7,3},{8,4},{9,5},{10,6},{11,7},{12,8},{13,9},{1... | collective-permute-start | bytes 466952 | tf_op jit(solution)/shard_map/ppermute | solution.py:39
  35.3 19.1 %collective-permute-start.10 = (bf16[2,1040,128]{2,1,0:T(8,128)(2,1)S(1)}, bf16[2,1040,128]{2,1,0:T(8,128)(2,1)S(1)}, u32[]{:S(2)}, u32[]{:S(2)}) collective-permute-start(bf16[2,1040,128]{2,1,0:T(8,128)(2,1)S(1)} %collective-permute-done.5), channel_id=1, source_target_pairs={{64,0},{208,16},{96,32},{240,48},{128,64},{16,80},{160,96},{48,112... | collective-permute-start | bytes 1597448 | tf_op jit(solution)/shard_map/ppermute | solution.py:47
  37.2 13.6 %collective-permute-start.14 = (bf16[576,256]{1,0:T(8,128)(2,1)S(1)}, bf16[576,256]{1,0:T(8,128)(2,1)S(1)}, u32[]{:S(2)}, u32[]{:S(2)}) collective-permute-start(bf16[576,256]{1,0:T(8,128)(2,1)S(1)} %pad_maximum_fusion.4), channel_id=1, source_target_pairs={{1,0},{2,1},{3,2},{0,3},{5,4},{6,5},{7,6},{4,7},{9,8},{10,9},{11,1... | collective-permute-start | bytes 884744 | tf_op jit(solution)/shard_map/ppermute | solution.py:39
  38.4 12.1 %collective-permute-start.15 = (bf16[576,256]{1,0:T(8,128)(2,1)S(1)}, bf16[576,256]{1,0:T(8,128)(2,1)S(1)}, u32[]{:S(2)}, u32[]{:S(2)}) collective-permute-start(bf16[576,256]{1,0:T(8,128)(2,1)S(1)} %pad_maximum_fusion.4), channel_id=1, source_target_pairs={{3,0},{0,1},{1,2},{2,3},{7,4},{4,5},{5,6},{6,7},{11,8},{8,9},{9,10... | collective-permute-start | bytes 884744 | tf_op jit(solution)/shard_map/ppermute | solution.py:39
  39.7 17.6 %collective-permute-start.12 = (bf16[1440,256]{1,0:T(8,128)(2,1)S(1)}, bf16[1440,256]{1,0:T(8,128)(2,1)S(1)}, u32[]{:S(2)}, u32[]{:S(2)}) collective-permute-start(bf16[1440,256]{1,0:T(8,128)(2,1)S(1)} %pad_maximum_fusion.1.refs_5_), channel_id=1, source_target_pairs={{4,0},{5,1},{6,2},{7,3},{8,4},{9,5},{10,6},{11,7},{12,8},{13,9},{1... | collective-permute-start | bytes 2211848 | tf_op jit(solution)/shard_map/ppermute | solution.py:39
  42.1 15.1 %collective-permute-start.13 = (bf16[1440,256]{1,0:T(8,128)(2,1)S(1)}, bf16[1440,256]{1,0:T(8,128)(2,1)S(1)}, u32[]{:S(2)}, u32[]{:S(2)}) collective-permute-start(bf16[1440,256]{1,0:T(8,128)(2,1)S(1)} %pad_maximum_fusion.1.refs_5_), channel_id=1, source_target_pairs={{12,0},{13,1},{14,2},{15,3},{0,4},{1,5},{2,6},{3,7},{4,8},{5,9},{6... | collective-permute-start | bytes 2211848 | tf_op jit(solution)/shard_map/ppermute | solution.py:39
  50.5 14.6 %collective-permute-start.18 = (bf16[288,256]{1,0:T(8,128)(2,1)S(1)}, bf16[288,256]{1,0:T(8,128)(2,1)S(1)}, u32[]{:S(2)}, u32[]{:S(2)}) collective-permute-start(bf16[288,256]{1,0:T(8,128)(2,1)S(1)} %slice.54), channel_id=1, source_target_pairs={{3,0},{0,1},{1,2},{2,3},{7,4},{4,5},{5,6},{6,7},{11,8},{8,9},{9,10... | collective-permute-start | bytes 442376 | tf_op jit(solution)/shard_map/ppermute | solution.py:39
  50.8 14.3 %collective-permute-start.19 = (bf16[288,256]{1,0:T(8,128)(2,1)S(1)}, bf16[288,256]{1,0:T(8,128)(2,1)S(1)}, u32[]{:S(2)}, u32[]{:S(2)}) collective-permute-start(bf16[288,256]{1,0:T(8,128)(2,1)S(1)} %slice.55), channel_id=1, source_target_pairs={{1,0},{2,1},{3,2},{0,3},{5,4},{6,5},{7,6},{4,7},{9,8},{10,9},{11,1... | collective-permute-start | bytes 442376 | tf_op jit(solution)/shard_map/ppermute | solution.py:39
  54.4 10.6 %collective-permute-start.11 = (bf16[2,1040,128]{2,1,0:T(8,128)(2,1)S(1)}, bf16[2,1040,128]{2,1,0:T(8,128)(2,1)S(1)}, u32[]{:S(2)}, u32[]{:S(2)}) collective-permute-start(bf16[2,1040,128]{2,1,0:T(8,128)(2,1)S(1)} %collective-permute-done.10), channel_id=1, source_target_pairs={{64,0},{208,16},{96,32},{240,48},{128,64},{16,80},{160,96},{48,112... | collective-permute-start | bytes 1597448 | tf_op jit(solution)/shard_map/ppermute | solution.py:47
  57.2 8.3 %collective-permute-start.16 = (bf16[720,256]{1,0:T(8,128)(2,1)S(1)}, bf16[720,256]{1,0:T(8,128)(2,1)S(1)}, u32[]{:S(2)}, u32[]{:S(2)}) collective-permute-start(bf16[720,256]{1,0:T(8,128)(2,1)S(1)} %slice.52), channel_id=1, source_target_pairs={{12,0},{13,1},{14,2},{15,3},{0,4},{1,5},{2,6},{3,7},{4,8},{5,9},{6... | collective-permute-start | bytes 1105928 | tf_op jit(solution)/shard_map/ppermute | solution.py:39
  57.3 8.1 %collective-permute-start.17 = (bf16[720,256]{1,0:T(8,128)(2,1)S(1)}, bf16[720,256]{1,0:T(8,128)(2,1)S(1)}, u32[]{:S(2)}, u32[]{:S(2)}) collective-permute-start(bf16[720,256]{1,0:T(8,128)(2,1)S(1)} %slice.53), channel_id=1, source_target_pairs={{4,0},{5,1},{6,2},{7,3},{8,4},{9,5},{10,6},{11,7},{12,8},{13,9},{1... | collective-permute-start | bytes 1105928 | tf_op jit(solution)/shard_map/ppermute | solution.py:39
  65.6 12.0 %collective-permute-start.20 = (bf16[8,1040,128]{2,1,0:T(8,128)(2,1)S(1)}, bf16[8,1040,128]{2,1,0:T(8,128)(2,1)S(1)}, u32[]{:S(2)}, u32[]{:S(2)}) collective-permute-start(bf16[8,1040,128]{2,1,0:T(8,128)(2,1)S(1)} %constant_dynamic-update-slice_fusion.tiles), channel_id=1, source_target_pairs={{16,0},{0,16},{48,32},{32,48},{80,64},{64,80},{112,96},{96,112},{1... | collective-permute-start | bytes 6389768 | tf_op jit(solution)/shard_map/ppermute | solution.py:47

commit v4 on v3

--- a/solution.py
+++ b/solution.py
@@ -47,7 +47,7 @@
     return lax.ppermute(value, "row", perm)
 
 
-def pair_tiles(position, tiles, wanted, codes, codes_smem, pairs, last, counts, sem):
+def pair_tiles(position, tiles, wanted, meanwhile, codes, codes_smem, pairs, last, counts, sem):
     n = tiles.shape[0]
     y, z = position[0], position[1]
     lane = lax.broadcasted_iota(jnp.int32, (1, TILE), 1)
@@ -64,6 +64,8 @@
     copy.start()
     for q in range(NQ + 1):
         counts[q] = 0
+        last[q] = 0
+    meanwhile()
     copy.wait()
 
     def put(i, n_pairs):
@@ -81,8 +83,6 @@
             n_pairs = n_pairs + (live & opens).astype(jnp.int32)
         return n_pairs
 
-    for q in range(NQ + 1):
-        last[q] = 0
     n_pairs = lax.fori_loop(0, n, put, jnp.int32(0))
     for i in range(2 * BATCH):
         pairs[n_pairs * 2 + i] = EMPTY
@@ -137,8 +137,11 @@
     copies = moves(plan, refs[:n_pieces], amps, sem)
     for copy in copies:
         copy.start()
-    sums[...] = jnp.zeros_like(sums)
-    n_pairs = pair_tiles(position, tiles, early_pair, *pairing, code_sem)
+
+    def clear():
+        sums[...] = jnp.zeros_like(sums)
+
+    n_pairs = pair_tiles(position, tiles, early_pair, clear, *pairing, code_sem)
     for copy in copies:
         copy.wait()
     accumulate(n_pairs, pairing[2], tiles, amps, sums)
@@ -149,12 +152,14 @@
     copies = moves(plan, refs[:n_pieces], amps, sem)
     for copy in copies:
         copy.start()
-    sums[...] = jnp.zeros_like(sums)
 
     def wanted(slot, block):
         return jnp.logical_not(early_pair(slot, block))
 
-    n_pairs = pair_tiles(position, tiles, wanted, *pairing, code_sem)
+    def clear():
+        sums[...] = jnp.zeros_like(sums)
+
+    n_pairs = pair_tiles(position, tiles, wanted, clear, *pairing, code_sem)
     for copy in copies:
         copy.wait()
     accumulate(n_pairs, pairing[2], tiles, amps, sums)
@@ -162,8 +167,11 @@
 
 def last_part(position, tiles, amps, first_sums, second_sums, out, *refs):
     *pairing, code_sem, sums, stage, out_sem = refs
-    sums[...] = first_sums[...] + second_sums[...]
-    n_pairs = pair_tiles(position, tiles, lambda slot, block: slot >= 0, *pairing, code_sem)
+
+    def add():
+        sums[...] = first_sums[...] + second_sums[...]
+
+    n_pairs = pair_tiles(position, tiles, lambda slot, block: slot >= 0, add, *pairing, code_sem)
     accumulate(n_pairs, pairing[2], tiles, amps, sums)
     writes = []
     for i in range(NQ // SPAN):
@@ -252,7 +260,7 @@
     z_up, z_down = (from_col(first, dz=dz) for dz in (1, 3))
     both = jnp.stack([block, block_z])
     near = jnp.concatenate([z_up, z_down], axis=0)
-    both, y_up, y_down, near = fence(both, y_up, y_down, near)
+    both, near = fence(both, near)
 
     x_blocks = [both]
     x_blocks.append(from_row(x_blocks[-1], dx=1))
@@ -265,6 +273,8 @@
     x_blocks.append(from_row(x_blocks[-1], dx=1))
     firsts += [from_col(firsts[0], dy=dy) for dy in (1, 3)]
     lasts += [from_col(lasts[0], dz=dz) for dz in (1, 3)]
+
+    x_blocks[-1], lasts[1], lasts[2] = fence(x_blocks[-1], lasts[1], lasts[2])
 
     plan = [(0, 0, ROWS, 0, 0), (1, 0, ROWS, 1, 0), (2, 0, ROWS, 2, 0), (3, 0, HALF, 3, 0)]
     plan.append((4, 0, ROWS - HALF, 3, HALF))

time: 85.6 us -> 85.5 us (level)
  transfers between devices with their start and end apart: 21 -> 21, of which waited for: 8 -> 8; matrix products, arithmetic and copies ran while one was open for 3% -> 3% of each run, Pallas kernels for 12% -> 13%
where the time goes in v4:
time: 85.5 us; the launch traced here: 85.3 us
  starting transfers between devices  37.8 us (44%)
  waiting for transfers between devices  25.4 us (30%)
  Pallas kernels  18.2 us (21%)
  other arithmetic  2.1 us (2%)
  local copies, waits for them, and re-layouts  1.42 us (2%)
    ppermute x16, starting transfers between devices, from_col(): return lax.ppermute(value, 'col', perm)  27.6 us
    ppermute x16, waiting for transfers between devices, from_col(): return lax.ppermute(value, 'col', perm)  19.7 us
    pallas_call x3, Pallas kernels, call(): pl.pallas_call(body, out_shape=out_shape, in_specs=[pl.BlockSpec(memory_s...  18.2 us
    ppermute x5, starting transfers between devices, from_row(): return lax.ppermute(value, 'row', perm)  10.2 us
    ppermute x5, waiting for transfers between devices, from_row(): return lax.ppermute(value, 'row', perm)  5.76 us
  transfers between devices with their start and end apart: 21, of which 8 were waited for; matrix products, arithmetic and copies ran while one was open for 3% of the time, Pallas kernels for 13%

profile of v4, /device:TPU:1, one launch (start us, length us, event | category | flops | bytes accessed | tf_op | source)
XLA Modules:
  0.0 85.3 jit_solution(18365727068519439938)
XLA Ops:
  0.0 0.0 copy-start
  0.0 1.0 %slice.39 = bf16[480,256]{1,0:T(8,128)(2,1)S(1)} slice(bf16[624,256]{1,0:T(8,128)(2,1)} %refs_0_.3), slice={[0:480], [0:256]} | slice | bytes 491520 | tf_op jit(solution)/shard_map/slice | solution.py:259
  1.0 6.9 %collective-permute-start.1 = (bf16[480,256]{1,0:T(8,128)(2,1)S(1)}, bf16[480,256]{1,0:T(8,128)(2,1)S(1)}, u32[]{:S(2)}, u32[]{:S(2)}) collective-permute-start(bf16[480,256]{1,0:T(8,128)(2,1)S(1)} %slice.39), channel_id=1, source_target_pairs={{1,0},{2,1},{3,2},{0,3},{5,4},{6,5},{7,6},{4,7},{9,8},{10,9},{11,1... | collective-permute-start | bytes 737288 | tf_op jit(solution)/shard_map/ppermute | solution.py:39
  8.0 0.0 collective-permute-start.2
  8.0 0.7 fusion.6
  8.6 1.0 %fusion.7 = (bf16[1,1040,128]{2,1,0:T(8,128)(2,1)S(1)}, bf16[1040,128]{1,0:T(8,128)(2,1)S(1)}) fusion(bf16[16,128]{1,0:T(8,128)(2,1)S(1)} %fusion.5, bf16[1024,128]{1,0:T(8,128)(2,1)} %bitcast.7), kind=kLoop, calls=%fused_computation.22 | loop fusion | flops 532480 | bytes 798720 | tf_op jit(solution)/shard_map/stack | solution.py:261
  9.7 0.8 collective-permute-start
  10.5 1.3 %collective-permute-start.4 = (bf16[624,256]{1,0:T(8,128)(2,1)}, bf16[624,256]{1,0:T(8,128)(2,1)S(1)}, u32[]{:S(2)}, u32[]{:S(2)}) collective-permute-start(bf16[624,256]{1,0:T(8,128)(2,1)} %refs_0_.3), channel_id=1, source_target_pairs={{12,0},{13,1},{14,2},{15,3},{0,4},{1,5},{2,6},{3,7},{4,8},{5,9},{6... | collective-permute-start | bytes 958472 | tf_op jit(solution)/shard_map/ppermute | solution.py:39
  11.8 1.4 %collective-permute-start.6 = (bf16[624,256]{1,0:T(8,128)(2,1)}, bf16[624,256]{1,0:T(8,128)(2,1)S(1)}, u32[]{:S(2)}, u32[]{:S(2)}) collective-permute-start(bf16[624,256]{1,0:T(8,128)(2,1)} %refs_0_.3), channel_id=1, source_target_pairs={{4,0},{5,1},{6,2},{7,3},{8,4},{9,5},{10,6},{11,7},{12,8},{13,9},{1... | collective-permute-start | bytes 958472 | tf_op jit(solution)/shard_map/ppermute | solution.py:39
  13.2 2.6 %collective-permute-done.1 = bf16[480,256]{1,0:T(8,128)(2,1)S(1)} collective-permute-done((bf16[480,256]{1,0:T(8,128)(2,1)S(1)}, bf16[480,256]{1,0:T(8,128)(2,1)S(1)}, u32[]{:S(2)}, u32[]{:S(2)}) %collective-permute-start.1) | collective-permute-done | bytes 245792 | tf_op jit(solution)/shard_map/ppermute | solution.py:39
  15.8 2.7 %collective-permute-done.2 = bf16[480,256]{1,0:T(8,128)(2,1)S(1)} collective-permute-done((bf16[480,256]{1,0:T(8,128)(2,1)S(1)}, bf16[480,256]{1,0:T(8,128)(2,1)S(1)}, u32[]{:S(2)}, u32[]{:S(2)}) %collective-permute-start.2) | collective-permute-done | bytes 245792 | tf_op jit(solution)/shard_map/ppermute | solution.py:39
  18.5 5.7 %collective-permute-done = bf16[1040,128]{1,0:T(8,128)(2,1)S(1)} collective-permute-done((bf16[1040,128]{1,0:T(8,128)(2,1)S(1)}, bf16[1040,128]{1,0:T(8,128)(2,1)S(1)}, u32[]{:S(2)}, u32[]{:S(2)}) %collective-permute-start) | collective-permute-done | bytes 266272 | tf_op jit(solution)/shard_map/ppermute | solution.py:47
  24.3 0.1 pad_maximum_fusion.2
  24.4 1.3 %collective-permute-start.3 = (bf16[2,1040,128]{2,1,0:T(8,128)(2,1)S(1)}, bf16[2,1040,128]{2,1,0:T(8,128)(2,1)S(1)}, u32[]{:S(2)}, u32[]{:S(2)}) collective-permute-start(bf16[2,1040,128]{2,1,0:T(8,128)(2,1)S(1)} %pad_maximum_fusion.2), channel_id=1, source_target_pairs={{64,0},{208,16},{96,32},{240,48},{128,64},{16,80},{160,96},{48,112... | collective-permute-start | bytes 1597448 | tf_op jit(solution)/shard_map/ppermute | solution.py:47
  25.7 1.1 %collective-permute-start.8 = (bf16[240,256]{1,0:T(8,128)(2,1)S(1)}, bf16[240,256]{1,0:T(8,128)(2,1)S(1)}, u32[]{:S(2)}, u32[]{:S(2)}) collective-permute-start(bf16[240,256]{1,0:T(8,128)(2,1)S(1)} %get-tuple-element.39), channel_id=1, source_target_pairs={{3,0},{0,1},{1,2},{2,3},{7,4},{4,5},{5,6},{6,7},{11,8},{8,9},{9,10... | collective-permute-start | bytes 368648 | tf_op jit(solution)/shard_map/ppermute | solution.py:39
  26.8 2.5 %collective-permute-start.9 = (bf16[240,256]{1,0:T(8,128)(2,1)S(1)}, bf16[240,256]{1,0:T(8,128)(2,1)S(1)}, u32[]{:S(2)}, u32[]{:S(2)}) collective-permute-start(bf16[240,256]{1,0:T(8,128)(2,1)S(1)} %get-tuple-element.40), channel_id=1, source_target_pairs={{1,0},{2,1},{3,2},{0,3},{5,4},{6,5},{7,6},{4,7},{9,8},{10,9},{11,1... | collective-permute-start | bytes 368648 | tf_op jit(solution)/shard_map/ppermute | solution.py:39
  29.3 0.0 copy-done
  29.3 0.1 pad_add_fusion.position
  29.4 0.0 collective-permute-done.4.refs_2_
  29.4 1.4 %collective-permute-start.5 = (bf16[320,256]{1,0:T(8,128)(2,1)S(1)}, bf16[320,256]{1,0:T(8,128)(2,1)S(1)}, u32[]{:S(2)}, u32[]{:S(2)}) collective-permute-start(bf16[320,256]{1,0:T(8,128)(2,1)S(1)} %slice.52), channel_id=1, source_target_pairs={{12,0},{13,1},{14,2},{15,3},{0,4},{1,5},{2,6},{3,7},{4,8},{5,9},{6... | collective-permute-start | bytes 491528 | tf_op jit(solution)/shard_map/ppermute | solution.py:39
  30.8 0.0 collective-permute-done.6.refs_1_
  30.8 1.5 %collective-permute-start.7 = (bf16[304,256]{1,0:T(8,128)(2,1)S(1)}, bf16[304,256]{1,0:T(8,128)(2,1)S(1)}, u32[]{:S(2)}, u32[]{:S(2)}) collective-permute-start(bf16[304,256]{1,0:T(8,128)(2,1)S(1)} %slice.53), channel_id=1, source_target_pairs={{4,0},{5,1},{6,2},{7,3},{8,4},{9,5},{10,6},{11,7},{12,8},{13,9},{1... | collective-permute-start | bytes 466952 | tf_op jit(solution)/shard_map/ppermute | solution.py:39
  32.4 0.0 collective-permute-done.8
  32.4 0.0 collective-permute-done.9
  32.4 0.1 pad_maximum_fusion.1.refs_5_
  32.5 2.8 %collective-permute-done.7.refs_4_ = bf16[304,256]{1,0:T(8,128)(2,1)S(1)} collective-permute-done((bf16[304,256]{1,0:T(8,128)(2,1)S(1)}, bf16[304,256]{1,0:T(8,128)(2,1)S(1)}, u32[]{:S(2)}, u32[]{:S(2)}) %collective-permute-start.7) | collective-permute-done | bytes 155680 | tf_op jit(solution)/shard_map/ppermute | solution.py:39
  35.3 0.0 collective-permute-done.5.refs_3_
  35.3 0.0 collective-permute-done.3
  35.3 1.9 %collective-permute-start.10 = (bf16[2,1040,128]{2,1,0:T(8,128)(2,1)S(1)}, bf16[2,1040,128]{2,1,0:T(8,128)(2,1)S(1)}, u32[]{:S(2)}, u32[]{:S(2)}) collective-permute-start(bf16[2,1040,128]{2,1,0:T(8,128)(2,1)S(1)} %collective-permute-done.3), channel_id=1, source_target_pairs={{64,0},{208,16},{96,32},{240,48},{128,64},{16,80},{160,96},{48,112... | collective-permute-start | bytes 1597448 | tf_op jit(solution)/shard_map/ppermute | solution.py:47
  37.2 1.2 %collective-permute-start.11 = (bf16[576,256]{1,0:T(8,128)(2,1)S(1)}, bf16[576,256]{1,0:T(8,128)(2,1)S(1)}, u32[]{:S(2)}, u32[]{:S(2)}) collective-permute-start(bf16[576,256]{1,0:T(8,128)(2,1)S(1)} %pad_maximum_fusion.4), channel_id=1, source_target_pairs={{1,0},{2,1},{3,2},{0,3},{5,4},{6,5},{7,6},{4,7},{9,8},{10,9},{11,1... | collective-permute-start | bytes 884744 | tf_op jit(solution)/shard_map/ppermute | solution.py:39
  38.3 1.3 %collective-permute-start.12 = (bf16[576,256]{1,0:T(8,128)(2,1)S(1)}, bf16[576,256]{1,0:T(8,128)(2,1)S(1)}, u32[]{:S(2)}, u32[]{:S(2)}) collective-permute-start(bf16[576,256]{1,0:T(8,128)(2,1)S(1)} %pad_maximum_fusion.4), channel_id=1, source_target_pairs={{3,0},{0,1},{1,2},{2,3},{7,4},{4,5},{5,6},{6,7},{11,8},{8,9},{9,10... | collective-permute-start | bytes 884744 | tf_op jit(solution)/shard_map/ppermute | solution.py:39
  39.7 2.4 %collective-permute-start.14 = (bf16[1440,256]{1,0:T(8,128)(2,1)S(1)}, bf16[1440,256]{1,0:T(8,128)(2,1)S(1)}, u32[]{:S(2)}, u32[]{:S(2)}) collective-permute-start(bf16[1440,256]{1,0:T(8,128)(2,1)S(1)} %pad_maximum_fusion.1.refs_5_), channel_id=1, source_target_pairs={{4,0},{5,1},{6,2},{7,3},{8,4},{9,5},{10,6},{11,7},{12,8},{13,9},{1... | collective-permute-start | bytes 2211848 | tf_op jit(solution)/shard_map/ppermute | solution.py:39
  42.1 0.0 collective-permute-start.15
  42.1 0.1 constant_dynamic-update-slice_fusion.2
  42.1 1.7 %collective-permute-done.11.refs_8_ = bf16[576,256]{1,0:T(8,128)(2,1)S(1)} collective-permute-done((bf16[576,256]{1,0:T(8,128)(2,1)S(1)}, bf16[576,256]{1,0:T(8,128)(2,1)S(1)}, u32[]{:S(2)}, u32[]{:S(2)}) %collective-permute-start.11) | collective-permute-done | bytes 294944 | tf_op jit(solution)/shard_map/ppermute | solution.py:39
  43.8 6.8 %collective-permute-done.12.refs_9_ = bf16[576,256]{1,0:T(8,128)(2,1)S(1)} collective-permute-done((bf16[576,256]{1,0:T(8,128)(2,1)S(1)}, bf16[576,256]{1,0:T(8,128)(2,1)S(1)}, u32[]{:S(2)}, u32[]{:S(2)}) %collective-permute-start.12) | collective-permute-done | bytes 294944 | tf_op jit(solution)/shard_map/ppermute | solution.py:39
  50.6 0.0 collective-permute-done.10
  50.6 0.0 collective-permute-start.13
  50.6 0.1 collective-permute-start.18
  50.8 3.6 %collective-permute-start.19 = (bf16[288,256]{1,0:T(8,128)(2,1)S(1)}, bf16[288,256]{1,0:T(8,128)(2,1)S(1)}, u32[]{:S(2)}, u32[]{:S(2)}) collective-permute-start(bf16[288,256]{1,0:T(8,128)(2,1)S(1)} %slice.51), channel_id=1, source_target_pairs={{1,0},{2,1},{3,2},{0,3},{5,4},{6,5},{7,6},{4,7},{9,8},{10,9},{11,1... | collective-permute-start | bytes 442376 | tf_op jit(solution)/shard_map/ppermute | solution.py:39
  54.4 0.2 pad_maximum_fusion.tiles
  54.6 0.1 constant_dynamic-update-slice_fusion.1
  54.7 2.3 %collective-permute-done.15.refs_7_ = bf16[1440,256]{1,0:T(8,128)(2,1)S(1)} collective-permute-done((bf16[1440,256]{1,0:T(8,128)(2,1)S(1)}, bf16[1440,256]{1,0:T(8,128)(2,1)S(1)}, u32[]{:S(2)}, u32[]{:S(2)}) %collective-permute-start.15) | collective-permute-done | bytes 737312 | tf_op jit(solution)/shard_map/ppermute | solution.py:39
  57.0 0.1 collective-permute-start.16
  57.1 0.0 collective-permute-done.14.refs_6_
  57.2 2.7 %collective-permute-start.17 = (bf16[720,256]{1,0:T(8,128)(2,1)S(1)}, bf16[720,256]{1,0:T(8,128)(2,1)S(1)}, u32[]{:S(2)}, u32[]{:S(2)}) collective-permute-start(bf16[720,256]{1,0:T(8,128)(2,1)S(1)} %slice.57), channel_id=1, source_target_pairs={{4,0},{5,1},{6,2},{7,3},{8,4},{9,5},{10,6},{11,7},{12,8},{13,9},{1... | collective-permute-start | bytes 1105928 | tf_op jit(solution)/shard_map/ppermute | solution.py:39
  59.9 4.9 %first_part.1.first_sums = f32[16,624,128]{2,1,0:T(8,128)S(1)} custom-call(s32[2]{0:T(128)S(1)} %pad_add_fusion.position, bf16[6,1040,128]{2,1,0:T(8,128)(2,1)S(1)} %pad_maximum_fusion.tiles, bf16[624,256]{1,0:T(8,128)(2,1)S(1)} %copy-done, bf16[624,256]{1,0:T(8,128)(2,1)S(1)} %collective-permute-done.6.refs_1_, ...), custom_call_target="tpu_custom_call" | custom-call | flops 5000000000 | bytes 16000000 | tf_op jit(solution)/shard_map/first_part/pallas_call | solution.py:196
  64.8 0.0 collective-permute-done.18.refs_12_
  64.8 0.0 collective-permute-done.19.refs_13_
  64.9 0.0 collective-permute-done.13
  64.9 0.7 collective-permute-done.16.refs_10_
  65.6 0.0 collective-permute-done.17.refs_11_
  65.6 0.1 constant_dynamic-update-slice_fusion.tiles
  65.7 6.2 %collective-permute-start.20 = (bf16[8,1040,128]{2,1,0:T(8,128)(2,1)S(1)}, bf16[8,1040,128]{2,1,0:T(8,128)(2,1)S(1)}, u32[]{:S(2)}, u32[]{:S(2)}) collective-permute-start(bf16[8,1040,128]{2,1,0:T(8,128)(2,1)S(1)} %constant_dynamic-update-slice_fusion.tiles), channel_id=1, source_target_pairs={{16,0},{0,16},{48,32},{32,48},{80,64},{64,80},{112,96},{96,112},{1... | collective-permute-start | bytes 6389768 | tf_op jit(solution)/shard_map/ppermute | solution.py:47
  71.9 6.1 %second_part.1 = (bf16[32,624,128]{2,1,0:T(8,128)(2,1)S(1)}, f32[16,624,128]{2,1,0:T(8,128)S(1)}) custom-call(s32[2]{0:T(128)S(1)} %pad_add_fusion.position, bf16[8,1040,128]{2,1,0:T(8,128)(2,1)S(1)} %constant_dynamic-update-slice_fusion.tiles, bf16[624,256]{1,0:T(8,128)(2,1)S(1)} %copy-done, bf16[624,256]{1,0:T(8,128)(2,1)S(1)} %collective-permute-done.6.refs_1_, ...), custom_call_target="tpu_custom_call" | custom-call | flops 5000000000 | bytes 16000000 | tf_op jit(solution)/shard_map/second_part/pallas_call | solution.py:196
  77.9 0.0 collective-permute-done.20.tiles
  78.0 7.1 %last_part.1 = bf16[624,2048]{1,0:T(8,128)(2,1)} custom-call(s32[2]{0:T(128)S(1)} %pad_add_fusion.position, bf16[8,1040,128]{2,1,0:T(8,128)(2,1)S(1)} %collective-permute-done.20.tiles, bf16[32,624,128]{2,1,0:T(8,128)(2,1)S(1)} %get-tuple-element.36.amps, f32[16,624,128]{2,1,0:T(8,128)S(1)} %first_part.1.first_sums, ...), custom_call_target="tpu_custom_call" | custom-call | flops 5000000000 | bytes 16000000 | tf_op jit(solution)/shard_map/last_part/pallas_call | solution.py:196
  (15 shorter events, 0.2 us)
Async XLA Ops:
  0.0 29.3 %copy-start = (bf16[624,256]{1,0:T(8,128)(2,1)S(1)}, bf16[624,256]{1,0:T(8,128)(2,1)}, u32[]{:S(2)}) copy-start(bf16[624,256]{1,0:T(8,128)(2,1)} %refs_0_.3) | copy-start | bytes 958468
  1.0 14.8 %collective-permute-start.1 = (bf16[480,256]{1,0:T(8,128)(2,1)S(1)}, bf16[480,256]{1,0:T(8,128)(2,1)S(1)}, u32[]{:S(2)}, u32[]{:S(2)}) collective-permute-start(bf16[480,256]{1,0:T(8,128)(2,1)S(1)} %slice.39), channel_id=1, source_target_pairs={{1,0},{2,1},{3,2},{0,3},{5,4},{6,5},{7,6},{4,7},{9,8},{10,9},{11,1... | collective-permute-start | bytes 737288 | tf_op jit(solution)/shard_map/ppermute | solution.py:39
  8.0 10.5 %collective-permute-start.2 = (bf16[480,256]{1,0:T(8,128)(2,1)S(1)}, bf16[480,256]{1,0:T(8,128)(2,1)S(1)}, u32[]{:S(2)}, u32[]{:S(2)}) collective-permute-start(bf16[480,256]{1,0:T(8,128)(2,1)S(1)} %slice.39), channel_id=1, source_target_pairs={{3,0},{0,1},{1,2},{2,3},{7,4},{4,5},{5,6},{6,7},{11,8},{8,9},{9,10... | collective-permute-start | bytes 737288 | tf_op jit(solution)/shard_map/ppermute | solution.py:39
  9.7 14.6 %collective-permute-start = (bf16[1040,128]{1,0:T(8,128)(2,1)S(1)}, bf16[1040,128]{1,0:T(8,128)(2,1)S(1)}, u32[]{:S(2)}, u32[]{:S(2)}) collective-permute-start(bf16[1040,128]{1,0:T(8,128)(2,1)S(1)} %get-tuple-element.42), channel_id=1, source_target_pairs={{32,0},{48,16},{0,32},{16,48},{96,64},{112,80},{64,96},{80,112},{1... | collective-permute-start | bytes 798728 | tf_op jit(solution)/shard_map/ppermute | solution.py:47
  10.5 18.9 %collective-permute-start.4 = (bf16[624,256]{1,0:T(8,128)(2,1)}, bf16[624,256]{1,0:T(8,128)(2,1)S(1)}, u32[]{:S(2)}, u32[]{:S(2)}) collective-permute-start(bf16[624,256]{1,0:T(8,128)(2,1)} %refs_0_.3), channel_id=1, source_target_pairs={{12,0},{13,1},{14,2},{15,3},{0,4},{1,5},{2,6},{3,7},{4,8},{5,9},{6... | collective-permute-start | bytes 958472 | tf_op jit(solution)/shard_map/ppermute | solution.py:39
  11.8 19.0 %collective-permute-start.6 = (bf16[624,256]{1,0:T(8,128)(2,1)}, bf16[624,256]{1,0:T(8,128)(2,1)S(1)}, u32[]{:S(2)}, u32[]{:S(2)}) collective-permute-start(bf16[624,256]{1,0:T(8,128)(2,1)} %refs_0_.3), channel_id=1, source_target_pairs={{4,0},{5,1},{6,2},{7,3},{8,4},{9,5},{10,6},{11,7},{12,8},{13,9},{1... | collective-permute-start | bytes 958472 | tf_op jit(solution)/shard_map/ppermute | solution.py:39
  24.4 10.9 %collective-permute-start.3 = (bf16[2,1040,128]{2,1,0:T(8,128)(2,1)S(1)}, bf16[2,1040,128]{2,1,0:T(8,128)(2,1)S(1)}, u32[]{:S(2)}, u32[]{:S(2)}) collective-permute-start(bf16[2,1040,128]{2,1,0:T(8,128)(2,1)S(1)} %pad_maximum_fusion.2), channel_id=1, source_target_pairs={{64,0},{208,16},{96,32},{240,48},{128,64},{16,80},{160,96},{48,112... | collective-permute-start | bytes 1597448 | tf_op jit(solution)/shard_map/ppermute | solution.py:47
  25.7 6.7 %collective-permute-start.8 = (bf16[240,256]{1,0:T(8,128)(2,1)S(1)}, bf16[240,256]{1,0:T(8,128)(2,1)S(1)}, u32[]{:S(2)}, u32[]{:S(2)}) collective-permute-start(bf16[240,256]{1,0:T(8,128)(2,1)S(1)} %get-tuple-element.39), channel_id=1, source_target_pairs={{3,0},{0,1},{1,2},{2,3},{7,4},{4,5},{5,6},{6,7},{11,8},{8,9},{9,10... | collective-permute-start | bytes 368648 | tf_op jit(solution)/shard_map/ppermute | solution.py:39
  26.8 5.6 %collective-permute-start.9 = (bf16[240,256]{1,0:T(8,128)(2,1)S(1)}, bf16[240,256]{1,0:T(8,128)(2,1)S(1)}, u32[]{:S(2)}, u32[]{:S(2)}) collective-permute-start(bf16[240,256]{1,0:T(8,128)(2,1)S(1)} %get-tuple-element.40), channel_id=1, source_target_pairs={{1,0},{2,1},{3,2},{0,3},{5,4},{6,5},{7,6},{4,7},{9,8},{10,9},{11,1... | collective-permute-start | bytes 368648 | tf_op jit(solution)/shard_map/ppermute | solution.py:39
  29.4 5.8 %collective-permute-start.5 = (bf16[320,256]{1,0:T(8,128)(2,1)S(1)}, bf16[320,256]{1,0:T(8,128)(2,1)S(1)}, u32[]{:S(2)}, u32[]{:S(2)}) collective-permute-start(bf16[320,256]{1,0:T(8,128)(2,1)S(1)} %slice.52), channel_id=1, source_target_pairs={{12,0},{13,1},{14,2},{15,3},{0,4},{1,5},{2,6},{3,7},{4,8},{5,9},{6... | collective-permute-start | bytes 491528 | tf_op jit(solution)/shard_map/ppermute | solution.py:39
  30.8 4.5 %collective-permute-start.7 = (bf16[304,256]{1,0:T(8,128)(2,1)S(1)}, bf16[304,256]{1,0:T(8,128)(2,1)S(1)}, u32[]{:S(2)}, u32[]{:S(2)}) collective-permute-start(bf16[304,256]{1,0:T(8,128)(2,1)S(1)} %slice.53), channel_id=1, source_target_pairs={{4,0},{5,1},{6,2},{7,3},{8,4},{9,5},{10,6},{11,7},{12,8},{13,9},{1... | collective-permute-start | bytes 466952 | tf_op jit(solution)/shard_map/ppermute | solution.py:39
  35.3 15.3 %collective-permute-start.10 = (bf16[2,1040,128]{2,1,0:T(8,128)(2,1)S(1)}, bf16[2,1040,128]{2,1,0:T(8,128)(2,1)S(1)}, u32[]{:S(2)}, u32[]{:S(2)}) collective-permute-start(bf16[2,1040,128]{2,1,0:T(8,128)(2,1)S(1)} %collective-permute-done.3), channel_id=1, source_target_pairs={{64,0},{208,16},{96,32},{240,48},{128,64},{16,80},{160,96},{48,112... | collective-permute-start | bytes 1597448 | tf_op jit(solution)/shard_map/ppermute | solution.py:47
  37.2 6.6 %collective-permute-start.11 = (bf16[576,256]{1,0:T(8,128)(2,1)S(1)}, bf16[576,256]{1,0:T(8,128)(2,1)S(1)}, u32[]{:S(2)}, u32[]{:S(2)}) collective-permute-start(bf16[576,256]{1,0:T(8,128)(2,1)S(1)} %pad_maximum_fusion.4), channel_id=1, source_target_pairs={{1,0},{2,1},{3,2},{0,3},{5,4},{6,5},{7,6},{4,7},{9,8},{10,9},{11,1... | collective-permute-start | bytes 884744 | tf_op jit(solution)/shard_map/ppermute | solution.py:39
  38.3 12.3 %collective-permute-start.12 = (bf16[576,256]{1,0:T(8,128)(2,1)S(1)}, bf16[576,256]{1,0:T(8,128)(2,1)S(1)}, u32[]{:S(2)}, u32[]{:S(2)}) collective-permute-start(bf16[576,256]{1,0:T(8,128)(2,1)S(1)} %pad_maximum_fusion.4), channel_id=1, source_target_pairs={{3,0},{0,1},{1,2},{2,3},{7,4},{4,5},{5,6},{6,7},{11,8},{8,9},{9,10... | collective-permute-start | bytes 884744 | tf_op jit(solution)/shard_map/ppermute | solution.py:39
  39.7 17.5 %collective-permute-start.14 = (bf16[1440,256]{1,0:T(8,128)(2,1)S(1)}, bf16[1440,256]{1,0:T(8,128)(2,1)S(1)}, u32[]{:S(2)}, u32[]{:S(2)}) collective-permute-start(bf16[1440,256]{1,0:T(8,128)(2,1)S(1)} %pad_maximum_fusion.1.refs_5_), channel_id=1, source_target_pairs={{4,0},{5,1},{6,2},{7,3},{8,4},{9,5},{10,6},{11,7},{12,8},{13,9},{1... | collective-permute-start | bytes 2211848 | tf_op jit(solution)/shard_map/ppermute | solution.py:39
  42.1 14.9 %collective-permute-start.15 = (bf16[1440,256]{1,0:T(8,128)(2,1)S(1)}, bf16[1440,256]{1,0:T(8,128)(2,1)S(1)}, u32[]{:S(2)}, u32[]{:S(2)}) collective-permute-start(bf16[1440,256]{1,0:T(8,128)(2,1)S(1)} %pad_maximum_fusion.1.refs_5_), channel_id=1, source_target_pairs={{12,0},{13,1},{14,2},{15,3},{0,4},{1,5},{2,6},{3,7},{4,8},{5,9},{6... | collective-permute-start | bytes 2211848 | tf_op jit(solution)/shard_map/ppermute | solution.py:39
  50.6 14.2 %collective-permute-start.13 = (bf16[2,1040,128]{2,1,0:T(8,128)(2,1)S(1)}, bf16[2,1040,128]{2,1,0:T(8,128)(2,1)S(1)}, u32[]{:S(2)}, u32[]{:S(2)}) collective-permute-start(bf16[2,1040,128]{2,1,0:T(8,128)(2,1)S(1)} %collective-permute-done.10), channel_id=1, source_target_pairs={{64,0},{208,16},{96,32},{240,48},{128,64},{16,80},{160,96},{48,112... | collective-permute-start | bytes 1597448 | tf_op jit(solution)/shard_map/ppermute | solution.py:47
  50.6 14.2 %collective-permute-start.18 = (bf16[288,256]{1,0:T(8,128)(2,1)S(1)}, bf16[288,256]{1,0:T(8,128)(2,1)S(1)}, u32[]{:S(2)}, u32[]{:S(2)}) collective-permute-start(bf16[288,256]{1,0:T(8,128)(2,1)S(1)} %slice.50), channel_id=1, source_target_pairs={{3,0},{0,1},{1,2},{2,3},{7,4},{4,5},{5,6},{6,7},{11,8},{8,9},{9,10... | collective-permute-start | bytes 442376 | tf_op jit(solution)/shard_map/ppermute | solution.py:39
  50.8 14.1 %collective-permute-start.19 = (bf16[288,256]{1,0:T(8,128)(2,1)S(1)}, bf16[288,256]{1,0:T(8,128)(2,1)S(1)}, u32[]{:S(2)}, u32[]{:S(2)}) collective-permute-start(bf16[288,256]{1,0:T(8,128)(2,1)S(1)} %slice.51), channel_id=1, source_target_pairs={{1,0},{2,1},{3,2},{0,3},{5,4},{6,5},{7,6},{4,7},{9,8},{10,9},{11,1... | collective-permute-start | bytes 442376 | tf_op jit(solution)/shard_map/ppermute | solution.py:39
  57.0 8.5 %collective-permute-start.16 = (bf16[720,256]{1,0:T(8,128)(2,1)S(1)}, bf16[720,256]{1,0:T(8,128)(2,1)S(1)}, u32[]{:S(2)}, u32[]{:S(2)}) collective-permute-start(bf16[720,256]{1,0:T(8,128)(2,1)S(1)} %slice.56), channel_id=1, source_target_pairs={{12,0},{13,1},{14,2},{15,3},{0,4},{1,5},{2,6},{3,7},{4,8},{5,9},{6... | collective-permute-start | bytes 1105928 | tf_op jit(solution)/shard_map/ppermute | solution.py:39
  57.2 8.4 %collective-permute-start.17 = (bf16[720,256]{1,0:T(8,128)(2,1)S(1)}, bf16[720,256]{1,0:T(8,128)(2,1)S(1)}, u32[]{:S(2)}, u32[]{:S(2)}) collective-permute-start(bf16[720,256]{1,0:T(8,128)(2,1)S(1)} %slice.57), channel_id=1, source_target_pairs={{4,0},{5,1},{6,2},{7,3},{8,4},{9,5},{10,6},{11,7},{12,8},{13,9},{1... | collective-permute-start | bytes 1105928 | tf_op jit(solution)/shard_map/ppermute | solution.py:39
  65.7 12.3 %collective-permute-start.20 = (bf16[8,1040,128]{2,1,0:T(8,128)(2,1)S(1)}, bf16[8,1040,128]{2,1,0:T(8,128)(2,1)S(1)}, u32[]{:S(2)}, u32[]{:S(2)}) collective-permute-start(bf16[8,1040,128]{2,1,0:T(8,128)(2,1)S(1)} %constant_dynamic-update-slice_fusion.tiles), channel_id=1, source_target_pairs={{16,0},{0,16},{48,32},{32,48},{80,64},{64,80},{112,96},{96,112},{1... | collective-permute-start | bytes 6389768 | tf_op jit(solution)/shard_map/ppermute | solution.py:47

commit v5 on v4

--- a/solution.py
+++ b/solution.py
@@ -22,6 +22,7 @@
 BATCH = 6
 SPAN = 4
 EMPTY = -1
+SECOND = 64 + BATCH
 
 
 def rank_of(d):
@@ -47,7 +48,7 @@
     return lax.ppermute(value, "row", perm)
 
 
-def pair_tiles(position, tiles, wanted, meanwhile, codes, codes_smem, pairs, last, counts, sem):
+def pair_tiles(position, tiles, wanted, meanwhile, split, codes, codes_smem, pairs, last, counts, sem):
     n = tiles.shape[0]
     y, z = position[0], position[1]
     lane = lax.broadcasted_iota(jnp.int32, (1, TILE), 1)
@@ -69,27 +70,31 @@
     copy.wait()
 
     def put(i, n_pairs):
+        low, high = n_pairs
         for j in range(SLOTS):
             code = codes_smem[i, j]
             live = code >= 0
             q = jnp.where(live, code >> 11, NQ)
             count = counts[q]
             opens = (count & 1) == 0
-            at = jnp.where(live, jnp.where(opens, n_pairs, last[q]), HELD + BATCH)
+            at = jnp.where(live, jnp.where(opens, jnp.where(q < split, low, SECOND + high), last[q]), 2 * SECOND)
             counts[q] = count + 1
             last[q] = at
             pairs[at * 2] = jnp.where(opens, code, pairs[at * 2])
             pairs[at * 2 + 1] = jnp.where(opens, EMPTY, code)
-            n_pairs = n_pairs + (live & opens).astype(jnp.int32)
-        return n_pairs
-
-    n_pairs = lax.fori_loop(0, n, put, jnp.int32(0))
+            new = (live & opens).astype(jnp.int32)
+            low = low + jnp.where(q < split, new, 0)
+            high = high + jnp.where(q < split, 0, new)
+        return low, high
+
+    low, high = lax.fori_loop(0, n, put, (jnp.int32(0), jnp.int32(0)))
     for i in range(2 * BATCH):
-        pairs[n_pairs * 2 + i] = EMPTY
-    return n_pairs
-
-
-def accumulate(n_pairs, pairs, tiles, amps, sums):
+        pairs[low * 2 + i] = EMPTY
+        pairs[(SECOND + high) * 2 + i] = EMPTY
+    return low, high
+
+
+def accumulate(n_pairs, pairs, tiles, amps, sums, first=0):
     def load(code):
         item = jnp.maximum(code, 0)
         slot = (item >> 5) & (HELD - 1)
@@ -100,7 +105,7 @@
     def step(batch, carry):
         values = []
         for i in range(BATCH):
-            at = (batch * BATCH + i) * 2
+            at = (first + batch * BATCH + i) * 2
             (left, upper), (right, lower) = load(pairs[at]), load(pairs[at + 1])
             value = jnp.dot(
                 jnp.concatenate([left, right], axis=1),
@@ -141,7 +146,7 @@
     def clear():
         sums[...] = jnp.zeros_like(sums)
 
-    n_pairs = pair_tiles(position, tiles, early_pair, clear, *pairing, code_sem)
+    n_pairs, _ = pair_tiles(position, tiles, early_pair, clear, NQ, *pairing, code_sem)
     for copy in copies:
         copy.wait()
     accumulate(n_pairs, pairing[2], tiles, amps, sums)
@@ -159,7 +164,7 @@
     def clear():
         sums[...] = jnp.zeros_like(sums)
 
-    n_pairs = pair_tiles(position, tiles, wanted, clear, *pairing, code_sem)
+    n_pairs, _ = pair_tiles(position, tiles, wanted, clear, NQ, *pairing, code_sem)
     for copy in copies:
         copy.wait()
     accumulate(n_pairs, pairing[2], tiles, amps, sums)
@@ -171,10 +176,12 @@
     def add():
         sums[...] = first_sums[...] + second_sums[...]
 
-    n_pairs = pair_tiles(position, tiles, lambda slot, block: slot >= 0, add, *pairing, code_sem)
-    accumulate(n_pairs, pairing[2], tiles, amps, sums)
+    low, high = pair_tiles(position, tiles, lambda slot, block: slot >= 0, add, NQ // 2, *pairing, code_sem)
+    accumulate(low, pairing[2], tiles, amps, sums)
     writes = []
     for i in range(NQ // SPAN):
+        if i * SPAN == NQ // 2:
+            accumulate(high, pairing[2], tiles, amps, sums, SECOND)
         for j in range(SPAN):
             stage[i, :, j * TILE : (j + 1) * TILE] = sums[i * SPAN + j].astype(jnp.bfloat16)
         columns = pl.ds(i * SPAN * TILE, SPAN * TILE)
@@ -188,7 +195,7 @@
     pairing = [
         pltpu.VMEM((8, TILE), jnp.int32),
         pltpu.SMEM((8, TILE), jnp.int32),
-        pltpu.SMEM((2 * (HELD + BATCH + 1),), jnp.int32),
+        pltpu.SMEM((4 * SECOND + 2,), jnp.int32),
         pltpu.SMEM((NQ + 1,), jnp.int32),
         pltpu.SMEM((NQ + 1,), jnp.int32),
         pltpu.SemaphoreType.DMA,

time: 85.5 us -> 85.9 us (level)
    pallas_call x3, Pallas kernels: 18.2 us -> 19 us  [call(): pl.pallas_call(body, out_shape=out_shape, in_specs=[pl.BlockSpec(memory_s...]
where the time goes in v5:
time: 85.9 us; the launch traced here: 86 us
  starting transfers between devices  37.8 us (44%)
  waiting for transfers between devices  25.3 us (29%)
  Pallas kernels  19 us (22%)
  other arithmetic  2.1 us (2%)
  local copies, waits for them, and re-layouts  1.42 us (2%)
    ppermute x16, starting transfers between devices, from_col(): return lax.ppermute(value, 'col', perm)  27.6 us
    ppermute x16, waiting for transfers between devices, from_col(): return lax.ppermute(value, 'col', perm)  19.6 us
    pallas_call x3, Pallas kernels, call(): pl.pallas_call(body, out_shape=out_shape, in_specs=[pl.BlockSpec(memory_s...  19 us
    ppermute x5, starting transfers between devices, from_row(): return lax.ppermute(value, 'row', perm)  10.2 us
    ppermute x5, waiting for transfers between devices, from_row(): return lax.ppermute(value, 'row', perm)  5.76 us
  transfers between devices with their start and end apart: 21, of which 8 were waited for; matrix products, arithmetic and copies ran while one was open for 3% of the time, Pallas kernels for 13%

profile of v5, /device:TPU:1, one launch (start us, length us, event | category | flops | bytes accessed | tf_op | source)
XLA Modules:
  0.0 86.0 jit_solution(7096349237415668430)
XLA Ops:
  0.0 0.0 copy-start
  0.0 1.0 %slice.39 = bf16[480,256]{1,0:T(8,128)(2,1)S(1)} slice(bf16[624,256]{1,0:T(8,128)(2,1)} %refs_0_.3), slice={[0:480], [0:256]} | slice | bytes 491520 | tf_op jit(solution)/shard_map/slice | solution.py:266
  1.0 6.9 %collective-permute-start.1 = (bf16[480,256]{1,0:T(8,128)(2,1)S(1)}, bf16[480,256]{1,0:T(8,128)(2,1)S(1)}, u32[]{:S(2)}, u32[]{:S(2)}) collective-permute-start(bf16[480,256]{1,0:T(8,128)(2,1)S(1)} %slice.39), channel_id=1, source_target_pairs={{1,0},{2,1},{3,2},{0,3},{5,4},{6,5},{7,6},{4,7},{9,8},{10,9},{11,1... | collective-permute-start | bytes 737288 | tf_op jit(solution)/shard_map/ppermute | solution.py:40
  8.0 0.0 collective-permute-start.2
  8.0 0.7 fusion.6
  8.6 1.0 %fusion.7 = (bf16[1,1040,128]{2,1,0:T(8,128)(2,1)S(1)}, bf16[1040,128]{1,0:T(8,128)(2,1)S(1)}) fusion(bf16[16,128]{1,0:T(8,128)(2,1)S(1)} %fusion.5, bf16[1024,128]{1,0:T(8,128)(2,1)} %bitcast.7), kind=kLoop, calls=%fused_computation.22 | loop fusion | flops 532480 | bytes 798720 | tf_op jit(solution)/shard_map/stack | solution.py:268
  9.7 0.8 collective-permute-start
  10.5 1.3 %collective-permute-start.4 = (bf16[624,256]{1,0:T(8,128)(2,1)}, bf16[624,256]{1,0:T(8,128)(2,1)S(1)}, u32[]{:S(2)}, u32[]{:S(2)}) collective-permute-start(bf16[624,256]{1,0:T(8,128)(2,1)} %refs_0_.3), channel_id=1, source_target_pairs={{12,0},{13,1},{14,2},{15,3},{0,4},{1,5},{2,6},{3,7},{4,8},{5,9},{6... | collective-permute-start | bytes 958472 | tf_op jit(solution)/shard_map/ppermute | solution.py:40
  11.8 1.4 %collective-permute-start.6 = (bf16[624,256]{1,0:T(8,128)(2,1)}, bf16[624,256]{1,0:T(8,128)(2,1)S(1)}, u32[]{:S(2)}, u32[]{:S(2)}) collective-permute-start(bf16[624,256]{1,0:T(8,128)(2,1)} %refs_0_.3), channel_id=1, source_target_pairs={{4,0},{5,1},{6,2},{7,3},{8,4},{9,5},{10,6},{11,7},{12,8},{13,9},{1... | collective-permute-start | bytes 958472 | tf_op jit(solution)/shard_map/ppermute | solution.py:40
  13.2 2.6 %collective-permute-done.1 = bf16[480,256]{1,0:T(8,128)(2,1)S(1)} collective-permute-done((bf16[480,256]{1,0:T(8,128)(2,1)S(1)}, bf16[480,256]{1,0:T(8,128)(2,1)S(1)}, u32[]{:S(2)}, u32[]{:S(2)}) %collective-permute-start.1) | collective-permute-done | bytes 245792 | tf_op jit(solution)/shard_map/ppermute | solution.py:40
  15.8 2.7 %collective-permute-done.2 = bf16[480,256]{1,0:T(8,128)(2,1)S(1)} collective-permute-done((bf16[480,256]{1,0:T(8,128)(2,1)S(1)}, bf16[480,256]{1,0:T(8,128)(2,1)S(1)}, u32[]{:S(2)}, u32[]{:S(2)}) %collective-permute-start.2) | collective-permute-done | bytes 245792 | tf_op jit(solution)/shard_map/ppermute | solution.py:40
  18.5 5.7 %collective-permute-done = bf16[1040,128]{1,0:T(8,128)(2,1)S(1)} collective-permute-done((bf16[1040,128]{1,0:T(8,128)(2,1)S(1)}, bf16[1040,128]{1,0:T(8,128)(2,1)S(1)}, u32[]{:S(2)}, u32[]{:S(2)}) %collective-permute-start) | collective-permute-done | bytes 266272 | tf_op jit(solution)/shard_map/ppermute | solution.py:48
  24.3 0.1 pad_maximum_fusion.2
  24.4 1.3 %collective-permute-start.3 = (bf16[2,1040,128]{2,1,0:T(8,128)(2,1)S(1)}, bf16[2,1040,128]{2,1,0:T(8,128)(2,1)S(1)}, u32[]{:S(2)}, u32[]{:S(2)}) collective-permute-start(bf16[2,1040,128]{2,1,0:T(8,128)(2,1)S(1)} %pad_maximum_fusion.2), channel_id=1, source_target_pairs={{64,0},{208,16},{96,32},{240,48},{128,64},{16,80},{160,96},{48,112... | collective-permute-start | bytes 1597448 | tf_op jit(solution)/shard_map/ppermute | solution.py:48
  25.7 1.1 %collective-permute-start.8 = (bf16[240,256]{1,0:T(8,128)(2,1)S(1)}, bf16[240,256]{1,0:T(8,128)(2,1)S(1)}, u32[]{:S(2)}, u32[]{:S(2)}) collective-permute-start(bf16[240,256]{1,0:T(8,128)(2,1)S(1)} %get-tuple-element.39), channel_id=1, source_target_pairs={{3,0},{0,1},{1,2},{2,3},{7,4},{4,5},{5,6},{6,7},{11,8},{8,9},{9,10... | collective-permute-start | bytes 368648 | tf_op jit(solution)/shard_map/ppermute | solution.py:40
  26.8 2.5 %collective-permute-start.9 = (bf16[240,256]{1,0:T(8,128)(2,1)S(1)}, bf16[240,256]{1,0:T(8,128)(2,1)S(1)}, u32[]{:S(2)}, u32[]{:S(2)}) collective-permute-start(bf16[240,256]{1,0:T(8,128)(2,1)S(1)} %get-tuple-element.40), channel_id=1, source_target_pairs={{1,0},{2,1},{3,2},{0,3},{5,4},{6,5},{7,6},{4,7},{9,8},{10,9},{11,1... | collective-permute-start | bytes 368648 | tf_op jit(solution)/shard_map/ppermute | solution.py:40
  29.3 0.0 copy-done
  29.3 0.1 pad_add_fusion.position
  29.4 0.0 collective-permute-done.4.refs_2_
  29.4 1.4 %collective-permute-start.5 = (bf16[320,256]{1,0:T(8,128)(2,1)S(1)}, bf16[320,256]{1,0:T(8,128)(2,1)S(1)}, u32[]{:S(2)}, u32[]{:S(2)}) collective-permute-start(bf16[320,256]{1,0:T(8,128)(2,1)S(1)} %slice.52), channel_id=1, source_target_pairs={{12,0},{13,1},{14,2},{15,3},{0,4},{1,5},{2,6},{3,7},{4,8},{5,9},{6... | collective-permute-start | bytes 491528 | tf_op jit(solution)/shard_map/ppermute | solution.py:40
  30.8 0.0 collective-permute-done.6.refs_1_
  30.8 1.5 %collective-permute-start.7 = (bf16[304,256]{1,0:T(8,128)(2,1)S(1)}, bf16[304,256]{1,0:T(8,128)(2,1)S(1)}, u32[]{:S(2)}, u32[]{:S(2)}) collective-permute-start(bf16[304,256]{1,0:T(8,128)(2,1)S(1)} %slice.53), channel_id=1, source_target_pairs={{4,0},{5,1},{6,2},{7,3},{8,4},{9,5},{10,6},{11,7},{12,8},{13,9},{1... | collective-permute-start | bytes 466952 | tf_op jit(solution)/shard_map/ppermute | solution.py:40
  32.4 0.0 collective-permute-done.8
  32.4 0.0 collective-permute-done.9
  32.4 0.1 pad_maximum_fusion.1.refs_5_
  32.5 2.8 %collective-permute-done.7.refs_4_ = bf16[304,256]{1,0:T(8,128)(2,1)S(1)} collective-permute-done((bf16[304,256]{1,0:T(8,128)(2,1)S(1)}, bf16[304,256]{1,0:T(8,128)(2,1)S(1)}, u32[]{:S(2)}, u32[]{:S(2)}) %collective-permute-start.7) | collective-permute-done | bytes 155680 | tf_op jit(solution)/shard_map/ppermute | solution.py:40
  35.3 0.0 collective-permute-done.5.refs_3_
  35.3 0.0 collective-permute-done.3
  35.3 1.9 %collective-permute-start.10 = (bf16[2,1040,128]{2,1,0:T(8,128)(2,1)S(1)}, bf16[2,1040,128]{2,1,0:T(8,128)(2,1)S(1)}, u32[]{:S(2)}, u32[]{:S(2)}) collective-permute-start(bf16[2,1040,128]{2,1,0:T(8,128)(2,1)S(1)} %collective-permute-done.3), channel_id=1, source_target_pairs={{64,0},{208,16},{96,32},{240,48},{128,64},{16,80},{160,96},{48,112... | collective-permute-start | bytes 1597448 | tf_op jit(solution)/shard_map/ppermute | solution.py:48
  37.2 1.2 %collective-permute-start.11 = (bf16[576,256]{1,0:T(8,128)(2,1)S(1)}, bf16[576,256]{1,0:T(8,128)(2,1)S(1)}, u32[]{:S(2)}, u32[]{:S(2)}) collective-permute-start(bf16[576,256]{1,0:T(8,128)(2,1)S(1)} %pad_maximum_fusion.4), channel_id=1, source_target_pairs={{1,0},{2,1},{3,2},{0,3},{5,4},{6,5},{7,6},{4,7},{9,8},{10,9},{11,1... | collective-permute-start | bytes 884744 | tf_op jit(solution)/shard_map/ppermute | solution.py:40
  38.3 1.3 %collective-permute-start.12 = (bf16[576,256]{1,0:T(8,128)(2,1)S(1)}, bf16[576,256]{1,0:T(8,128)(2,1)S(1)}, u32[]{:S(2)}, u32[]{:S(2)}) collective-permute-start(bf16[576,256]{1,0:T(8,128)(2,1)S(1)} %pad_maximum_fusion.4), channel_id=1, source_target_pairs={{3,0},{0,1},{1,2},{2,3},{7,4},{4,5},{5,6},{6,7},{11,8},{8,9},{9,10... | collective-permute-start | bytes 884744 | tf_op jit(solution)/shard_map/ppermute | solution.py:40
  39.7 2.4 %collective-permute-start.14 = (bf16[1440,256]{1,0:T(8,128)(2,1)S(1)}, bf16[1440,256]{1,0:T(8,128)(2,1)S(1)}, u32[]{:S(2)}, u32[]{:S(2)}) collective-permute-start(bf16[1440,256]{1,0:T(8,128)(2,1)S(1)} %pad_maximum_fusion.1.refs_5_), channel_id=1, source_target_pairs={{4,0},{5,1},{6,2},{7,3},{8,4},{9,5},{10,6},{11,7},{12,8},{13,9},{1... | collective-permute-start | bytes 2211848 | tf_op jit(solution)/shard_map/ppermute | solution.py:40
  42.1 0.0 collective-permute-start.15
  42.1 0.1 constant_dynamic-update-slice_fusion.2
  42.1 1.7 %collective-permute-done.11.refs_8_ = bf16[576,256]{1,0:T(8,128)(2,1)S(1)} collective-permute-done((bf16[576,256]{1,0:T(8,128)(2,1)S(1)}, bf16[576,256]{1,0:T(8,128)(2,1)S(1)}, u32[]{:S(2)}, u32[]{:S(2)}) %collective-permute-start.11) | collective-permute-done | bytes 294944 | tf_op jit(solution)/shard_map/ppermute | solution.py:40
  43.8 6.8 %collective-permute-done.12.refs_9_ = bf16[576,256]{1,0:T(8,128)(2,1)S(1)} collective-permute-done((bf16[576,256]{1,0:T(8,128)(2,1)S(1)}, bf16[576,256]{1,0:T(8,128)(2,1)S(1)}, u32[]{:S(2)}, u32[]{:S(2)}) %collective-permute-start.12) | collective-permute-done | bytes 294944 | tf_op jit(solution)/shard_map/ppermute | solution.py:40
  50.6 0.0 collective-permute-done.10
  50.6 0.0 collective-permute-start.13
  50.6 0.1 collective-permute-start.18
  50.8 3.6 %collective-permute-start.19 = (bf16[288,256]{1,0:T(8,128)(2,1)S(1)}, bf16[288,256]{1,0:T(8,128)(2,1)S(1)}, u32[]{:S(2)}, u32[]{:S(2)}) collective-permute-start(bf16[288,256]{1,0:T(8,128)(2,1)S(1)} %slice.51), channel_id=1, source_target_pairs={{1,0},{2,1},{3,2},{0,3},{5,4},{6,5},{7,6},{4,7},{9,8},{10,9},{11,1... | collective-permute-start | bytes 442376 | tf_op jit(solution)/shard_map/ppermute | solution.py:40
  54.4 0.2 pad_maximum_fusion.tiles
  54.6 0.1 constant_dynamic-update-slice_fusion.1
  54.7 2.3 %collective-permute-done.15.refs_7_ = bf16[1440,256]{1,0:T(8,128)(2,1)S(1)} collective-permute-done((bf16[1440,256]{1,0:T(8,128)(2,1)S(1)}, bf16[1440,256]{1,0:T(8,128)(2,1)S(1)}, u32[]{:S(2)}, u32[]{:S(2)}) %collective-permute-start.15) | collective-permute-done | bytes 737312 | tf_op jit(solution)/shard_map/ppermute | solution.py:40
  57.0 0.1 collective-permute-start.16
  57.1 0.0 collective-permute-done.14.refs_6_
  57.2 2.7 %collective-permute-start.17 = (bf16[720,256]{1,0:T(8,128)(2,1)S(1)}, bf16[720,256]{1,0:T(8,128)(2,1)S(1)}, u32[]{:S(2)}, u32[]{:S(2)}) collective-permute-start(bf16[720,256]{1,0:T(8,128)(2,1)S(1)} %slice.57), channel_id=1, source_target_pairs={{4,0},{5,1},{6,2},{7,3},{8,4},{9,5},{10,6},{11,7},{12,8},{13,9},{1... | collective-permute-start | bytes 1105928 | tf_op jit(solution)/shard_map/ppermute | solution.py:40
  59.9 5.0 %first_part.1.first_sums = f32[16,624,128]{2,1,0:T(8,128)S(1)} custom-call(s32[2]{0:T(128)S(1)} %pad_add_fusion.position, bf16[6,1040,128]{2,1,0:T(8,128)(2,1)S(1)} %pad_maximum_fusion.tiles, bf16[624,256]{1,0:T(8,128)(2,1)S(1)} %copy-done, bf16[624,256]{1,0:T(8,128)(2,1)S(1)} %collective-permute-done.6.refs_1_, ...), custom_call_target="tpu_custom_call" | custom-call | flops 5000000000 | bytes 16000000 | tf_op jit(solution)/shard_map/first_part/pallas_call | solution.py:203
  64.9 0.0 collective-permute-done.18.refs_12_
  65.0 0.0 collective-permute-done.19.refs_13_
  65.0 0.0 collective-permute-done.13
  65.0 0.6 collective-permute-done.16.refs_10_
  65.6 0.0 collective-permute-done.17.refs_11_
  65.6 0.1 constant_dynamic-update-slice_fusion.tiles
  65.7 6.2 %collective-permute-start.20 = (bf16[8,1040,128]{2,1,0:T(8,128)(2,1)S(1)}, bf16[8,1040,128]{2,1,0:T(8,128)(2,1)S(1)}, u32[]{:S(2)}, u32[]{:S(2)}) collective-permute-start(bf16[8,1040,128]{2,1,0:T(8,128)(2,1)S(1)} %constant_dynamic-update-slice_fusion.tiles), channel_id=1, source_target_pairs={{16,0},{0,16},{48,32},{32,48},{80,64},{64,80},{112,96},{96,112},{1... | collective-permute-start | bytes 6389768 | tf_op jit(solution)/shard_map/ppermute | solution.py:48
  71.9 6.2 %second_part.1 = (bf16[32,624,128]{2,1,0:T(8,128)(2,1)S(1)}, f32[16,624,128]{2,1,0:T(8,128)S(1)}) custom-call(s32[2]{0:T(128)S(1)} %pad_add_fusion.position, bf16[8,1040,128]{2,1,0:T(8,128)(2,1)S(1)} %constant_dynamic-update-slice_fusion.tiles, bf16[624,256]{1,0:T(8,128)(2,1)S(1)} %copy-done, bf16[624,256]{1,0:T(8,128)(2,1)S(1)} %collective-permute-done.6.refs_1_, ...), custom_call_target="tpu_custom_call" | custom-call | flops 5000000000 | bytes 16000000 | tf_op jit(solution)/shard_map/second_part/pallas_call | solution.py:203
  78.0 0.0 collective-permute-done.20.tiles
  78.0 7.8 %last_part.1 = bf16[624,2048]{1,0:T(8,128)(2,1)} custom-call(s32[2]{0:T(128)S(1)} %pad_add_fusion.position, bf16[8,1040,128]{2,1,0:T(8,128)(2,1)S(1)} %collective-permute-done.20.tiles, bf16[32,624,128]{2,1,0:T(8,128)(2,1)S(1)} %get-tuple-element.36.amps, f32[16,624,128]{2,1,0:T(8,128)S(1)} %first_part.1.first_sums, ...), custom_call_target="tpu_custom_call" | custom-call | flops 5000000000 | bytes 16000000 | tf_op jit(solution)/shard_map/last_part/pallas_call | solution.py:203
  (15 shorter events, 0.2 us)
Async XLA Ops:
  0.0 29.3 %copy-start = (bf16[624,256]{1,0:T(8,128)(2,1)S(1)}, bf16[624,256]{1,0:T(8,128)(2,1)}, u32[]{:S(2)}) copy-start(bf16[624,256]{1,0:T(8,128)(2,1)} %refs_0_.3) | copy-start | bytes 958468
  1.0 14.8 %collective-permute-start.1 = (bf16[480,256]{1,0:T(8,128)(2,1)S(1)}, bf16[480,256]{1,0:T(8,128)(2,1)S(1)}, u32[]{:S(2)}, u32[]{:S(2)}) collective-permute-start(bf16[480,256]{1,0:T(8,128)(2,1)S(1)} %slice.39), channel_id=1, source_target_pairs={{1,0},{2,1},{3,2},{0,3},{5,4},{6,5},{7,6},{4,7},{9,8},{10,9},{11,1... | collective-permute-start | bytes 737288 | tf_op jit(solution)/shard_map/ppermute | solution.py:40
  8.0 10.5 %collective-permute-start.2 = (bf16[480,256]{1,0:T(8,128)(2,1)S(1)}, bf16[480,256]{1,0:T(8,128)(2,1)S(1)}, u32[]{:S(2)}, u32[]{:S(2)}) collective-permute-start(bf16[480,256]{1,0:T(8,128)(2,1)S(1)} %slice.39), channel_id=1, source_target_pairs={{3,0},{0,1},{1,2},{2,3},{7,4},{4,5},{5,6},{6,7},{11,8},{8,9},{9,10... | collective-permute-start | bytes 737288 | tf_op jit(solution)/shard_map/ppermute | solution.py:40
  9.7 14.6 %collective-permute-start = (bf16[1040,128]{1,0:T(8,128)(2,1)S(1)}, bf16[1040,128]{1,0:T(8,128)(2,1)S(1)}, u32[]{:S(2)}, u32[]{:S(2)}) collective-permute-start(bf16[1040,128]{1,0:T(8,128)(2,1)S(1)} %get-tuple-element.42), channel_id=1, source_target_pairs={{32,0},{48,16},{0,32},{16,48},{96,64},{112,80},{64,96},{80,112},{1... | collective-permute-start | bytes 798728 | tf_op jit(solution)/shard_map/ppermute | solution.py:48
  10.5 18.9 %collective-permute-start.4 = (bf16[624,256]{1,0:T(8,128)(2,1)}, bf16[624,256]{1,0:T(8,128)(2,1)S(1)}, u32[]{:S(2)}, u32[]{:S(2)}) collective-permute-start(bf16[624,256]{1,0:T(8,128)(2,1)} %refs_0_.3), channel_id=1, source_target_pairs={{12,0},{13,1},{14,2},{15,3},{0,4},{1,5},{2,6},{3,7},{4,8},{5,9},{6... | collective-permute-start | bytes 958472 | tf_op jit(solution)/shard_map/ppermute | solution.py:40
  11.8 19.0 %collective-permute-start.6 = (bf16[624,256]{1,0:T(8,128)(2,1)}, bf16[624,256]{1,0:T(8,128)(2,1)S(1)}, u32[]{:S(2)}, u32[]{:S(2)}) collective-permute-start(bf16[624,256]{1,0:T(8,128)(2,1)} %refs_0_.3), channel_id=1, source_target_pairs={{4,0},{5,1},{6,2},{7,3},{8,4},{9,5},{10,6},{11,7},{12,8},{13,9},{1... | collective-permute-start | bytes 958472 | tf_op jit(solution)/shard_map/ppermute | solution.py:40
  24.4 10.9 %collective-permute-start.3 = (bf16[2,1040,128]{2,1,0:T(8,128)(2,1)S(1)}, bf16[2,1040,128]{2,1,0:T(8,128)(2,1)S(1)}, u32[]{:S(2)}, u32[]{:S(2)}) collective-permute-start(bf16[2,1040,128]{2,1,0:T(8,128)(2,1)S(1)} %pad_maximum_fusion.2), channel_id=1, source_target_pairs={{64,0},{208,16},{96,32},{240,48},{128,64},{16,80},{160,96},{48,112... | collective-permute-start | bytes 1597448 | tf_op jit(solution)/shard_map/ppermute | solution.py:48
  25.7 6.7 %collective-permute-start.8 = (bf16[240,256]{1,0:T(8,128)(2,1)S(1)}, bf16[240,256]{1,0:T(8,128)(2,1)S(1)}, u32[]{:S(2)}, u32[]{:S(2)}) collective-permute-start(bf16[240,256]{1,0:T(8,128)(2,1)S(1)} %get-tuple-element.39), channel_id=1, source_target_pairs={{3,0},{0,1},{1,2},{2,3},{7,4},{4,5},{5,6},{6,7},{11,8},{8,9},{9,10... | collective-permute-start | bytes 368648 | tf_op jit(solution)/shard_map/ppermute | solution.py:40
  26.8 5.6 %collective-permute-start.9 = (bf16[240,256]{1,0:T(8,128)(2,1)S(1)}, bf16[240,256]{1,0:T(8,128)(2,1)S(1)}, u32[]{:S(2)}, u32[]{:S(2)}) collective-permute-start(bf16[240,256]{1,0:T(8,128)(2,1)S(1)} %get-tuple-element.40), channel_id=1, source_target_pairs={{1,0},{2,1},{3,2},{0,3},{5,4},{6,5},{7,6},{4,7},{9,8},{10,9},{11,1... | collective-permute-start | bytes 368648 | tf_op jit(solution)/shard_map/ppermute | solution.py:40
  29.4 5.8 %collective-permute-start.5 = (bf16[320,256]{1,0:T(8,128)(2,1)S(1)}, bf16[320,256]{1,0:T(8,128)(2,1)S(1)}, u32[]{:S(2)}, u32[]{:S(2)}) collective-permute-start(bf16[320,256]{1,0:T(8,128)(2,1)S(1)} %slice.52), channel_id=1, source_target_pairs={{12,0},{13,1},{14,2},{15,3},{0,4},{1,5},{2,6},{3,7},{4,8},{5,9},{6... | collective-permute-start | bytes 491528 | tf_op jit(solution)/shard_map/ppermute | solution.py:40
  30.8 4.5 %collective-permute-start.7 = (bf16[304,256]{1,0:T(8,128)(2,1)S(1)}, bf16[304,256]{1,0:T(8,128)(2,1)S(1)}, u32[]{:S(2)}, u32[]{:S(2)}) collective-permute-start(bf16[304,256]{1,0:T(8,128)(2,1)S(1)} %slice.53), channel_id=1, source_target_pairs={{4,0},{5,1},{6,2},{7,3},{8,4},{9,5},{10,6},{11,7},{12,8},{13,9},{1... | collective-permute-start | bytes 466952 | tf_op jit(solution)/shard_map/ppermute | solution.py:40
  35.3 15.3 %collective-permute-start.10 = (bf16[2,1040,128]{2,1,0:T(8,128)(2,1)S(1)}, bf16[2,1040,128]{2,1,0:T(8,128)(2,1)S(1)}, u32[]{:S(2)}, u32[]{:S(2)}) collective-permute-start(bf16[2,1040,128]{2,1,0:T(8,128)(2,1)S(1)} %collective-permute-done.3), channel_id=1, source_target_pairs={{64,0},{208,16},{96,32},{240,48},{128,64},{16,80},{160,96},{48,112... | collective-permute-start | bytes 1597448 | tf_op jit(solution)/shard_map/ppermute | solution.py:48
  37.2 6.6 %collective-permute-start.11 = (bf16[576,256]{1,0:T(8,128)(2,1)S(1)}, bf16[576,256]{1,0:T(8,128)(2,1)S(1)}, u32[]{:S(2)}, u32[]{:S(2)}) collective-permute-start(bf16[576,256]{1,0:T(8,128)(2,1)S(1)} %pad_maximum_fusion.4), channel_id=1, source_target_pairs={{1,0},{2,1},{3,2},{0,3},{5,4},{6,5},{7,6},{4,7},{9,8},{10,9},{11,1... | collective-permute-start | bytes 884744 | tf_op jit(solution)/shard_map/ppermute | solution.py:40
  38.3 12.3 %collective-permute-start.12 = (bf16[576,256]{1,0:T(8,128)(2,1)S(1)}, bf16[576,256]{1,0:T(8,128)(2,1)S(1)}, u32[]{:S(2)}, u32[]{:S(2)}) collective-permute-start(bf16[576,256]{1,0:T(8,128)(2,1)S(1)} %pad_maximum_fusion.4), channel_id=1, source_target_pairs={{3,0},{0,1},{1,2},{2,3},{7,4},{4,5},{5,6},{6,7},{11,8},{8,9},{9,10... | collective-permute-start | bytes 884744 | tf_op jit(solution)/shard_map/ppermute | solution.py:40
  39.7 17.5 %collective-permute-start.14 = (bf16[1440,256]{1,0:T(8,128)(2,1)S(1)}, bf16[1440,256]{1,0:T(8,128)(2,1)S(1)}, u32[]{:S(2)}, u32[]{:S(2)}) collective-permute-start(bf16[1440,256]{1,0:T(8,128)(2,1)S(1)} %pad_maximum_fusion.1.refs_5_), channel_id=1, source_target_pairs={{4,0},{5,1},{6,2},{7,3},{8,4},{9,5},{10,6},{11,7},{12,8},{13,9},{1... | collective-permute-start | bytes 2211848 | tf_op jit(solution)/shard_map/ppermute | solution.py:40
  42.1 14.9 %collective-permute-start.15 = (bf16[1440,256]{1,0:T(8,128)(2,1)S(1)}, bf16[1440,256]{1,0:T(8,128)(2,1)S(1)}, u32[]{:S(2)}, u32[]{:S(2)}) collective-permute-start(bf16[1440,256]{1,0:T(8,128)(2,1)S(1)} %pad_maximum_fusion.1.refs_5_), channel_id=1, source_target_pairs={{12,0},{13,1},{14,2},{15,3},{0,4},{1,5},{2,6},{3,7},{4,8},{5,9},{6... | collective-permute-start | bytes 2211848 | tf_op jit(solution)/shard_map/ppermute | solution.py:40
  50.6 14.3 %collective-permute-start.13 = (bf16[2,1040,128]{2,1,0:T(8,128)(2,1)S(1)}, bf16[2,1040,128]{2,1,0:T(8,128)(2,1)S(1)}, u32[]{:S(2)}, u32[]{:S(2)}) collective-permute-start(bf16[2,1040,128]{2,1,0:T(8,128)(2,1)S(1)} %collective-permute-done.10), channel_id=1, source_target_pairs={{64,0},{208,16},{96,32},{240,48},{128,64},{16,80},{160,96},{48,112... | collective-permute-start | bytes 1597448 | tf_op jit(solution)/shard_map/ppermute | solution.py:48
  50.6 14.3 %collective-permute-start.18 = (bf16[288,256]{1,0:T(8,128)(2,1)S(1)}, bf16[288,256]{1,0:T(8,128)(2,1)S(1)}, u32[]{:S(2)}, u32[]{:S(2)}) collective-permute-start(bf16[288,256]{1,0:T(8,128)(2,1)S(1)} %slice.50), channel_id=1, source_target_pairs={{3,0},{0,1},{1,2},{2,3},{7,4},{4,5},{5,6},{6,7},{11,8},{8,9},{9,10... | collective-permute-start | bytes 442376 | tf_op jit(solution)/shard_map/ppermute | solution.py:40
  50.8 14.2 %collective-permute-start.19 = (bf16[288,256]{1,0:T(8,128)(2,1)S(1)}, bf16[288,256]{1,0:T(8,128)(2,1)S(1)}, u32[]{:S(2)}, u32[]{:S(2)}) collective-permute-start(bf16[288,256]{1,0:T(8,128)(2,1)S(1)} %slice.51), channel_id=1, source_target_pairs={{1,0},{2,1},{3,2},{0,3},{5,4},{6,5},{7,6},{4,7},{9,8},{10,9},{11,1... | collective-permute-start | bytes 442376 | tf_op jit(solution)/shard_map/ppermute | solution.py:40
  57.0 8.5 %collective-permute-start.16 = (bf16[720,256]{1,0:T(8,128)(2,1)S(1)}, bf16[720,256]{1,0:T(8,128)(2,1)S(1)}, u32[]{:S(2)}, u32[]{:S(2)}) collective-permute-start(bf16[720,256]{1,0:T(8,128)(2,1)S(1)} %slice.56), channel_id=1, source_target_pairs={{12,0},{13,1},{14,2},{15,3},{0,4},{1,5},{2,6},{3,7},{4,8},{5,9},{6... | collective-permute-start | bytes 1105928 | tf_op jit(solution)/shard_map/ppermute | solution.py:40
  57.2 8.4 %collective-permute-start.17 = (bf16[720,256]{1,0:T(8,128)(2,1)S(1)}, bf16[720,256]{1,0:T(8,128)(2,1)S(1)}, u32[]{:S(2)}, u32[]{:S(2)}) collective-permute-start(bf16[720,256]{1,0:T(8,128)(2,1)S(1)} %slice.57), channel_id=1, source_target_pairs={{4,0},{5,1},{6,2},{7,3},{8,4},{9,5},{10,6},{11,7},{12,8},{13,9},{1... | collective-permute-start | bytes 1105928 | tf_op jit(solution)/shard_map/ppermute | solution.py:40
  65.7 12.4 %collective-permute-start.20 = (bf16[8,1040,128]{2,1,0:T(8,128)(2,1)S(1)}, bf16[8,1040,128]{2,1,0:T(8,128)(2,1)S(1)}, u32[]{:S(2)}, u32[]{:S(2)}) collective-permute-start(bf16[8,1040,128]{2,1,0:T(8,128)(2,1)S(1)} %constant_dynamic-update-slice_fusion.tiles), channel_id=1, source_target_pairs={{16,0},{0,16},{48,32},{32,48},{80,64},{64,80},{112,96},{96,112},{1... | collective-permute-start | bytes 6389768 | tf_op jit(solution)/shard_map/ppermute | solution.py:48
